TPU v7x, 128 devices: a whole 4x4x4 slice. The times are simulated.
128 devices in a mesh: grp: 2 (over x_hi), tp: 64 (over y, x_lo, z, core).
Axes of the slice: x: 4 (x_hi: 2, x_lo: 2; x = x_hi * 2 + x_lo), y: 4, z: 4, core: 2. Of those that a mesh axis runs over, the one named last changes fastest.
Arguments:
- tokens: bfloat16 [32768, 1664], P(('grp', 'tp')), may hold values from -6 to 6
- keep_mask: int32 [32768], P(('grp', 'tp')), may hold values 0 or 1
- shard_counts: int32 [128], P(('grp', 'tp')), may hold values from 1 to 256, 24576 in all
- latents: bfloat16 [512, 4096], P('grp', 'tp'), may hold values from -1.5 to 1.5
- query_weight: bfloat16 [4096, 1024], P('tp'), may hold values from -0.09375 to 0.09375
- keyval_weight: bfloat16 [1664, 2048], P(('grp', 'tp')), may hold values from -0.15625 to 0.15625
- output_weight: bfloat16 [1024, 4096], P(None, 'tp'), may hold values from -6 to 6
- project_weight: bfloat16 [4096, 8192], P(None, 'tp'), may hold values from -0.09375 to 0.09375
- llm_gain: bfloat16 [8192], P('tp'), may hold values from 0.5 to 1.5
- input_grad: bfloat16 [512, 8192], P('grp', 'tp'), may hold values from -6 to 6
Outputs:
- llm_input: bfloat16 [512, 8192], P('grp', 'tp')
- grad_latents: float32 [512, 4096], P('grp', 'tp')
- grad_query_weight: float32 [4096, 1024], P('tp')
- grad_keyval_weight: float32 [1664, 2048], P(('grp', 'tp'))
- grad_output_weight: float32 [1024, 4096], P(None, 'tp')
- grad_project_weight: float32 [4096, 8192], P(None, 'tp')
- grad_llm_gain: float32 [8192], P('tp')
All inputs are finite; a program needn't handle non-finite values. No bound on the sum of `keep_mask` or of `shard_counts` on one device may be relied on, other than what follows from the above.
Results may differ from a plain program's by a relative error of at most 0.015.
Values may be sent and summed in bfloat16 or wider, within the bound.
A program may use at most 128 MiB of HBM per device.

v0:
```python
import math

import jax
import jax.numpy as jnp
from jax import lax
from jax.sharding import PartitionSpec as P

D_LAT = 4096
HEADS = 8
HEAD_DIM = 128
D_LLM = 8192


score_cap = 5.0


def row_dot(left, right):
    return lax.dot_general(
        left, right, (((0,), (0,)), ((), ())), preferred_element_type=jnp.float32
    )


def col_dot(left, right):
    return lax.dot_general(
        left, right, (((1,), (1,)), ((), ())), preferred_element_type=jnp.float32
    )


def local(
    tokens,
    keep_mask,
    shard_counts,
    latents,
    query_weight,
    keyval_weight,
    output_weight,
    project_weight,
    llm_gain,
    input_grad,
):
    group_rows = latents.shape[0]
    tok_rows = tokens.shape[0]
    inner_width = query_weight.shape[1]
    group_start = lax.axis_index("grp") * group_rows
    latent_f32 = latents.astype(jnp.float32)
    square_part = jnp.sum(latent_f32 * latent_f32, axis=1)
    product_part = jnp.dot(latents, query_weight, preferred_element_type=jnp.float32)
    square_total, proj_query = lax.psum((square_part, product_part), "tp")
    latent_rinv = lax.rsqrt(square_total / D_LAT + 1e-06)
    query_own = (proj_query * latent_rinv[:, None]).astype(jnp.bfloat16)
    query_all = lax.all_gather(query_own, "grp", axis=0, tiled=True)
    full_weight = lax.all_gather(keyval_weight, ("grp", "tp"), axis=0, tiled=True)
    keyval = jnp.dot(tokens, full_weight, preferred_element_type=jnp.float32)
    key_rows = keyval[:, :inner_width].astype(jnp.bfloat16)
    values = keyval[:, inner_width:].astype(jnp.bfloat16)
    positions = jnp.arange(tok_rows, dtype=jnp.int32)
    valid_rows = (((keep_mask == 1) | (positions == 0)) & (positions < shard_counts[0])).astype(
        jnp.float32
    )
    capped_list = []
    weight_list = []
    half_list = []
    numer_list = []
    total_list = []
    for head_num in range(HEADS):
        lower = head_num * HEAD_DIM
        raw_scores = col_dot(
            query_all[:, lower : lower + HEAD_DIM], key_rows[:, lower : lower + HEAD_DIM]
        ) / math.sqrt(HEAD_DIM)
        capped = score_cap * jnp.tanh(raw_scores / score_cap)
        weights = jnp.exp(capped) * valid_rows[None, :]
        weights_half = weights.astype(jnp.bfloat16)
        numer_list.append(
            jnp.dot(
                weights_half,
                values[:, lower : lower + HEAD_DIM],
                preferred_element_type=jnp.float32,
            )
        )
        total_list.append(jnp.sum(weights, axis=1))
        capped_list.append(capped)
        weight_list.append(weights)
        half_list.append(weights_half)
    numer_part = jnp.concatenate(numer_list, axis=1)
    total_part = jnp.stack(total_list, axis=1)
    numer_whole, total_whole = lax.psum((numer_part, total_part), ("grp", "tp"))
    numer_own = lax.dynamic_slice_in_dim(numer_whole, group_start, group_rows, 0)
    total_own = lax.dynamic_slice_in_dim(total_whole, group_start, group_rows, 0)
    attended = (
        (numer_own.reshape(group_rows, HEADS, HEAD_DIM) / total_own[:, :, None])
        .reshape(group_rows, inner_width)
        .astype(jnp.bfloat16)
    )
    latents_out = (
        latent_f32 + jnp.dot(attended, output_weight, preferred_element_type=jnp.float32)
    ).astype(jnp.bfloat16)
    latents_full = lax.all_gather(latents_out, "tp", axis=1, tiled=True)
    hidden = jnp.dot(latents_full, project_weight, preferred_element_type=jnp.float32).astype(
        jnp.bfloat16
    )
    hidden_f32 = hidden.astype(jnp.float32)
    hidden_square = lax.psum(jnp.sum(hidden_f32 * hidden_f32, axis=1), "tp")
    hidden_rinv = lax.rsqrt(hidden_square / D_LLM + 1e-05)
    gain_f32 = llm_gain.astype(jnp.float32)
    llm_input = (hidden_f32 * hidden_rinv[:, None] * gain_f32[None, :]).astype(jnp.bfloat16)
    grad_f32 = input_grad.astype(jnp.float32)
    scaled_dy = grad_f32 * gain_f32[None, :]
    gain_part = jnp.sum(grad_f32 * hidden_f32 * hidden_rinv[:, None], axis=0)
    dot_total = lax.psum(jnp.sum(hidden_f32 * scaled_dy, axis=1), "tp")
    grad_hidden = (
        hidden_rinv[:, None] * scaled_dy
        - (hidden_rinv**3 / D_LLM * dot_total)[:, None] * hidden_f32
    ).astype(jnp.bfloat16)
    grad_project_weight, grad_llm_gain = lax.psum(
        (row_dot(latents_full, grad_hidden), gain_part), "grp"
    )
    grad_lat_out = lax.psum_scatter(
        col_dot(grad_hidden, project_weight), "tp", scatter_dimension=1, tiled=True
    ).astype(jnp.bfloat16)
    grad_output_weight = lax.psum(row_dot(attended, grad_lat_out), "grp")
    grad_attended = lax.psum(col_dot(grad_lat_out, output_weight), "tp").astype(jnp.bfloat16)
    grad_heads = grad_attended.astype(jnp.float32).reshape(group_rows, HEADS, HEAD_DIM)
    row_delta = jnp.sum(
        grad_heads * attended.astype(jnp.float32).reshape(group_rows, HEADS, HEAD_DIM), axis=2
    )
    scaled_grad = (
        (grad_heads / total_own[:, :, None]).reshape(group_rows, inner_width).astype(jnp.bfloat16)
    )
    scaled_delta = (row_delta / total_own).astype(jnp.bfloat16)
    grad_rows, delta_rows = (
        lax.all_gather(scaled_grad, "grp", axis=0, tiled=True),
        lax.all_gather(scaled_delta, "grp", axis=0, tiled=True),
    )
    query_list = []
    key_list = []
    value_list = []
    for head_num in range(HEADS):
        lower = head_num * HEAD_DIM
        grad_head = grad_rows[:, lower : lower + HEAD_DIM]
        prob_grad = col_dot(grad_head, values[:, lower : lower + HEAD_DIM])
        capped = capped_list[head_num]
        dscore = (
            weight_list[head_num]
            * (prob_grad - delta_rows[:, head_num].astype(jnp.float32)[:, None])
            * (1.0 - (capped / score_cap) ** 2)
            / math.sqrt(HEAD_DIM)
        ).astype(jnp.bfloat16)
        query_list.append(
            jnp.dot(
                dscore, key_rows[:, lower : lower + HEAD_DIM], preferred_element_type=jnp.float32
            )
        )
        key_list.append(
            row_dot(dscore, query_all[:, lower : lower + HEAD_DIM]).astype(jnp.bfloat16)
        )
        value_list.append(row_dot(half_list[head_num], grad_head).astype(jnp.bfloat16))
    query_part = jnp.concatenate(query_list, axis=1)
    grad_keyval = jnp.concatenate(key_list + value_list, axis=1)
    query_whole = lax.psum(query_part, ("grp", "tp"))
    grad_query = lax.dynamic_slice_in_dim(query_whole, group_start, group_rows, 0)
    weight_term = row_dot(tokens, grad_keyval)
    grad_keyval_weight = lax.psum_scatter(
        weight_term, ("grp", "tp"), scatter_dimension=0, tiled=True
    )
    scaled_query = (grad_query * latent_rinv[:, None]).astype(jnp.bfloat16)
    grad_query_weight = lax.psum(row_dot(latents, scaled_query), "grp")
    ratio_dot = jnp.sum(grad_query * proj_query, axis=1)
    grad_latents = (
        grad_lat_out.astype(jnp.float32)
        + col_dot(scaled_query, query_weight)
        - (latent_rinv**3 / D_LAT * ratio_dot)[:, None] * latent_f32
    )
    return (
        llm_input,
        grad_latents,
        grad_query_weight,
        grad_keyval_weight,
        grad_output_weight,
        grad_project_weight,
        grad_llm_gain,
    )


def solution(mesh):
    in_specs = (
        P(("grp", "tp"), None),
        P(("grp", "tp")),
        P(("grp", "tp")),
        P("grp", "tp"),
        P("tp", None),
        P(("grp", "tp"), None),
        P(None, "tp"),
        P(None, "tp"),
        P("tp"),
        P("grp", "tp"),
    )
    out_specs = (
        P("grp", "tp"),
        P("grp", "tp"),
        P("tp", None),
        P(("grp", "tp"), None),
        P(None, "tp"),
        P(None, "tp"),
        P("tp"),
    )
    return jax.shard_map(local, mesh=mesh, in_specs=in_specs, out_specs=out_specs, check_vma=False)
```

profile of v0, /device:TPU:1, one launch (start us, length us, event | category | flops | bytes accessed | tf_op | source)
XLA Modules:
  0.0 2031.9 jit_solution(10228909082375570997)
XLA Ops:
  8.1 2.3 fusion.173
  11.1 141.0 %psum.85 = f32[256]{0:T(256)S(1)} all-reduce(f32[256]{0:T(256)S(1)} %fusion.116), channel_id=1, replica_groups=mesh['grp'=2,'tp'=64] {'tp'}, use_global_device_ids=true, to_apply=%region_2.0 | all-reduce | flops 256 | bytes 2048 | tf_op jit(solution)/shard_map/psum | solution.py:48
  152.1 410.3 %all-reduce.9.cloned.1.call-done = f32[256,1024]{1,0:T(8,128)} async-done(((f32[256,1024]{1,0:T(8,128)}), f32[256,1024]{1,0:T(8,128)}) %all-reduce.9.cloned.1.call-update) | async-done | bytes 1048592 | tf_op jit(solution)/shard_map/psum | solution.py:48
  562.4 2.1 multiply_convert_fusion.1
  565.3 9.3 reshape.38
  574.7 5.2 convolution_convert_fusion
  579.9 10.2 all-gather.6.cloned.1.call-done
  595.6 1.8 convolution_dynamic-update-slice_fusion.13
  606.1 65.8 %psum.87 = f32[512,8]{0,1:T(8,128)S(1)} all-reduce(f32[512,8]{0,1:T(8,128)S(1)} %stack.35), channel_id=1, replica_groups=mesh['grp'=2,'tp'=64] {'grp','tp'}, use_global_device_ids=true, to_apply=%region_12.0 | all-reduce | flops 4096 | bytes 32768 | tf_op jit(solution)/shard_map/psum | solution.py:86
  671.9 83.8 %all-reduce.11.cloned.1.call-done = f32[512,1024]{0,1:T(8,128)} async-done(((f32[512,1024]{0,1:T(8,128)}), f32[512,1024]{0,1:T(8,128)}) %all-reduce.11.cloned.1.call-update) | async-done | bytes 2097168 | tf_op jit(solution)/shard_map/psum | solution.py:86
  758.1 101.9 %all-gather.8.cloned.1.call-done = bf16[256,4096]{0,1:T(8,128)(2,1)} async-done(((bf16[256,64]{0,1:T(8,128)(2,1)}), bf16[256,4096]{0,1:T(8,128)(2,1)}) %all-gather.8.cloned.1.call-update) | async-done | bytes 2097168 | tf_op jit(solution)/shard_map/all_gather | solution.py:97
  860.0 2.2 multiply_reduce_fusion.1
  862.2 138.1 %psum.88 = f32[256]{0:T(256)S(1)} all-reduce(f32[256]{0:T(256)S(1)} %get-tuple-element.54), channel_id=1, replica_groups=mesh['grp'=2,'tp'=64] {'tp'}, use_global_device_ids=true, to_apply=%region_14.0 | all-reduce | flops 256 | bytes 2048 | tf_op jit(solution)/shard_map/psum | solution.py:102
  1000.4 141.2 %psum.89 = f32[256]{0:T(256)S(1)} all-reduce(f32[256]{0:T(256)S(1)} %get-tuple-element.29), channel_id=1, replica_groups=mesh['grp'=2,'tp'=64] {'tp'}, use_global_device_ids=true, to_apply=%region_16.0 | all-reduce | flops 256 | bytes 2048 | tf_op jit(solution)/shard_map/psum | solution.py:109
  1141.7 2.6 fusion.175
  1144.4 280.8 %reduce-scatter.3.cloned.1.call-done = f32[256,64]{0,1:T(8,128)} async-done(((f32[256,4096]{0,1:T(8,128)}), f32[256,64]{0,1:T(8,128)}) %reduce-scatter.3.cloned.1.call-update) | async-done | bytes 65552 | tf_op jit(solution)/shard_map/reduce_scatter | solution.py:117
  1425.2 2.2 fusion.155
  1427.4 284.4 %all-reduce.16 = bf16[256,1024]{0,1:T(8,128)(2,1)S(1)} all-reduce(f32[256,1024]{0,1:T(8,128)} %fusion.155), channel_id=1, replica_groups=mesh['grp'=2,'tp'=64] {'tp'}, use_global_device_ids=true, to_apply=%region_18.0 | all-reduce | flops 262144 | bytes 1572864 | tf_op jit(solution)/shard_map/psum | solution.py:121
  1712.9 5.0 all_gather.19
  1717.9 22.0 %all-gather.10.cloned.1.call-done = bf16[512,1024]{0,1:T(8,128)(2,1)} async-done(((bf16[256,1024]{0,1:T(8,128)(2,1)}), bf16[512,1024]{0,1:T(8,128)(2,1)}) %all-gather.10.cloned.1.call-update) | async-done | bytes 1048592 | tf_op jit(solution)/shard_map/all_gather | solution.py:131
  1740.0 1.4 fusion.39
  1751.8 7.0 convolution_bitcast_fusion
  1758.9 3.7 fusion.174
  1763.5 170.8 %all-reduce.13.cloned.1.call-done = (f32[512,1024]{1,0:T(8,128)}, f32[1664,2048]{0,1:T(8,128)}) async-done(((f32[512,1024]{1,0:T(8,128)}, f32[1664,2048]{0,1:T(8,128)}), (f32[512,1024]{1,0:T(8,128)}, f32[1664,2048]{0,1:T(8,128)})) %all-reduce.13.cloned.1.call-update) | async-done | bytes 15728656 | tf_op jit(solution)/shard_map/psum | solution.py:159
  1934.3 2.2 convolution_bitcast_fusion.1
  1937.3 5.8 psum.95
  1943.0 1.9 constant_dynamic-slice_fusion.1
  1946.0 1.4 multiply_reduce_fusion
  1948.4 69.9 %all-reduce.15.cloned.1.call-done = (f32[64,1024]{1,0:T(8,128)}, f32[1024,64]{0,1:T(8,128)}, f32[4096,128]{1,0:T(8,128)}) async-done(((f32[64,1024]{1,0:T(8,128)}, f32[1024,64]{0,1:T(8,128)}, f32[4096,128]{1,0:T(8,128)}), (f32[64,1024]{1,0:T(8,128)}, f32[1024,64]{0,1:T(8,128)}, f32[4096,128]{1,0:T(8,128)})) %all-reduce.15.cloned.1.call-update) | async-done | bytes 2621456 | tf_op jit(solution)/shard_map/psum | solution.py:166
  2018.2 1.7 copy.135
  2019.9 1.8 copy.136
  2021.7 3.0 copy.137
  (149 shorter events, 32.5 us)
Async XLA Ops:
  8.0 852.0 %copy-start = (bf16[4096,128]{1,0:T(8,128)(2,1)S(1)}, bf16[4096,128]{1,0:T(8,128)(2,1)}, u32[]{:S(2)}) copy-start(bf16[4096,128]{1,0:T(8,128)(2,1)} %param.17) | copy-start | bytes 3145732
  8.0 3.0 copy-start.23
  8.0 557.3 %copy-start.29 = (s32[256]{0:T(256)S(1)}, s32[256]{0:T(256)}, u32[]{:S(2)}) copy-start(s32[256]{0:T(256)} %param.11) | copy-start | bytes 3076
  8.0 554.4 %all-reduce.9.cloned.1.call-start = ((), (), s32[]{:S(2)}) async-start(), calls=%async_computation.1 | async-start | bytes 2097152 | tf_op jit(solution)/shard_map/psum | solution.py:48
  10.4 554.9 %all-gather.12.cloned.1.call-start = ((), (), s32[]{:S(2)}) async-start(), calls=%async_computation.7 | async-start | bytes 8454144 | tf_op jit(solution)/shard_map/all_gather | solution.py:52
  11.0 579.1 %all-gather.6.cloned.1.call-start = ((), (), s32[]{:S(2)}) async-start(), calls=%async_computation.2 | async-start | bytes 1572864 | tf_op jit(solution)/shard_map/all_gather | solution.py:51
  564.6 191.1 %all-reduce.11.cloned.1.call-start = ((), (), s32[]{:S(2)}) async-start(), calls=%async_computation.3 | async-start | bytes 4194304 | tf_op jit(solution)/shard_map/psum | solution.py:86
  565.3 9.4 copy-start.21
  579.9 13.6 copy-start.15
  590.1 4.4 copy-start.12
  591.3 11.9 copy-start.9
  594.4 4.1 copy-start.16
  599.8 4.4 copy-start.3
  601.0 3.1 copy-start.5
  606.0 151.1 %copy-start.26 = (bf16[1024,64]{0,1:T(8,128)(2,1)S(1)}, bf16[1024,64]{0,1:T(8,128)(2,1)}, u32[]{:S(2)}) copy-start(bf16[1024,64]{0,1:T(8,128)(2,1)} %param.16) | copy-start | bytes 393220
  606.0 152.0 %copy-start.30 = (bf16[128]{0:T(256)(128)(2,1)S(1)}, bf16[128]{0:T(256)(128)(2,1)}, u32[]{:S(2)}) copy-start(bf16[128]{0:T(256)(128)(2,1)} %param.18) | copy-start | bytes 772
  606.0 152.0 %copy-start.28 = (bf16[256,128]{1,0:T(8,128)(2,1)S(1)}, bf16[256,128]{1,0:T(8,128)(2,1)}, u32[]{:S(2)}) copy-start(bf16[256,128]{1,0:T(8,128)(2,1)} %param.19) | copy-start | bytes 196612
  606.0 254.0 %all-gather.8.cloned.1.call-start = ((), (), s32[]{:S(2)}) async-start(), calls=%async_computation.4 | async-start | bytes 2129920 | tf_op jit(solution)/shard_map/all_gather | solution.py:97
  757.9 667.3 %reduce-scatter.3.cloned.1.call-start = ((), (), s32[]{:S(2)}) async-start(), calls=%async_computation.5 | async-start | bytes 4259840 | tf_op jit(solution)/shard_map/reduce_scatter | solution.py:117
  1144.3 280.9 %copy-start.27 = (bf16[1024,64]{0,1:T(8,128)(2,1)S(1)}, bf16[1024,64]{0,1:T(8,128)(2,1)}, u32[]{:S(2)}) copy-start(bf16[1024,64]{0,1:T(8,128)(2,1)} %param.16) | copy-start | bytes 393220
  1144.4 595.6 %all-gather.10.cloned.1.call-start = ((), (), s32[]{:S(2)}) async-start(), calls=%async_computation.6 | async-start | bytes 1572864 | tf_op jit(solution)/shard_map/all_gather | solution.py:131
  1427.4 312.6 %copy-start.10 = (f32[512,256]{0,1:T(8,128)S(1)}, f32[512,256]{0,1:T(8,128)}, u32[]{:S(2)}) copy-start(f32[512,256]{0,1:T(8,128)} %copy-done.9) | copy-start | bytes 1572868
  1712.7 221.6 %all-reduce.13.cloned.1.call-start = ((), (), s32[]{:S(2)}) async-start(), calls=%async_computation.8 | async-start | bytes 31457280 | tf_op jit(solution)/shard_map/psum | solution.py:159
  1740.0 3.7 copy-start.17
  1740.0 4.0 copy-start.20
  1747.0 2.3 copy-start.11
  1747.5 2.2 copy-start.14
  1758.8 3.7 copy-start.24
  1758.8 259.4 %all-reduce.15.cloned.1.call-start = ((), (), s32[]{:S(2)}) async-start(), calls=%async_computation.9 | async-start | bytes 5242880 | tf_op jit(solution)/shard_map/psum | solution.py:166
  1936.5 9.5 copy-start.2
  1945.0 2.4 copy-start.25
  2019.9 4.8 copy-start.1
  (8 other events, 10.3 us)
Sparse Core Ops, SparseCore 0:
  11.9 550.4 all-reduce.8
  758.0 101.9 all-gather.7
  1144.5 280.6 reduce-scatter.2
Sparse Core Ops, SparseCore 1:
  12.7 207.3 all-gather.11
  564.7 25.4 all-gather.5
  606.1 149.6 all-reduce.10
  1712.8 27.2 all-gather.9
  1758.9 175.3 all-reduce.12
  1937.7 80.5 all-reduce.14
where the time goes:
time: 2030 us
  waiting for transfers between devices  1150 us (57%)
  blocking collectives  781 us (38%)
  matrix products  56.3 us (3%)
  local copies, waits for them, and re-layouts  20.7 us (1%)
    psum x1, waiting for transfers between devices, local(): square_total, proj_query = lax.psum((square_part, product_part), 'tp')  410 us
    psum x1, blocking collectives, local(): lax.psum(col_dot(grad_lat_out, output_weight), 'tp').astype(jnp.bfloat16)  284 us
    reduce_scatter x1, waiting for transfers between devices, local(): lax.psum_scatter(col_dot(grad_hidden, project_weight), 'tp', scatter_dime...  281 us
    psum x1, waiting for transfers between devices, local(): query_whole = lax.psum(query_part, ('grp', 'tp'))  171 us
    psum x1, blocking collectives, local(): dot_total = lax.psum(jnp.sum(hidden_f32 * scaled_dy, axis=1), 'tp')  141 us
    psum x1, blocking collectives, local(): square_total, proj_query = lax.psum((square_part, product_part), 'tp')  141 us
    psum x1, blocking collectives, local(): hidden_square = lax.psum(jnp.sum(hidden_f32 * hidden_f32, axis=1), 'tp')  138 us
    all_gather x1, waiting for transfers between devices, local(): latents_full = lax.all_gather(latents_out, 'tp', axis=1, tiled=True)  102 us
  transfers between devices with their start and end apart: 9, of which 8 were waited for; matrix products, arithmetic and copies ran while one was open for 1% of the time, Pallas kernels for 0%

commit v1 on v0

v1 whole, which is shorter than its diff:
```python
import functools
import math

import jax
import jax.numpy as jnp
import numpy as np
from jax import lax
from jax.experimental import pallas as pl
from jax.experimental.pallas import tpu as pltpu
from jax.sharding import PartitionSpec as P

D_LAT = 4096
HEAD_DIM = 128
D_LLM = 8192
SCORE_CAP = 5.0
SCALE = 1.0 / math.sqrt(HEAD_DIM)
CHIPS = 64
GROUP = 64

F32 = jnp.float32
BF16 = jnp.bfloat16
MESH = pl.DeviceIdType.MESH
ANY = pl.BlockSpec(memory_space=pl.ANY)
VMEM = pl.BlockSpec(memory_space=pltpu.VMEM)

ORDERS = ((2, 1, 0), (1, 0, 2), (0, 2, 1))
WIDE = ((0, 384), (384, 384), (768, 256))
WIDE_TURNED = ((0, 256), (256, 384), (640, 384))
ROWS_64 = ((0, 16), (16, 32), (48, 16))


def row_dot(left, right):
    return lax.dot_general(left, right, (((0,), (0,)), ((), ())), preferred_element_type=F32)


def col_dot(left, right):
    return lax.dot_general(left, right, (((1,), (1,)), ((), ())), preferred_element_type=F32)


def dot(left, right):
    return jnp.dot(left, right, preferred_element_type=F32)


class Place:
    def __init__(self):
        self.g = lax.axis_index("grp")
        self.t = lax.axis_index("tp")
        self.core = self.t % 2
        self.j = self.t // 2
        self.z = self.j % 4
        self.xl = (self.j // 4) % 2
        self.y = self.j // 8
        self.x = self.g * 2 + self.xl

    def chip(self, x, y, z):
        return x // 2, (y * 2 + x % 2) * 4 + z

    def plane_peer(self, k):
        return self.chip((self.x + k // 16) % 4, (self.y + (k // 4) % 4) % 4, (self.z + k % 4) % 4)

    def group_peer(self, k):
        y = (self.y + k // 16) % 4
        xl = (self.xl + (k // 8) % 2) % 2
        z = (self.z + (k // 2) % 4) % 4
        return ((y * 2 + xl) * 4 + z) * 2 + (self.core + k % 2) % 2

    def sibling(self):
        return self.g, self.j * 2 + 1 - self.core


def remote(src, dst, sends, recvs, device):
    return pltpu.make_async_remote_copy(
        src_ref=src, dst_ref=dst, send_sem=sends, recv_sem=recvs, device_id=device, device_id_type=MESH
    )


def each_peer(n, do):
    def body(k, carry):
        do(k)
        return carry

    lax.fori_loop(1, n, body, 0)


class Gather:
    def __init__(self, place, ref, view, sends, recvs):
        self.place, self.ref, self.view, self.sends, self.recvs = place, ref, view, sends, recvs

    def copies(self, phase):
        pc = self.place
        mine = [pc.x, pc.y, pc.z]
        for part, order in enumerate(ORDERS):
            held = list(mine)
            for axis in order[:phase]:
                held[axis] = None
            block = self.view(self.ref, *held, part)
            for step in (1, 3, 2):
                peer = list(mine)
                peer[order[phase]] = (peer[order[phase]] + step) % 4
                g, j = pc.chip(*peer)
                spot = (part * 3 + phase) * 3 + step - 1
                yield remote(
                    block, block, self.sends.at[spot], self.recvs.at[spot], (g, j * 2 + pc.core)
                )

    def start(self, phase):
        for copy in self.copies(phase):
            copy.start()

    def wait(self, phase):
        for copy in self.copies(phase):
            copy.wait_recv()

    def drain(self):
        for phase in range(3):
            for copy in self.copies(phase):
                copy.wait_send()


def pick(value):
    return slice(None) if value is None else value


def halves(x):
    return (slice(None), slice(None)) if x is None else (x // 2, x % 2)


def view_weight(ref, x, y, z, part):
    return ref.at[pick(x), pick(y), pick(z), :, :, pl.ds(*WIDE[part])]


def view_output(core, ref, x, y, z, part):
    hi, lo = halves(x)
    return ref.at[pick(y), lo, pick(z), core, hi, :, pl.ds(*WIDE_TURNED[part])]


def view_latents(core, ref, x, y, z, part):
    hi, lo = halves(x)
    return ref.at[hi, pick(y), lo, pick(z), core, pl.ds(*ROWS_64[part]), :]


def total_slots(own, slots, n):
    def body(k, total):
        return total + slots[k].astype(F32)

    return lax.fori_loop(1, n, body, own.astype(F32))


def start_kernel(
    wpl, tokp, val, qpart, owt, lt,
    wg, tg, vg, qg, owg, lg, proj, rinv,
    recvq, qblk, w_s, w_r, ow_s, ow_r, l_s, l_r, q_s, q_r, qa_s, qa_r, sib_s, sib_r, loc,
):
    pc = Place()
    core = pc.core
    sib = pc.sibling()
    rows = pl.multiple_of((pc.j // 2) * 16, 16)

    w_sib = remote(wpl.at[1 - core], wg.at[pc.x, pc.y, pc.z, core], sib_s.at[0], sib_r.at[0], sib)
    w_sib.start()
    w_own = pltpu.make_async_copy(wpl.at[core], wg.at[pc.x, pc.y, pc.z, core], loc.at[0])
    w_own.start()

    def q_copy(k):
        t = pc.group_peer(k)
        j, c = t // 2, t % 2
        src = qpart.at[c * 2 + j % 2, pl.ds(pl.multiple_of((j // 2) * 16, 16), 16), :]
        return remote(src, recvq.at[k], q_s.at[k], q_r.at[k], (pc.g, t))

    each_peer(GROUP, lambda k: q_copy(k).start())
    t_sib = remote(tokp, tg.at[core], sib_s.at[1], sib_r.at[1], sib)
    t_sib.start()
    v_sib = remote(val, vg.at[core], sib_s.at[2], sib_r.at[2], sib)
    v_sib.start()
    own = [
        pltpu.make_async_copy(tokp, tg.at[core], loc.at[1]),
        pltpu.make_async_copy(val, vg.at[core], loc.at[2]),
        pltpu.make_async_copy(
            owt.at[pl.ds(pl.multiple_of(pc.g * 32, 32), 32), :],
            owg.at[pc.y, pc.xl, pc.z, core, pc.g],
            loc.at[3],
        ),
        pltpu.make_async_copy(lt, lg.at[pc.g, pc.y, pc.xl, pc.z, core], loc.at[4]),
    ]
    for copy in own:
        copy.start()

    weight = Gather(pc, wg, view_weight, w_s, w_r)
    output = Gather(pc, owg, functools.partial(view_output, core), ow_s, ow_r)
    latents = Gather(pc, lg, functools.partial(view_latents, core), l_s, l_r)
    w_own.wait()
    w_sib.wait_recv()
    weight.start(0)

    each_peer(GROUP, lambda k: q_copy(k).wait_recv())
    total = total_slots(qpart[core * 2 + pc.j % 2, pl.ds(rows, 16), :], recvq, GROUP)
    inv = lax.rsqrt(total[:, 256:] / D_LAT + 1e-06)
    rinv[...] = inv
    proj[...] = total[:, :256]
    qblk[...] = (total[:, :256] * inv[:, :1]).astype(BF16)
    columns = pl.multiple_of((pc.j % 2) * 256, 256)
    q_spot = qg.at[pl.ds(pl.multiple_of(pc.g * 256 + rows, 16), 16), pl.ds(columns, 256)]

    def qa_copy(k):
        g, j = pc.plane_peer(k)
        return remote(qblk, q_spot, qa_s.at[k], qa_r.at[k], (g, j * 2 + core))

    each_peer(CHIPS, lambda k: qa_copy(k).start())
    q_own = pltpu.make_async_copy(qblk, q_spot, loc.at[5])
    q_own.start()

    weight.wait(0)
    weight.start(1)
    for copy in own:
        copy.wait()
    latents.start(0)
    output.start(0)
    weight.wait(1)
    weight.start(2)
    latents.wait(0)
    latents.start(1)
    output.wait(0)
    output.start(1)
    weight.wait(2)
    latents.wait(1)
    latents.start(2)
    output.wait(1)
    output.start(2)
    each_peer(CHIPS, lambda k: qa_copy(k).wait_recv())
    q_own.wait()
    latents.wait(2)
    output.wait(2)
    t_sib.wait()
    v_sib.wait()
    w_sib.wait_send()
    each_peer(GROUP, lambda k: q_copy(k).wait_send())
    each_peer(CHIPS, lambda k: qa_copy(k).wait_send())
    for gather in (weight, latents, output):
        gather.drain()


def attend_kernel(
    npk, owi, li,
    attf, ow, la, ablk, tot,
    recv, s_s, s_r, a_s, a_r, sib_s, sib_r, loc,
):
    pc = Place()
    core = pc.core
    sib = pc.sibling()
    rows = pl.multiple_of(pc.g * 256 + (pc.j // 2) * 16, 16)
    pair = pc.j % 2

    def n_copy(k):
        g, j = pc.plane_peer(k)
        src = npk.at[j % 2, pl.ds(pl.multiple_of(g * 256 + (j // 2) * 16, 16), 16), :]
        return remote(src, recv.at[k], s_s.at[k], s_r.at[k], (g, j * 2 + core))

    each_peer(CHIPS, lambda k: n_copy(k).start())
    big = [
        remote(ow.at[:, :, :, core], ow.at[:, :, :, core], sib_s.at[0], sib_r.at[0], sib),
        remote(la.at[:, :, :, :, core], la.at[:, :, :, :, core], sib_s.at[1], sib_r.at[1], sib),
    ]
    for copy in big:
        copy.start()
    each_peer(CHIPS, lambda k: n_copy(k).wait_recv())
    total = total_slots(npk[pair, pl.ds(rows, 16), :], recv, CHIPS)
    first = total[:, 256:257]
    second = total[:, 320:321]
    both = jnp.concatenate(
        [jnp.broadcast_to(first, (16, 128)), jnp.broadcast_to(second, (16, 128))], axis=1
    )
    tot[...] = both
    ablk[...] = (total[:, :256] / both).astype(BF16)
    spot = attf.at[core, pl.ds(rows, 16), pl.ds(pl.multiple_of(pair * 256, 256), 256)]

    def a_copy(k):
        g, j = pc.plane_peer(k)
        return remote(ablk, spot, a_s.at[k], a_r.at[k], (g, j * 2 + core))

    each_peer(CHIPS, lambda k: a_copy(k).start())
    own = pltpu.make_async_copy(ablk, spot, loc.at[0])
    own.start()
    own.wait()
    each_peer(CHIPS, lambda k: a_copy(k).wait_recv())
    cross = remote(attf.at[core], attf.at[core], sib_s.at[2], sib_r.at[2], sib)
    cross.start()
    cross.wait()
    for copy in big:
        copy.wait()
    each_peer(CHIPS, lambda k: n_copy(k).wait_send())
    each_peer(CHIPS, lambda k: a_copy(k).wait_send())


def sums_kernel(part, out, recv, s_s, s_r):
    pc = Place()

    def copy(k):
        return remote(part, recv.at[k], s_s.at[k], s_r.at[k], (pc.g, pc.group_peer(k)))

    each_peer(GROUP, lambda k: copy(k).start())
    each_peer(GROUP, lambda k: copy(k).wait_recv())
    out[...] = total_slots(part[...], recv, GROUP)
    each_peer(GROUP, lambda k: copy(k).wait_send())


def grad_kernel(
    gap, glp, gh, att, tot,
    gg, gl, ghf,
    recv, recvl, gblk, lblk, g_s, g_r, l_s, l_r, a_s, a_r, x_s, x_r, loc,
):
    pc = Place()
    core = pc.core
    pair = pc.j % 2
    rows = pl.multiple_of((pc.j // 2) * 16, 16)
    partner = (1 - pc.g, pc.t)

    def g_copy(k):
        t = pc.group_peer(k)
        j, c = t // 2, t % 2
        src = gap.at[
            pl.ds(pl.multiple_of((j // 2) * 16, 16), 16),
            pl.ds(pl.multiple_of((c * 2 + j % 2) * 256, 256), 256),
        ]
        return remote(src, recv.at[k], g_s.at[k], g_r.at[k], (pc.g, t))

    def l_copy(k):
        t = pc.group_peer(k)
        return remote(glp.at[t], recvl.at[k], l_s.at[k], l_r.at[k], (pc.g, t))

    each_peer(GROUP, lambda k: g_copy(k).start())
    h_cross = remote(gh, ghf.at[pc.g], x_s.at[0], x_r.at[0], partner)
    h_cross.start()
    each_peer(GROUP, lambda k: l_copy(k).start())
    own = [
        pltpu.make_async_copy(gh, ghf.at[pc.g], loc.at[0]),
        pltpu.make_async_copy(glp.at[pc.t], recvl.at[0], loc.at[1]),
    ]
    for copy in own:
        copy.start()

    each_peer(GROUP, lambda k: g_copy(k).wait_recv())
    mine = gap[pl.ds(rows, 16), pl.ds(pl.multiple_of((core * 2 + pair) * 256, 256), 256)]
    grad = total_slots(mine, recv, GROUP).astype(BF16).astype(F32)
    whole = tot[...]
    prod = grad * att[...].astype(F32)
    first = jnp.sum(prod[:, :128], axis=1, keepdims=True) / whole[:, :1]
    second = jnp.sum(prod[:, 128:], axis=1, keepdims=True) / whole[:, 128:129]
    lane = lax.broadcasted_iota(jnp.int32, (16, 128), 1)
    gblk[:, :256] = (grad / whole).astype(BF16)
    gblk[:, 256:] = jnp.where(lane < 64, first, second).astype(BF16)
    spot = gg.at[pair, pl.ds(pl.multiple_of(pc.g * 256 + rows, 16), 16), :]

    def a_copy(k):
        g, j = pc.plane_peer(k)
        return remote(gblk, spot, a_s.at[k], a_r.at[k], (g, j * 2 + core))

    each_peer(CHIPS, lambda k: a_copy(k).start())
    mine_g = pltpu.make_async_copy(gblk, spot, loc.at[2])
    mine_g.start()

    for copy in own:
        copy.wait()
    each_peer(GROUP, lambda k: l_copy(k).wait_recv())
    lblk[...] = total_slots(recvl[0], recvl, GROUP).astype(BF16)
    l_cross = remote(lblk, gl.at[pc.g], x_s.at[1], x_r.at[1], partner)
    l_cross.start()
    mine_l = pltpu.make_async_copy(lblk, gl.at[pc.g], loc.at[3])
    mine_l.start()
    each_peer(CHIPS, lambda k: a_copy(k).wait_recv())
    l_cross.wait()
    h_cross.wait()
    mine_g.wait()
    mine_l.wait()
    each_peer(GROUP, lambda k: g_copy(k).wait_send())
    each_peer(GROUP, lambda k: l_copy(k).wait_send())
    each_peer(CHIPS, lambda k: a_copy(k).wait_send())


def end_kernel(
    gqp, gp, proj, rinv,
    sq, gw,
    recv, sblk, r1a, r1b, r1c, s1a, s1b, s1c, r2a, r2b, r2c, s2a, s2b, s2c, r3a, r3b, r3c, fin, oth,
    g_s, g_r, a_s, a_r, p_s, p_r, x_s, x_r, loc,
):
    pc = Place()
    core = pc.core
    pair = pc.j % 2
    sib = pc.sibling()
    rows = pl.multiple_of(pc.g * 256 + (pc.j // 2) * 16, 16)
    mine = [pc.x, pc.y, pc.z]
    first, once = (r1a, r1b, r1c), (s1a, s1b, s1c)
    second, twice = (r2a, r2b, r2c), (s2a, s2b, s2c)
    third = (r3a, r3b, r3c)

    def g_copy(k):
        g, j = pc.plane_peer(k)
        src = gqp.at[
            pl.ds(pl.multiple_of(g * 256 + (j // 2) * 16, 16), 16),
            pl.ds(pl.multiple_of((j % 2) * 256, 256), 256),
        ]
        return remote(src, recv.at[k], g_s.at[k], g_r.at[k], (g, j * 2 + core))

    def slab(part, phase, spot):
        order = ORDERS[part]
        index = [spot if axis == order[phase] else slice(None) for axis in range(3) if axis not in order[:phase]]
        if phase == 0:
            return gp.at[(*index, slice(None), pl.ds(*WIDE[part]))]
        return (once, twice)[phase - 1][part].at[tuple(index)]

    def copies(part, phase):
        axis = ORDERS[part][phase]
        for step in (1, 3, 2):
            peer = list(mine)
            peer[axis] = (peer[axis] + step) % 4
            g, j = pc.chip(*peer)
            spot = (part * 3 + phase) * 3 + step - 1
            yield remote(
                slab(part, phase, peer[axis]),
                (first, second, third)[phase][part].at[step],
                p_s.at[spot], p_r.at[spot], (g, j * 2 + core),
            )

    each_peer(CHIPS, lambda k: g_copy(k).start())
    own = []
    for part in range(3):
        for copy in copies(part, 0):
            copy.start()
        copy = pltpu.make_async_copy(
            slab(part, 0, mine[ORDERS[part][0]]), first[part].at[0], loc.at[part]
        )
        copy.start()
        own.append(copy)

    each_peer(CHIPS, lambda k: g_copy(k).wait_recv())
    grad = total_slots(
        gqp[pl.ds(rows, 16), pl.ds(pl.multiple_of(pair * 256, 256), 256)], recv, CHIPS
    )
    sblk[:, :256] = (grad * rinv[:, :1]).astype(BF16)
    ratio = jnp.sum(grad * proj[...], axis=1, keepdims=True)
    sblk[:, 256:] = jnp.broadcast_to(ratio, (16, 128)).astype(BF16)
    spot_q = sq.at[core, pair, pl.ds(rows, 16), :]

    def a_copy(k):
        g, j = pc.plane_peer(k)
        return remote(sblk, spot_q, a_s.at[k], a_r.at[k], (g, j * 2 + core))

    each_peer(CHIPS, lambda k: a_copy(k).start())
    own_q = pltpu.make_async_copy(sblk, spot_q, loc.at[3])
    own_q.start()

    for part in range(3):
        own[part].wait()
        for copy in copies(part, 0):
            copy.wait_recv()
        src, dst = first[part], once[part]

        def add_first(n, carry, src=src, dst=dst):
            a, b = n // 4, n % 4
            dst[a, b] = sum(src[s, a, b].astype(F32) for s in range(4)).astype(BF16)
            return carry

        lax.fori_loop(0, 16, add_first, 0)
        for copy in copies(part, 1):
            copy.start()

    own_q.wait()
    each_peer(CHIPS, lambda k: a_copy(k).wait_recv())
    cross = remote(sq.at[core], sq.at[core], x_s.at[0], x_r.at[0], sib)
    cross.start()

    for part in range(3):
        for copy in copies(part, 1):
            copy.wait_recv()
        src, dst, held = second[part], twice[part], once[part]
        left = [axis for axis in range(3) if axis != ORDERS[part][0]]
        leading = left[0] == ORDERS[part][1]
        here = mine[ORDERS[part][1]]

        def add_second(n, carry, src=src, dst=dst, held=held, leading=leading, here=here):
            base = held[here, n] if leading else held[n, here]
            dst[n] = (base.astype(F32) + sum(src[s, n].astype(F32) for s in range(1, 4))).astype(BF16)
            return carry

        lax.fori_loop(0, 4, add_second, 0)
        for copy in copies(part, 2):
            copy.start()
    for part in range(3):
        for copy in copies(part, 2):
            copy.wait_recv()
        here = mine[ORDERS[part][2]]
        fin[:, pl.ds(*WIDE[part])] = twice[part][here].astype(F32) + sum(
            third[part][s].astype(F32) for s in range(1, 4)
        )
    give = remote(
        fin.at[pl.ds(pl.multiple_of((1 - core) * 16, 16), 16), :], oth, x_s.at[1], x_r.at[1], sib
    )
    give.start()
    gw[core] = fin[pl.ds(pl.multiple_of(core * 16, 16), 16), :]
    give.wait()
    gw[1 - core] = oth[...]
    cross.wait()
    for part in range(3):
        for phase in range(3):
            for copy in copies(part, phase):
                copy.wait_send()
    each_peer(CHIPS, lambda k: g_copy(k).wait_send())
    each_peer(CHIPS, lambda k: a_copy(k).wait_send())


def sems(*counts):
    return [pltpu.SemaphoreType.DMA((n,)) for n in counts]


def call(body, outs, ins_any, outs_any, scratch, aliases=None, name=None):
    def spec(is_any):
        return ANY if is_any else VMEM

    return pl.pallas_call(
        body,
        out_shape=[jax.ShapeDtypeStruct(s, d) for s, d in outs],
        in_specs=[spec(a) for a in ins_any],
        out_specs=[spec(a) for a in outs_any],
        scratch_shapes=scratch,
        input_output_aliases=aliases or {},
        compiler_params=pltpu.CompilerParams(has_side_effects=True, vmem_limit_bytes=40 << 20),
        name=name,
    )


def spread_matrix():
    row = lax.broadcasted_iota(jnp.int32, (1664, 2048), 0)
    col = lax.broadcasted_iota(jnp.int32, (1664, 2048), 1)
    dev, rest = col // 16, col % 16
    core, z, y, x = dev % 2, (dev // 2) % 4, (dev // 8) % 4, dev // 32
    t = ((y * 2 + x % 2) * 4 + z) * 2 + core
    src = ((x // 2) * 64 + t) * 13 + rest
    return ((row == src) & (rest < 13)).astype(BF16)


def local(
    tokens, keep_mask, shard_counts, latents, query_weight, keyval_weight, output_weight,
    project_weight, llm_gain, input_grad,
):
    g = lax.axis_index("grp")
    t = lax.axis_index("tp")
    latent_f32 = latents.astype(F32)

    squares = jnp.sum(latent_f32 * latent_f32, axis=1)
    product = dot(latents, query_weight)
    qpart = jnp.concatenate(
        [
            product.reshape(256, 4, 256).transpose(1, 0, 2),
            jnp.broadcast_to(squares[None, :, None], (4, 256, 128)),
        ],
        axis=2,
    ).astype(BF16)
    padded = jnp.pad(keyval_weight, ((0, 3), (0, 0)))
    wpl = padded.reshape(16, 2, 2, 512).transpose(2, 0, 1, 3).reshape(2, 16, 1024)
    tokp = dot(tokens, spread_matrix()).astype(BF16)
    positions = jnp.arange(256, dtype=jnp.int32)
    valid = (((keep_mask == 1) | (positions == 0)) & (positions < shard_counts[0])).astype(F32)
    val = jnp.broadcast_to(valid[None, :], (8, 256))
    owt = output_weight.T
    lt = latents.T

    wg, tg, vg, qg, owg, lg, proj, rinv = call(
        start_kernel,
        [
            ((4, 4, 4, 2, 16, 1024), BF16),
            ((2, 256, 2048), BF16),
            ((2, 8, 256), F32),
            ((512, 512), BF16),
            ((4, 2, 4, 2, 2, 32, 1024), BF16),
            ((2, 4, 2, 4, 2, 64, 256), BF16),
            ((16, 256), F32),
            ((16, 128), F32),
        ],
        [1, 1, 1, 0, 1, 1],
        [1, 1, 1, 1, 1, 1, 0, 0],
        [pltpu.VMEM((64, 16, 384), BF16), pltpu.VMEM((16, 256), BF16)]
        + sems(27, 27, 27, 27, 27, 27, 64, 64, 64, 64, 3, 3, 6),
        name="start",
    )(wpl, tokp, val, qpart, owt, lt)

    tok = tg.reshape(512, 2048)
    keyval = dot(tok, wg.reshape(2048, 1024)).astype(BF16)
    valid_rows = vg[:, 0, :].reshape(512)
    saved = []
    numer_list = []
    for pair in range(2):
        cols = []
        sums = []
        for half in range(2):
            lower = (pair * 2 + half) * HEAD_DIM
            raw = col_dot(qg[:, lower : lower + HEAD_DIM], keyval[:, lower : lower + HEAD_DIM]) * SCALE
            squash = jnp.tanh(raw / SCORE_CAP)
            weights = jnp.exp(SCORE_CAP * squash) * valid_rows[None, :]
            weights_half = weights.astype(BF16)
            cols.append(dot(weights_half, keyval[:, 512 + lower : 512 + lower + HEAD_DIM]))
            sums.append(jnp.broadcast_to(jnp.sum(weights, axis=1)[:, None], (512, 64)))
            saved.append((squash, weights, weights_half))
        numer_list.append(jnp.concatenate(cols + sums, axis=1))
    npk = jnp.stack(numer_list, axis=0).astype(BF16)

    attf, ow, la, ablk, tot = call(
        attend_kernel,
        [
            ((2, 512, 512), BF16),
            ((4, 2, 4, 2, 2, 32, 1024), BF16),
            ((2, 4, 2, 4, 2, 64, 256), BF16),
            ((16, 256), BF16),
            ((16, 256), F32),
        ],
        [0, 1, 1],
        [1, 1, 1, 0, 0],
        [pltpu.VMEM((64, 16, 384), BF16)] + sems(64, 64, 64, 64, 3, 3, 1),
        aliases={1: 1, 2: 2},
        name="attend",
    )(npk, owg, lg)

    out_t = ow.reshape(4096, 1024)
    lat_t = la.reshape(2, 4096, 256)
    fold = row_dot(out_t, project_weight).astype(BF16)
    lat_own = lax.dynamic_index_in_dim(lat_t, g, 0, keepdims=False)
    att_own = lax.dynamic_slice_in_dim(attf, g * 256, 256, 1)
    hidden = (
        row_dot(lat_own, project_weight) + dot(att_own[0], fold[:512]) + dot(att_own[1], fold[512:])
    ).astype(BF16)
    hidden_f32 = hidden.astype(F32)
    gain_f32 = llm_gain.astype(F32)
    grad_f32 = input_grad.astype(F32)
    scaled_dy = grad_f32 * gain_f32[None, :]
    sums = jnp.concatenate(
        [
            jnp.sum(hidden_f32 * hidden_f32, axis=1).reshape(2, 128),
            jnp.sum(hidden_f32 * scaled_dy, axis=1).reshape(2, 128),
            jnp.zeros((4, 128), F32),
        ],
        axis=0,
    )
    (sums_all,) = call(
        sums_kernel,
        [((8, 128), F32)],
        [0],
        [0],
        [pltpu.VMEM((64, 8, 128), F32)] + sems(64, 64),
        name="sums",
    )(sums)
    hidden_rinv = lax.rsqrt(sums_all[0:2].reshape(256) / D_LLM + 1e-05)
    dot_total = sums_all[2:4].reshape(256)
    normed = hidden_f32 * hidden_rinv[:, None]
    llm_input = (normed * gain_f32[None, :]).astype(BF16)
    gain_part = jnp.sum(grad_f32 * normed, axis=0)
    grad_hidden = (
        hidden_rinv[:, None] * scaled_dy
        - (hidden_rinv**3 / D_LLM * dot_total)[:, None] * hidden_f32
    ).astype(BF16)
    gap = col_dot(grad_hidden, fold).astype(BF16)
    glp = col_dot(project_weight, grad_hidden).astype(BF16).reshape(64, 64, 256)

    gg, gl, ghf = call(
        grad_kernel,
        [((2, 512, 384), BF16), ((2, 64, 256), BF16), ((2, 256, 128), BF16)],
        [0, 1, 1, 0, 0],
        [1, 1, 1],
        [
            pltpu.VMEM((64, 16, 256), BF16),
            pltpu.VMEM((64, 64, 256), BF16),
            pltpu.VMEM((16, 384), BF16),
            pltpu.VMEM((64, 256), BF16),
        ]
        + sems(64, 64, 64, 64, 64, 64, 2, 2, 4),
        name="grad",
    )(gap, glp, grad_hidden, ablk, tot)

    query_list, key_list, value_list = [], [], []
    for head in range(4):
        lower = head * HEAD_DIM
        pair, half = head // 2, head % 2
        squash, weights, weights_half = saved[head]
        grad_head = gg[pair, :, half * 128 : half * 128 + 128]
        delta = gg[pair, :, 256 + half * 64 : 257 + half * 64].astype(F32)
        prob_grad = col_dot(grad_head, keyval[:, 512 + lower : 512 + lower + HEAD_DIM])
        dscore = (weights * (prob_grad - delta) * (1.0 - squash * squash) * SCALE).astype(BF16)
        query_list.append(dot(dscore, keyval[:, lower : lower + HEAD_DIM]))
        key_list.append(row_dot(dscore, qg[:, lower : lower + HEAD_DIM]).astype(BF16))
        value_list.append(row_dot(weights_half, grad_head).astype(BF16))
    gqp = jnp.concatenate(query_list, axis=1).astype(BF16)
    grad_keyval = jnp.concatenate(key_list + value_list, axis=1)
    gp = row_dot(tok, grad_keyval).astype(BF16).reshape(4, 4, 4, 32, 1024)

    widths = [w for _, w in WIDE]
    sq, gw = call(
        end_kernel,
        [((2, 2, 512, 384), BF16), ((2, 16, 1024), F32)],
        [0, 1, 0, 0],
        [1, 0],
        [pltpu.VMEM((64, 16, 256), BF16), pltpu.VMEM((16, 384), BF16)]
        + [pltpu.VMEM((4, 4, 4, 32, w), BF16) for w in widths]
        + [pltpu.VMEM((4, 4, 32, w), BF16) for w in widths]
        + [pltpu.VMEM((4, 4, 32, w), BF16) for w in widths]
        + [pltpu.VMEM((4, 32, w), BF16) for w in widths]
        + [pltpu.VMEM((4, 32, w), BF16) for w in widths]
        + [pltpu.VMEM((32, 1024), F32), pltpu.VMEM((16, 1024), F32)]
        + sems(64, 64, 64, 64, 27, 27, 2, 2, 4),
        name="end",
    )(gqp, gp, proj, rinv)

    grad_keyval_weight = gw[:, :13].reshape(2, 13, 2, 512).transpose(1, 2, 0, 3).reshape(13, 2048)

    gh_all = ghf.reshape(512, 128)
    att_all = jnp.concatenate([attf[0], attf[1]], axis=1)
    mixed = row_dot(att_all, gh_all).astype(BF16)
    grad_project_weight = (
        row_dot(lat_t[0].T, ghf[0]) + row_dot(lat_t[1].T, ghf[1]) + dot(out_t, mixed)
    )
    grad_llm_gain = lax.psum(gain_part, "grp")
    gl_all = gl.transpose(1, 0, 2).reshape(64, 512)
    grad_output_weight = col_dot(att_all.T, gl_all)

    scaled_query = sq[..., :256].transpose(2, 0, 1, 3).reshape(512, 1024)
    ratio = jnp.sum(sq[..., 256].astype(F32), axis=(0, 1))
    lat_feats = lax.dynamic_slice_in_dim(lat_t, t * 64, 64, 1)
    grad_query_weight = dot(lat_feats[0], scaled_query[:256]) + dot(lat_feats[1], scaled_query[256:])
    own_query = lax.dynamic_slice_in_dim(scaled_query, g * 256, 256, 0)
    own_ratio = lax.dynamic_slice_in_dim(ratio, g * 256, 256, 0)
    gl_own = lax.dynamic_index_in_dim(gl, g, 0, keepdims=False)
    square_total = jnp.sum(jnp.square(lat_own.astype(F32)), axis=0)
    latent_rinv = lax.rsqrt(square_total / D_LAT + 1e-06)
    grad_latents = (
        gl_own.T.astype(F32)
        + col_dot(own_query, query_weight)
        - (latent_rinv**3 / D_LAT * own_ratio)[:, None] * latent_f32
    )
    return (
        llm_input,
        grad_latents,
        grad_query_weight,
        grad_keyval_weight,
        grad_output_weight,
        grad_project_weight,
        grad_llm_gain,
    )


def solution(mesh):
    in_specs = (
        P(("grp", "tp"), None),
        P(("grp", "tp")),
        P(("grp", "tp")),
        P("grp", "tp"),
        P("tp", None),
        P(("grp", "tp"), None),
        P(None, "tp"),
        P(None, "tp"),
        P("tp"),
        P("grp", "tp"),
    )
    out_specs = (
        P("grp", "tp"),
        P("grp", "tp"),
        P("tp", None),
        P(("grp", "tp"), None),
        P(None, "tp"),
        P(None, "tp"),
        P("tp"),
    )
    return jax.shard_map(local, mesh=mesh, in_specs=in_specs, out_specs=out_specs, check_vma=False)
```

time: 2030 us -> 364 us (0.18)
  waiting for transfers between devices: 1150 us -> 0 us
  blocking collectives: 781 us -> 5.77 us
  Pallas kernels: 0 us -> 281 us
    psum x6 -> x1, blocking collectives: 776 us -> 5.77 us  [local(): grad_llm_gain = lax.psum(gain_part, 'grp')]
    psum x4 -> x0, waiting for transfers between devices: 735 us -> none  [the longest x1 410 us: local(): square_total, proj_query = lax.psum((square_part, product_part), 'tp')]
    pallas_call x0 -> x5, Pallas kernels: none -> 281 us  [the longest x1 98.1 us: local(): call(start_kernel, [((4, 4, 4, 2, 16, 1024), BF16), ((2, 256, 2048), BF16...]
    reduce_scatter x1 -> x0, waiting for transfers between devices: 281 us -> none  [local(): lax.psum_scatter(col_dot(grad_hidden, project_weight), 'tp', scatter_dime...]
    all_gather x4 -> x0, waiting for transfers between devices: 134 us -> none  [the longest x1 102 us: local(): latents_full = lax.all_gather(latents_out, 'tp', axis=1, tiled=True)]
  transfers between devices with their start and end apart: 9 -> 0, of which waited for: 8 -> 0; matrix products, arithmetic and copies ran while one was open for 1% -> 0% of each run, Pallas kernels for 0% -> 0%
where the time goes in v1:
time: 364 us
  Pallas kernels  281 us (77%)
  matrix products  48.5 us (13%)
  local copies, waits for them, and re-layouts  20.9 us (6%)
  blocking collectives  5.77 us (2%)
  other arithmetic  5.13 us (1%)
    pallas_call x1, Pallas kernels, local(): call(start_kernel, [((4, 4, 4, 2, 16, 1024), BF16), ((2, 256, 2048), BF16...  98.1 us
    pallas_call x1, Pallas kernels, local(): call(grad_kernel, [((2, 512, 384), BF16), ((2, 64, 256), BF16), ((2, 256,...  67 us
    pallas_call x1, Pallas kernels, local(): call(end_kernel, [((2, 2, 512, 384), BF16), ((2, 16, 1024), F32)], [0, 1,...  58.9 us
    pallas_call x1, Pallas kernels, local(): call(attend_kernel, [((2, 512, 512), BF16), ((4, 2, 4, 2, 2, 32, 1024), B...  40.1 us
    dot_general x16, matrix products, dot(): return jnp.dot(left, right, preferred_element_type=F32)  24.4 us
    pallas_call x1, Pallas kernels, local(): call(sums_kernel, [((8, 128), F32)], [0], [0], [pltpu.VMEM((64, 8, 128),...  17.2 us
    dot_general x13, matrix products, row_dot(): lax.dot_general(left, right, (((0,), (0,)), ((), ())), preferred_element_...  15.2 us
    dot_general x12, matrix products, col_dot(): lax.dot_general(left, right, (((1,), (1,)), ((), ())), preferred_element_...  8.87 us

profile of v1, /device:TPU:1, one launch (start us, length us, event | category | flops | bytes accessed | tf_op | source)
XLA Modules:
  0.0 363.8 jit_solution(11589502775966694559)
XLA Ops:
  0.7 5.8 %fusion.52.tokp = bf16[256,2048]{1,0:T(8,128)(2,1)S(1)} fusion(bf16[256,1664]{1,0:T(8,128)(2,1)} %param.10, s32[2048]{0:T(1024)S(1)} %get-tuple-element.65, s32[2048]{0:T(1024)S(1)} %get-tuple-element.66, s32[2048]{0:T(1024)S(1)} %get-tuple-element.64, s32[2048]{0:T(1024)S(1)} %get-tuple-element.67, pred[2048]{0:T(1024)(128)(4,1)S(1)} %get-tuple-element.68, ...), kind=kOutput, calls=%fused_computation.81 | convolution fusion | flops 2069102592 | bytes 1937408 | tf_op jit(solution)/shard_map/dot_general | solution.py:41
  7.1 1.0 copy.66
  8.2 1.1 pad_maximum_fusion.1.qpart
  10.2 98.1 %start.1 = (bf16[4,4,4,2,16,1024]{5,4,3,2,1,0:T(8,128)(2,1)S(1)}, bf16[2,256,2048]{2,1,0:T(8,128)(2,1)S(1)}, f32[2,8,256]{2,1,0:T(8,128)S(1)}, bf16[512,512]{1,0...) custom-call(bf16[2,16,1024]{2,1,0:T(8,128)(2,1)S(1)} %reshape.145.wp, ...), custom_call_target="tpu_custom_call" | custom-call | tf_op jit(solution)/shard_map/start/pallas_call | solution.py:566
  108.3 2.4 convolution_convert_fusion.2
  111.7 0.9 fusion.96
  116.2 40.1 %attend.1 = (bf16[2,512,512]{2,1,0:T(8,128)(2,1)S(1)}, bf16[4,2,4,2,2,32,1024]{6,5,4,3,2,1,0:T(8,128)(2,1)S(1)}, bf16[2,4,2,4,2,64,256]{6,5,4,3,2,1,0:T(8,128)(2...) custom-call(bf16[2,512,384]{2,1,0:T(8,128)(2,1)S(1)} %pad_maximum_fusion.2.npk, ...), custom_call_target="tpu_custom_call", output_to_operand_aliasing={{1}: (1, {}), {2}: (2, {})} | custom-call | tf_op jit(solution)/shard_map/attend/pallas_call | solution.py:605
  156.3 2.4 convolution_convert_fusion.6
  158.8 2.0 copy-done.2
  160.7 2.3 fusion.55
  163.8 17.2 %sums.1 = f32[8,128]{1,0:T(8,128)S(1)} custom-call(f32[8,128]{1,0:T(8,128)S(1)} %maximum_maximum_fusion.part), custom_call_target="tpu_custom_call" | custom-call | tf_op jit(solution)/shard_map/sums/pallas_call | solution.py:641
  181.8 2.0 fusion.47
  183.9 3.3 copy.74
  187.1 1.2 convolution_convert_fusion.3.gap
  188.4 67.0 %grad.1 = (bf16[2,512,384]{2,1,0:T(8,128)(2,1)S(1)}, bf16[2,64,256]{2,1,0:T(8,128)(2,1)S(1)}, bf16[2,256,128]{2,1,0:T(8,128)(2,1)S(1)}) custom-call(bf16[256,1024]{1,0:T(8,128)(2,1)S(1)} %convolution_convert_fusion.3.gap, bf16[64,64,256]{2,1,0:T(8,128)(2,1)S(1)} %bitcast.139, bf16[256,128]{1,0:T(8,128)(2,1)S(1)} %get-tuple-element.60.gh, ...), custom_call_target="tpu_custom_call" | custom-call | tf_op jit(solution)/shard_map/grad/pallas_call | solution.py:661
  255.4 4.4 %fusion.193 = (bf16[1,4,2,4,2,64,256]{6,5,4,3,2,1,0:T(8,128)(2,1)}, bf16[1,4,2,4,2,64,256]{6,5,4,3,2,1,0:T(8,128)(2,1)S(1)}) fusion(bf16[2,4,2,4,2,64,256]{6,5,4,3,2,1,0:T(8,128)(2,1)} %copy-done.1), kind=kLoop, calls=%fused_computation.283 | loop fusion | bytes 8388608 | tf_op jit(solution)/shard_map/slice | solution.py:715
  261.0 1.1 slice_bitcast_fusion.2
  262.1 8.0 %fusion.89 = f32[4096,128]{1,0:T(8,128)} fusion(bf16[4096,1024]{1,0:T(8,128)(2,1)} %bitcast.138, bf16[512,128]{1,0:T(8,128)(2,1)S(1)} %bitcast.141, bf16[512,512]{1,0:T(8,128)(2,1)} %get-tuple-element.56, bf16[512,512]{1,0:T(8,128)(2,1)} %get-tuple-element.55), kind=kOutput, calls=%fused_computation.149 | convolution fusion | flops 1210187776 | bytes 11665408 | tf_op jit(solution)/shard_map/dot_general | solution.py:41
  270.1 4.4 %fusion.48 = f32[4096,128]{1,0:T(8,128)} fusion(f32[4096,128]{1,0:T(8,128)} %fusion.89, f32[4096,128]{1,0:T(8,128)S(1)} %fusion.150, bf16[4096,256]{1,0:T(8,128)(2,1)} %bitcast.150, bf16[2,256,128]{2,1,0:T(8,128)(2,1)S(1)} %get-tuple-element.42), kind=kOutput, calls=%fused_computation.77 | convolution fusion | flops 269484032 | bytes 8454144 | tf_op jit(solution)/shard_map/dot_general | solution.py:33
  274.6 1.0 fusion.98
  280.9 2.4 convolution_convert_fusion.1
  285.0 58.9 %end.1 = (bf16[2,2,512,384]{3,2,1,0:T(8,128)(2,1)S(1)}, f32[2,16,1024]{2,1,0:T(8,128)S(1)}) custom-call(bf16[512,512]{1,0:T(8,128)(2,1)S(1)} %pad_maximum_fusion.6.gqp, bf16[4,4,4,32,1024]{4,3,2,1,0:T(8,128)(2,1)S(1)} %bitcast.140, f32[16,256]{1,0:T(8,128)S(1)} %get-tuple-element.38.proj, f32[16,128]{1,0:T(8,128)S(1)} %get-tuple-element.39.rinv), custom_call_target="tpu_custom_call" | custom-call | tf_op jit(solution)/shard_map/end/pallas_call | solution.py:693
  344.0 1.0 copy-done.19
  345.0 1.1 fusion.194
  346.1 1.3 copy.84
  347.4 1.7 fusion.154
  349.1 1.2 copy.85
  350.4 2.0 convolution_add_fusion.1
  352.5 2.2 multiply_reduce_fusion
  354.8 1.5 copy.83
  356.3 0.9 fusion.88
  358.0 5.8 %psum.7 = f32[128]{0:T(128)} all-reduce(f32[128]{0:T(128)S(1)} %get-tuple-element.59), channel_id=1, replica_groups=mesh['grp'=2,'tp'=64] {'grp'}, use_global_device_ids=true, to_apply=%region_10.11 | all-reduce | flops 128 | bytes 1024 | tf_op jit(solution)/shard_map/psum | solution.py:717
  (132 shorter events, 16.0 us)
Async XLA Ops:
  0.6 155.7 %copy-start = (bf16[4096,128]{1,0:T(8,128)(2,1)S(1)}, bf16[4096,128]{1,0:T(8,128)(2,1)}, u32[]{:S(2)}) copy-start(bf16[4096,128]{1,0:T(8,128)(2,1)} %param.17) | copy-start | bytes 3145732
  0.7 5.8 %copy-start.9 = (bf16[256,64]{0,1:T(8,128)(2,1)S(1)}, bf16[256,64]{0,1:T(8,128)(2,1)}, u32[]{:S(2)}) copy-start(bf16[256,64]{0,1:T(8,128)(2,1)} %param.13) | copy-start | bytes 98308
  0.7 5.8 %copy-start.27 = (bf16[64,1024]{1,0:T(8,128)(2,1)S(1)}, bf16[64,1024]{1,0:T(8,128)(2,1)}, u32[]{:S(2)}) copy-start(bf16[64,1024]{1,0:T(8,128)(2,1)} %param.14) | copy-start | bytes 393220
  6.5 2.8 copy-start.30
  6.5 3.6 %copy-start.31 = (s32[256]{0:T(256)S(1)}, s32[256]{0:T(256)}, u32[]{:S(2)}) copy-start(s32[256]{0:T(256)} %param.11) | copy-start | bytes 3076
  6.5 3.7 %copy-start.10 = (bf16[1024,64]{0,1:T(8,128)(2,1)S(1)}, bf16[1024,64]{0,1:T(8,128)(2,1)}, u32[]{:S(2)}) copy-start(bf16[1024,64]{0,1:T(8,128)(2,1)} %param.16) | copy-start | bytes 393220
  108.3 2.4 copy-start.11
  108.3 3.4 copy-start.5
  110.7 4.2 %copy-start.24 = (bf16[512,1024]{1,0:T(8,128)(2,1)}, bf16[512,1024]{1,0:T(8,128)(2,1)S(1)}, u32[]{:S(2)}) copy-start(bf16[512,1024]{1,0:T(8,128)(2,1)S(1)} %convolution_convert_fusion.2) | copy-start | bytes 3145732
  111.0 2.4 copy-start.17
  111.3 3.0 copy-start.15
  111.3 4.3 %slice-start = ((s8[8388608]{0:T(1024)(128)(4,1)}), s8[4194304]{0:T(1024)(128)(4,1)S(1)}, s32[]{:S(2)}) async-start(s8[8388608]{0:T(1024)(128)(4,1)} %bitcast.135), calls=%async_computation | async-start | bytes 8388608
  111.6 3.3 copy-start.13
  112.6 3.0 copy-start.20
  113.3 2.9 slice-start.1
  156.3 2.5 copy-start.1
  156.3 4.5 %copy-start.2 = (bf16[4,2,4,2,2,32,1024]{6,5,4,3,2,1,0:T(8,128)(2,1)}, bf16[4,2,4,2,2,32,1024]{6,5,4,3,2,1,0:T(8,128)(2,1)S(1)}, u32[]{:S(2)}) copy-start(bf16[4,2,4,2,2,32,1024]{6,5,4,3,2,1,0:T(8,128)(2,1)S(1)} %get-tuple-element.33) | copy-start | bytes 25165828
  156.3 7.0 %copy-start.3 = (bf16[2,512,512]{2,1,0:T(8,128)(2,1)}, bf16[2,512,512]{2,1,0:T(8,128)(2,1)S(1)}, u32[]{:S(2)}) copy-start(bf16[2,512,512]{2,1,0:T(8,128)(2,1)S(1)} %get-tuple-element.32) | copy-start | bytes 3145732
  156.3 7.0 %copy-start.32 = (bf16[128]{0:T(256)(128)(2,1)S(1)}, bf16[128]{0:T(256)(128)(2,1)}, u32[]{:S(2)}) copy-start(bf16[128]{0:T(256)(128)(2,1)} %param.18) | copy-start | bytes 772
  156.3 7.0 %copy-start.29 = (bf16[256,128]{1,0:T(8,128)(2,1)S(1)}, bf16[256,128]{1,0:T(8,128)(2,1)}, u32[]{:S(2)}) copy-start(bf16[256,128]{1,0:T(8,128)(2,1)} %param.19) | copy-start | bytes 196612
  158.8 23.1 %copy-start.26 = (bf16[1024,128]{1,0:T(8,128)(2,1)}, bf16[1024,128]{1,0:T(8,128)(2,1)S(1)}, u32[]{:S(2)}) copy-start(bf16[1024,128]{1,0:T(8,128)(2,1)S(1)} %convolution_convert_fusion.6) | copy-start | bytes 786436
  255.4 4.4 %copy-start.7 = (bf16[2,512,384]{2,1,0:T(8,128)(2,1)}, bf16[2,512,384]{2,1,0:T(8,128)(2,1)S(1)}, u32[]{:S(2)}) copy-start(bf16[2,512,384]{2,1,0:T(8,128)(2,1)S(1)} %get-tuple-element.37) | copy-start | bytes 2359300
  270.1 4.4 %copy-start.22 = (bf16[512,512]{1,0:T(8,128)(2,1)S(1)}, bf16[512,512]{1,0:T(8,128)(2,1)}, u32[]{:S(2)}) copy-start(bf16[512,512]{1,0:T(8,128)(2,1)} %get-tuple-element.55) | copy-start | bytes 1572868
  270.1 4.4 %copy-start.23 = (bf16[512,512]{1,0:T(8,128)(2,1)S(1)}, bf16[512,512]{1,0:T(8,128)(2,1)}, u32[]{:S(2)}) copy-start(bf16[512,512]{1,0:T(8,128)(2,1)} %get-tuple-element.56) | copy-start | bytes 1572868
  270.1 5.5 %copy-start.8 = (bf16[2,512,384]{2,1,0:T(8,128)(2,1)S(1)}, bf16[2,512,384]{2,1,0:T(8,128)(2,1)}, u32[]{:S(2)}) copy-start(bf16[2,512,384]{2,1,0:T(8,128)(2,1)} %copy-done.7) | copy-start | bytes 2359300
  270.1 5.8 %copy-start.21 = (f32[512,512]{0,1:T(8,128)S(1)}, f32[512,512]{0,1:T(8,128)}, u32[]{:S(2)}) copy-start(f32[512,512]{0,1:T(8,128)} %copy-done.20) | copy-start | bytes 3145732
  270.1 5.8 %copy-start.25 = (bf16[512,1024]{1,0:T(8,128)(2,1)S(1)}, bf16[512,1024]{1,0:T(8,128)(2,1)}, u32[]{:S(2)}) copy-start(bf16[512,1024]{1,0:T(8,128)(2,1)} %copy-done.24) | copy-start | bytes 3145732
  274.5 2.2 copy-start.18
  275.6 2.0 copy-start.16
  276.4 1.9 copy-start.14
  278.3 2.5 copy-start.12
  346.1 10.2 %copy-start.28 = (bf16[64,1024]{1,0:T(8,128)(2,1)S(1)}, bf16[64,1024]{1,0:T(8,128)(2,1)}, u32[]{:S(2)}) copy-start(bf16[64,1024]{1,0:T(8,128)(2,1)} %param.14) | copy-start | bytes 393220
  (3 other events, 4.0 us)

commit v2 on v0

v2 whole, which is shorter than its diff:
```python
import functools
import math

import jax
import jax.numpy as jnp
import numpy as np
from jax import lax
from jax.experimental import pallas as pl
from jax.experimental.pallas import tpu as pltpu
from jax.sharding import PartitionSpec as P

D_LAT = 4096
HEAD_DIM = 128
D_LLM = 8192
SCORE_CAP = 5.0
SCALE = 1.0 / math.sqrt(HEAD_DIM)
CHIPS = 64
GROUP = 32

F32 = jnp.float32
BF16 = jnp.bfloat16
MESH = pl.DeviceIdType.MESH
ANY = pl.BlockSpec(memory_space=pl.ANY)
VMEM = pl.BlockSpec(memory_space=pltpu.VMEM)

ORDERS = ((2, 1, 0), (1, 0, 2), (0, 2, 1))
WIDE = ((0, 384), (384, 384), (768, 256))
WIDE_TURNED = ((0, 256), (256, 384), (640, 384))
ROWS_64 = ((0, 16), (16, 32), (48, 16))


def row_dot(left, right):
    return lax.dot_general(left, right, (((0,), (0,)), ((), ())), preferred_element_type=F32)


def col_dot(left, right):
    return lax.dot_general(left, right, (((1,), (1,)), ((), ())), preferred_element_type=F32)


def dot(left, right):
    return jnp.dot(left, right, preferred_element_type=F32)


class Place:
    def __init__(self):
        self.g = lax.axis_index("grp")
        self.t = lax.axis_index("tp")
        self.core = self.t % 2
        self.j = self.t // 2
        self.z = self.j % 4
        self.xl = (self.j // 4) % 2
        self.y = self.j // 8
        self.x = self.g * 2 + self.xl

    def chip(self, x, y, z):
        return x // 2, (y * 2 + x % 2) * 4 + z

    def plane_peer(self, k):
        return self.chip((self.x + k // 16) % 4, (self.y + (k // 4) % 4) % 4, (self.z + k % 4) % 4)

    def group_peer(self, k):
        y = (self.y + k // 8) % 4
        xl = (self.xl + (k // 4) % 2) % 2
        z = (self.z + k % 4) % 4
        return (y * 2 + xl) * 4 + z

    def sibling(self):
        return self.g, self.j * 2 + 1 - self.core


def remote(src, dst, sends, recvs, device):
    return pltpu.make_async_remote_copy(
        src_ref=src, dst_ref=dst, send_sem=sends, recv_sem=recvs, device_id=device, device_id_type=MESH
    )


def each_peer(n, do):
    def body(k, carry):
        do(k)
        return carry

    lax.fori_loop(1, n, body, 0)


class Gather:
    def __init__(self, place, ref, view, sends, recvs):
        self.place, self.ref, self.view, self.sends, self.recvs = place, ref, view, sends, recvs

    def copies(self, phase):
        pc = self.place
        mine = [pc.x, pc.y, pc.z]
        for part, order in enumerate(ORDERS):
            held = list(mine)
            for axis in order[:phase]:
                held[axis] = None
            block = self.view(self.ref, *held, part)
            for step in (1, 3, 2):
                peer = list(mine)
                peer[order[phase]] = (peer[order[phase]] + step) % 4
                g, j = pc.chip(*peer)
                spot = (part * 3 + phase) * 3 + step - 1
                yield remote(
                    block, block, self.sends.at[spot], self.recvs.at[spot], (g, j * 2 + pc.core)
                )

    def start(self, phase):
        for copy in self.copies(phase):
            copy.start()

    def wait(self, phase):
        for copy in self.copies(phase):
            copy.wait_recv()

    def drain(self):
        for phase in range(3):
            for copy in self.copies(phase):
                copy.wait_send()


def pick(value):
    return slice(None) if value is None else value


def halves(x):
    return (slice(None), slice(None)) if x is None else (x // 2, x % 2)


def view_weight(ref, x, y, z, part):
    return ref.at[pick(x), pick(y), pick(z), :, pl.ds(*WIDE[part])]


def view_output(core, ref, x, y, z, part):
    hi, lo = halves(x)
    return ref.at[pick(y), lo, pick(z), core, hi, :, pl.ds(*WIDE_TURNED[part])]


def view_latents(core, ref, x, y, z, part):
    hi, lo = halves(x)
    return ref.at[hi, pick(y), lo, pick(z), core, pl.ds(*ROWS_64[part]), :]


def total_slots(own, slots, n):
    def body(k, total):
        return total + slots[k].astype(F32)

    return lax.fori_loop(1, n, body, own.astype(F32))


class Pushes:
    def __init__(self, n, make):
        self.n, self.make = n, make

    def start(self):
        each_peer(self.n, lambda k: self.make(k).start())

    def landed(self):
        each_peer(self.n, lambda k: self.make(k).wait_recv())

    def drain(self):
        each_peer(self.n, lambda k: self.make(k).wait_send())


def at16(n):
    return pl.ds(pl.multiple_of(n * 16, 16), 16)


def at256(n):
    return pl.ds(pl.multiple_of(n * 256, 256), 256)


def turned(value, dtype=BF16):
    return value.astype(F32).T.astype(dtype)


def whole_kernel(
    tokens, val, qpart, wpl, owt, lt, pw, igrad, gain, qw,
    llm_t, gain_out, gpw, gow_t, gqw, gl_out, gw,
    wg, tokb, tok_t, valb, qx, qsum, recvq, qblk, qg, ow, la, kv, kv_t, fac, half, npk, recvn,
    ablk, attf, pw_t, pwx, fold, foldx, sumx, sumo, sumr, gh_t, ghx, ghp, gap, recvg, glp, recvl,
    lblk, glf, gblk, gg, ds, gqp, recvgq, gkv, sblk, sq, r1a, r1b, r1c, s1a, s1b, s1c,
    r2a, r2b, r2c, s2a, s2b, s2c, r3a, r3b, r3c, fin, oth,
    w_s, w_r, ow_s, ow_r, l_s, l_r, q_s, q_r, qa_s, qa_r, n_s, n_r, a_s, a_r, t_s, t_r,
    g_s, g_r, gl_s, gl_r, gga_s, gga_r, gq_s, gq_r, sqa_s, sqa_r, p_s, p_r, x_s, x_r, loc,
):
    pc = Place()
    core = pc.core
    sib = pc.sibling()
    partner = (1 - pc.g, pc.t)
    mine = [pc.x, pc.y, pc.z]
    pair = pc.j % 2
    own_rows = at16(pc.j // 2)
    all_rows = at16(pc.g * 16 + pc.j // 2)

    def chip_device(g, j):
        return (g, j * 2 + core)

    def over(index, src, dst, device):
        return remote(src, dst, x_s.at[index], x_r.at[index], device)

    barrier = pltpu.get_barrier_semaphore()

    def greet(k):
        pl.semaphore_signal(barrier, inc=1, device_id=chip_device(*pc.plane_peer(k)), device_id_type=MESH)

    pl.semaphore_signal(barrier, inc=1, device_id=sib, device_id_type=MESH)
    each_peer(CHIPS, greet)

    local_copies = [
        pltpu.make_async_copy(
            owt.at[pl.ds(pl.multiple_of(pc.g * 32, 32), 32), :],
            ow.at[pc.y, pc.xl, pc.z, core, pc.g],
            loc.at[0],
        ),
        pltpu.make_async_copy(lt, la.at[pc.g, pc.y, pc.xl, pc.z, core], loc.at[1]),
        pltpu.make_async_copy(val, valb.at[core], loc.at[2]),
        pltpu.make_async_copy(wpl.at[core], wg.at[pc.x, pc.y, pc.z, at16(core)], loc.at[3]),
    ]
    for copy in local_copies:
        copy.start()
    pl.semaphore_wait(barrier, CHIPS)

    w_sib = over(0, wpl.at[1 - core], wg.at[pc.x, pc.y, pc.z, at16(core)], sib)
    w_sib.start()
    q_sib = over(1, qpart.at[1 - core], qx, sib)
    q_sib.start()

    for block in range(16):
        x, y = block // 4, block % 4
        begin = (((x // 2) * 4 + y) * 2 + x % 2) * 104
        base = begin // 128 * 128
        width = min(256, 1664 - base)
        row = lax.broadcasted_iota(jnp.int32, (width, 128), 0)
        col = lax.broadcasted_iota(jnp.int32, (width, 128), 1)
        rest = col & 15
        hit = (row == (begin - base) + (col >> 4) * 13 + rest) & (rest < 13)
        place = jnp.where(hit, 1.0, 0.0).astype(BF16)
        tokb[core, :, pl.ds(block * 128, 128)] = dot(tokens[:, pl.ds(base, width)], place).astype(BF16)

    weight = Gather(pc, wg, view_weight, w_s, w_r)
    output = Gather(pc, ow, functools.partial(view_output, core), ow_s, ow_r)
    latents = Gather(pc, la, functools.partial(view_latents, core), l_s, l_r)
    for copy in local_copies:
        copy.wait()
    w_sib.wait_recv()
    weight.start(0)

    q_sib.wait_recv()
    for p in range(2):
        qsum[p] = (qpart[core, p].astype(F32) + qx[p].astype(F32)).astype(BF16)

    def q_copy(k):
        j = pc.group_peer(k)
        return remote(
            qsum.at[j % 2, at16(j // 2), :], recvq.at[k], q_s.at[k], q_r.at[k], chip_device(pc.g, j)
        )

    q_push = Pushes(GROUP, q_copy)
    q_push.start()
    t_sib = over(2, tokb.at[core], tokb.at[core], sib)
    t_sib.start()
    v_sib = over(3, val, valb.at[core], sib)
    v_sib.start()
    pw_sib = over(4, pw.at[:, 1 - core], pwx, sib)
    pw_sib.start()
    weight.wait(0)
    weight.start(1)
    q_push.landed()
    total = total_slots(qsum[pair, own_rows, :], recvq, GROUP)
    rinv = lax.rsqrt(total[:, 256:] / D_LAT + 1e-06)
    proj = total[:, :256]
    qblk[...] = (proj * rinv[:, :1]).astype(BF16)
    q_spot = qg.at[all_rows, at256(pair)]
    qa_push = Pushes(
        CHIPS,
        lambda k: remote(qblk, q_spot, qa_s.at[k], qa_r.at[k], chip_device(*pc.plane_peer(k))),
    )
    qa_push.start()
    q_own = pltpu.make_async_copy(qblk, q_spot, loc.at[4])
    q_own.start()
    latents.start(0)
    t_sib.wait()
    v_sib.wait()
    weight.wait(1)
    weight.start(2)
    output.start(0)

    for y in range(4):
        pw_t[:, pl.ds(y * 1024, 1024)] = turned(pw[pl.ds(y * 8, 8)].reshape(1024, 128))
    for block in range(4):
        tok_t[pl.ds(block * 512, 512), :] = turned(
            tokb[:, :, pl.ds(block * 512, 512)].reshape(512, 512)
        )
    latents.wait(0)
    weight.wait(2)
    latents.start(1)
    output.wait(0)
    output.start(1)

    tok = tokb[...].reshape(512, 2048)

    def project(n, carry):
        columns = at256(n)
        kv[:, columns] = dot(tok, wg[:, :, :, :, columns].reshape(2048, 256)).astype(BF16)
        return carry

    lax.fori_loop(0, 4, project, 0)
    for n in range(4):
        kv_t[pl.ds(n * 256, 256), :] = turned(kv[:, n * 256 : n * 256 + 256])
    q_own.wait()
    qa_push.landed()

    def n_copy(p, k):
        g, j = pc.plane_peer(k)
        return remote(
            npk.at[j % 2, at16(g * 16 + j // 2), :], recvn.at[k], n_s.at[k], n_r.at[k], chip_device(g, j)
        )

    for p in range(2):
        packed = []
        sums = []
        for side in range(2):
            head = p * 2 + side
            columns = pl.ds(head * 128, 128)
            query = qg[:, columns]
            total = jnp.zeros((1, 512), F32)
            for chunk in range(4):
                slots = pl.ds(chunk * 128, 128)
                raw = col_dot(kv[slots, columns], query)
                squash = jnp.tanh(raw * (SCALE / SCORE_CAP))
                keep = valb[chunk // 2, pl.ds(chunk % 2 * 128, 128), :][:, :1]
                weights = jnp.exp(SCORE_CAP * squash) * keep
                half[head, slots, :] = weights.astype(BF16)
                fac[head, slots, :] = weights * (1.0 - squash * squash) * SCALE
                total = total + jnp.sum(weights, axis=0, keepdims=True)
            packed.append(dot(kv_t[pl.ds(512 + head * 128, 128), :], half[head]))
            sums.append(jnp.broadcast_to(total, (64, 512)))
        npk[p] = jnp.concatenate(packed + sums, axis=0).T.astype(BF16)
    n_push = Pushes(CHIPS, lambda k: n_copy(0, k))
    n_push.start()

    latents.wait(1)
    latents.start(2)
    output.wait(1)
    output.start(2)
    weight.drain()
    n_push.landed()
    total = total_slots(npk[pair, all_rows, :], recvn, CHIPS)
    whole = jnp.concatenate(
        [jnp.broadcast_to(total[:, 256:257], (16, 128)), jnp.broadcast_to(total[:, 320:321], (16, 128))],
        axis=1,
    )
    ablk[...] = (total[:, :256] / whole).astype(BF16)
    a_spot = attf.at[core, all_rows, at256(pair)]
    a_push = Pushes(
        CHIPS,
        lambda k: remote(ablk, a_spot, a_s.at[k], a_r.at[k], chip_device(*pc.plane_peer(k))),
    )
    a_push.start()
    a_own = pltpu.make_async_copy(ablk, a_spot, loc.at[5])
    a_own.start()

    latents.wait(2)
    la_sib = over(5, la.at[:, :, :, :, core], la.at[:, :, :, :, core], sib)
    la_sib.start()
    output.wait(2)
    ow_sib = over(6, ow.at[:, :, :, core], ow.at[:, :, :, core], sib)
    ow_sib.start()
    a_own.wait()
    a_push.landed()
    a_sib = over(7, attf.at[core], attf.at[core], sib)
    a_sib.start()

    la_sib.wait()
    ow_sib.wait()

    def fold_in(n, carry):
        columns = at256(n)
        fold[:, columns] = dot(pw_t[...], ow[:, :, :, :, :, :, columns].reshape(4096, 256)).astype(BF16)
        return carry

    lax.fori_loop(0, 4, fold_in, 0)
    f_sib = over(8, fold.at[:, pl.ds(pl.multiple_of((1 - core) * 512, 512), 512)], foldx, sib)
    f_sib.start()
    hidden = dot(pw_t[...], la[pc.g].reshape(4096, 256))
    a_sib.wait()
    group_rows = at256(pc.g)
    hidden = hidden + col_dot(fold[:, :512], attf[0, group_rows, :])
    hidden = (hidden + col_dot(fold[:, 512:], attf[1, group_rows, :])).astype(BF16).astype(F32)
    grad_y = igrad[...].astype(F32).T
    scaled_dy = grad_y * gain[...]
    sumo[...] = jnp.concatenate(
        [
            jnp.sum(hidden * hidden, axis=0, keepdims=True),
            jnp.sum(hidden * scaled_dy, axis=0, keepdims=True),
            jnp.zeros((6, 256), F32),
        ],
        axis=0,
    )
    s_sib = over(9, sumo, sumx.at[0], sib)
    s_sib.start()
    s_sib.wait()
    sumx[1] = sumx[0] + sumo[...]
    t_push = Pushes(
        GROUP,
        lambda k: remote(sumx.at[1], sumr.at[k], t_s.at[k], t_r.at[k], chip_device(pc.g, pc.group_peer(k))),
    )
    t_push.start()
    t_push.landed()
    total = total_slots(sumx[1], sumr, GROUP)
    hrinv = lax.rsqrt(total[0:1, :] / D_LLM + 1e-05)
    normed = hidden * hrinv
    llm_t[...] = (normed * gain[...]).astype(BF16)
    gain_own = jnp.broadcast_to(jnp.sum(grad_y * normed, axis=1, keepdims=True), (128, 128))
    grad_h = hrinv * scaled_dy - (hrinv * hrinv * hrinv / D_LLM * total[1:2, :]) * hidden
    gh_t[...] = grad_h.astype(BF16)
    h_sib = over(10, gh_t, ghx, sib)
    h_sib.start()
    ghp[pc.g] = gh_t[...]
    h_part = over(11, gh_t, ghp.at[pc.g], partner)
    h_part.start()
    gain_out[pc.g] = gain_own
    gain_part = over(12, gain_out.at[pc.g], gain_out.at[pc.g], partner)
    gain_part.start()

    f_sib.wait()
    own_half = fold[:, pl.ds(pl.multiple_of(core * 512, 512), 512)]
    partial = dot(turned(gh_t[...]), own_half)
    h_sib.wait()
    gap[...] = (partial + dot(turned(ghx[...]), foldx[...])).astype(BF16)

    def g_copy(k):
        j = pc.group_peer(k)
        return remote(
            gap.at[at16(j // 2), at256(j % 2)], recvg.at[k], g_s.at[k], g_r.at[k], chip_device(pc.g, j)
        )

    g_push = Pushes(GROUP, g_copy)
    g_push.start()

    pw_sib.wait()
    for n in range(4):
        part = dot(pw[pl.ds(n * 8, 8), core].reshape(512, 128), gh_t[...])
        part = part + dot(pwx[pl.ds(n * 8, 8)].reshape(512, 128), ghx[...])
        glp[pl.ds(n * 8, 8)] = part.astype(BF16).reshape(8, 64, 256)

    def l_copy(k):
        j = pc.group_peer(k)
        return remote(glp.at[j], recvl.at[k], gl_s.at[k], gl_r.at[k], chip_device(pc.g, j))

    l_push = Pushes(GROUP, l_copy)
    l_push.start()
    g_push.landed()
    grad = total_slots(gap[own_rows, at256(pair)], recvg, GROUP).astype(BF16).astype(F32)
    prod = grad * ablk[...].astype(F32)
    first = jnp.sum(prod[:, :128], axis=1, keepdims=True) / whole[:, :1]
    second = jnp.sum(prod[:, 128:], axis=1, keepdims=True) / whole[:, 128:129]
    lane = lax.broadcasted_iota(jnp.int32, (16, 128), 1)
    gblk[:, :256] = (grad / whole).astype(BF16)
    gblk[:, 256:] = jnp.where(lane < 64, first, second).astype(BF16)
    g_spot = gg.at[pair, all_rows, :]
    gga_push = Pushes(
        CHIPS,
        lambda k: remote(gblk, g_spot, gga_s.at[k], gga_r.at[k], chip_device(*pc.plane_peer(k))),
    )
    gga_push.start()
    g_own = pltpu.make_async_copy(gblk, g_spot, loc.at[6])
    g_own.start()
    l_push.landed()
    lblk[...] = total_slots(glp[pc.j], recvl, GROUP).astype(BF16)
    glf[pc.g] = lblk[...]
    l_part = over(13, lblk, glf.at[pc.g], partner)
    l_part.start()
    g_own.wait()
    gga_push.landed()

    for p in range(2):
        deltas = gg[p, :, 256:].astype(F32).T
        for side in range(2):
            head = p * 2 + side
            columns = pl.ds(head * 128, 128)
            grads = gg[p, :, side * 128 : side * 128 + 128]
            query = qg[:, columns]
            delta = deltas[side * 64 : side * 64 + 1, :]
            for chunk in range(4):
                slots = pl.ds(chunk * 128, 128)
                prob = col_dot(kv[slots, 512 + head * 128 : 640 + head * 128], grads)
                score = (fac[head, slots, :] * (prob - delta)).astype(BF16)
                ds[head, slots, :] = score
                gkv[slots, columns] = dot(score, query).astype(BF16)
                gkv[slots, 512 + head * 128 : 640 + head * 128] = dot(half[head, slots, :], grads).astype(BF16)

    first, once = (r1a, r1b, r1c), (s1a, s1b, s1c)
    second, twice = (r2a, r2b, r2c), (s2a, s2b, s2c)
    third = (r3a, r3b, r3c)

    for x in range(4):
        for n in range(2):
            wg[x, :, :, :, n * 512 : n * 512 + 512] = (
                dot(tok_t[x * 512 : x * 512 + 512, :], gkv[:, n * 512 : n * 512 + 512])
                .astype(BF16)
                .reshape(4, 4, 32, 512)
            )

    def slab(part, phase, spot):
        order = ORDERS[part]
        index = [spot if axis == order[phase] else slice(None) for axis in range(3) if axis not in order[:phase]]
        if phase == 0:
            return wg.at[(*index, slice(None), pl.ds(*WIDE[part]))]
        return (once, twice)[phase - 1][part].at[tuple(index)]

    def copies(part, phase):
        axis = ORDERS[part][phase]
        for step in (1, 3, 2):
            peer = list(mine)
            peer[axis] = (peer[axis] + step) % 4
            spot = (part * 3 + phase) * 3 + step - 1
            yield remote(
                slab(part, phase, peer[axis]),
                (first, second, third)[phase][part].at[step],
                p_s.at[spot], p_r.at[spot], chip_device(*pc.chip(*peer)),
            )

    held_first = []
    for part in range(3):
        for copy in copies(part, 0):
            copy.start()
        copy = pltpu.make_async_copy(slab(part, 0, mine[ORDERS[part][0]]), first[part].at[0], loc.at[7 + part])
        copy.start()
        held_first.append(copy)

    for p in range(2):
        parts = [
            dot(kv_t[pl.ds(head * 128, 128), :], ds[head]) for head in (p * 2, p * 2 + 1)
        ]
        gqp[:, p * 256 : p * 256 + 256] = jnp.concatenate(parts, axis=0).T.astype(BF16)

    def gq_copy(k):
        g, j = pc.plane_peer(k)
        return remote(
            gqp.at[at16(g * 16 + j // 2), at256(j % 2)], recvgq.at[k], gq_s.at[k], gq_r.at[k], chip_device(g, j)
        )

    gq_push = Pushes(CHIPS, gq_copy)
    gq_push.start()

    h_part.wait()
    mixed = [
        (dot(ghp[0], attf[c, :256, :]) + dot(ghp[1], attf[c, 256:, :])).astype(BF16) for c in range(2)
    ]
    mixed_t = jnp.concatenate(mixed, axis=1)
    gh_both = [turned(ghp[n]) for n in range(2)]

    def project_grad(n, carry):
        y, xl = n // 2, n % 2
        gpw[y, xl] = (
            dot(la[0, y, xl].reshape(512, 256), gh_both[0])
            + dot(la[1, y, xl].reshape(512, 256), gh_both[1])
            + col_dot(ow[y, xl].reshape(512, 1024), mixed_t)
        )
        return carry

    lax.fori_loop(0, 8, project_grad, 0)

    gq_push.landed()
    grad = total_slots(gqp[all_rows, at256(pair)], recvgq, CHIPS)
    sblk[:, :256] = (grad * rinv[:, :1]).astype(BF16)
    ratio = jnp.sum(grad * proj, axis=1, keepdims=True) * (rinv * rinv * rinv / D_LAT)
    sblk[:, 256:] = ratio.astype(BF16)
    s_spot = sq.at[core, pair, all_rows, :]
    sqa_push = Pushes(
        CHIPS,
        lambda k: remote(sblk, s_spot, sqa_s.at[k], sqa_r.at[k], chip_device(*pc.plane_peer(k))),
    )
    sqa_push.start()
    s_own = pltpu.make_async_copy(sblk, s_spot, loc.at[10])
    s_own.start()

    for part in range(3):
        held_first[part].wait()
        for copy in copies(part, 0):
            copy.wait_recv()
        src, dst = first[part], once[part]

        def add_first(n, carry, src=src, dst=dst):
            a, b = n // 4, n % 4
            dst[a, b] = sum(src[s, a, b].astype(F32) for s in range(4)).astype(BF16)
            return carry

        lax.fori_loop(0, 16, add_first, 0)
        for copy in copies(part, 1):
            copy.start()

    l_part.wait()
    gow_t[...] = jnp.concatenate(
        [dot(glf[0], attf[c, :256, :]) + dot(glf[1], attf[c, 256:, :]) for c in range(2)], axis=1
    )
    s_own.wait()
    sqa_push.landed()
    s_sib2 = over(14, sq.at[core], sq.at[core], sib)
    s_sib2.start()

    for part in range(3):
        for copy in copies(part, 1):
            copy.wait_recv()
        src, dst, held = second[part], twice[part], once[part]
        left = [axis for axis in range(3) if axis != ORDERS[part][0]]
        leading = left[0] == ORDERS[part][1]
        here = mine[ORDERS[part][1]]

        def add_second(n, carry, src=src, dst=dst, held=held, leading=leading, here=here):
            base = held[here, n] if leading else held[n, here]
            dst[n] = (base.astype(F32) + sum(src[s, n].astype(F32) for s in range(1, 4))).astype(BF16)
            return carry

        lax.fori_loop(0, 4, add_second, 0)
        for copy in copies(part, 2):
            copy.start()

    s_sib2.wait()
    feats = [la[n, pc.y, pc.xl, pc.z, core] for n in range(2)]
    for c in range(2):
        for p in range(2):
            columns = pl.ds((c * 2 + p) * 256, 256)
            gqw[:, columns] = dot(feats[0], sq[c, p, :256, :256]) + dot(feats[1], sq[c, p, 256:, :256])
    mine_f = la[pc.g, pc.y, pc.xl, pc.z, core].astype(F32)
    back = glf[pc.g].astype(F32)
    coef = jnp.zeros((256, 128), F32)
    for c in range(2):
        for p in range(2):
            block = sq[c, p, group_rows, :]
            back = back + col_dot(qw[:, (c * 2 + p) * 256 : (c * 2 + p) * 256 + 256], block[:, :256])
            coef = coef + block[:, 256:].astype(F32)
    gl_out[...] = back - coef.T[:1, :] * mine_f

    for part in range(3):
        for copy in copies(part, 2):
            copy.wait_recv()
        here = mine[ORDERS[part][2]]
        fin[:, pl.ds(*WIDE[part])] = twice[part][here].astype(F32) + sum(
            third[part][s].astype(F32) for s in range(1, 4)
        )
    give = over(15, fin.at[at16(1 - core), :], oth, sib)
    give.start()
    gw[core] = fin[at16(core), :]
    give.wait()
    gw[1 - core] = oth[...]

    gain_part.wait()
    w_sib.wait_send()
    q_sib.wait_send()
    for gather in (latents, output):
        gather.drain()
    for push in (q_push, qa_push, n_push, a_push, t_push, g_push, l_push, gga_push, gq_push, sqa_push):
        push.drain()
    for part in range(3):
        for phase in range(3):
            for copy in copies(part, phase):
                copy.wait_send()


def sems(*counts):
    return [pltpu.SemaphoreType.DMA((n,)) for n in counts]


def local(
    tokens, keep_mask, shard_counts, latents, query_weight, keyval_weight, output_weight,
    project_weight, llm_gain, input_grad,
):
    latent_f32 = latents.astype(F32)
    squares = jnp.sum(latent_f32 * latent_f32, axis=1)
    product = dot(latents, query_weight)
    qpart = jnp.concatenate(
        [
            product.reshape(256, 4, 256).transpose(1, 0, 2),
            jnp.broadcast_to(squares[None, :, None], (4, 256, 128)),
        ],
        axis=2,
    ).astype(BF16)
    padded = jnp.pad(keyval_weight, ((0, 3), (0, 0)))
    wpl = padded.reshape(16, 2, 2, 512).transpose(2, 0, 1, 3).reshape(2, 16, 1024)
    positions = jnp.arange(256, dtype=jnp.int32)
    valid = (((keep_mask == 1) | (positions == 0)) & (positions < shard_counts[0])).astype(F32)
    val = jnp.broadcast_to(valid[:, None], (256, 128))
    gain = jnp.broadcast_to(llm_gain.astype(F32)[:, None], (128, 256))

    widths = [w for _, w in WIDE]
    scratch = [
        ((4, 4, 4, 32, 1024), BF16),
        ((2, 256, 2048), BF16),
        ((2048, 512), BF16),
        ((2, 256, 128), F32),
        ((2, 256, 384), BF16),
        ((2, 256, 384), BF16),
        ((32, 16, 384), BF16),
        ((16, 256), BF16),
        ((512, 512), BF16),
        ((4, 2, 4, 2, 2, 32, 1024), BF16),
        ((2, 4, 2, 4, 2, 64, 256), BF16),
        ((512, 1024), BF16),
        ((1024, 512), BF16),
        ((4, 512, 512), F32),
        ((4, 512, 512), BF16),
        ((2, 512, 384), BF16),
        ((64, 16, 384), BF16),
        ((16, 256), BF16),
        ((2, 512, 512), BF16),
        ((128, 4096), BF16),
        ((32, 64, 128), BF16),
        ((128, 1024), BF16),
        ((128, 512), BF16),
        ((2, 8, 256), F32),
        ((8, 256), F32),
        ((32, 8, 256), F32),
        ((128, 256), BF16),
        ((128, 256), BF16),
        ((2, 128, 256), BF16),
        ((256, 512), BF16),
        ((32, 16, 256), BF16),
        ((32, 64, 256), BF16),
        ((32, 64, 256), BF16),
        ((64, 256), BF16),
        ((2, 64, 256), BF16),
        ((16, 384), BF16),
        ((2, 512, 384), BF16),
        ((4, 512, 512), BF16),
        ((512, 512), BF16),
        ((64, 16, 256), BF16),
        ((512, 1024), BF16),
        ((16, 384), BF16),
        ((2, 2, 512, 384), BF16),
        *[((4, 4, 4, 32, w), BF16) for w in widths],
        *[((4, 4, 32, w), BF16) for w in widths],
        *[((4, 4, 32, w), BF16) for w in widths],
        *[((4, 32, w), BF16) for w in widths],
        *[((4, 32, w), BF16) for w in widths],
        ((32, 1024), F32),
        ((16, 1024), F32),
    ]
    llm_t, gain_out, gpw, gow_t, gqw, gl_out, gw = pl.pallas_call(
        whole_kernel,
        out_shape=[
            jax.ShapeDtypeStruct(s, d)
            for s, d in (
                ((128, 256), BF16),
                ((2, 128, 128), F32),
                ((4, 2, 512, 128), F32),
                ((64, 1024), F32),
                ((64, 1024), F32),
                ((64, 256), F32),
                ((2, 16, 1024), F32),
            )
        ],
        in_specs=[VMEM] * 10,
        out_specs=[VMEM] * 7,
        scratch_shapes=[pltpu.VMEM(s, d) for s, d in scratch]
        + sems(27, 27, 27, 27, 27, 27, 32, 32, 64, 64, 64, 64, 64, 64, 32, 32)
        + sems(32, 32, 32, 32, 64, 64, 64, 64, 64, 64, 27, 27, 16, 16, 11),
        compiler_params=pltpu.CompilerParams(
            has_side_effects=True, vmem_limit_bytes=62 << 20, collective_id=0
        ),
        name="whole",
    )(
        tokens, val, qpart.reshape(2, 2, 256, 384), wpl, output_weight.T, latents.T,
        project_weight.reshape(32, 2, 64, 128), input_grad, gain, query_weight,
    )

    return (
        llm_t.T,
        gl_out.T,
        gqw,
        gw[:, :13].reshape(2, 13, 2, 512).transpose(1, 2, 0, 3).reshape(13, 2048),
        gow_t.T,
        gpw.reshape(4096, 128),
        gain_out[0, :, 0] + gain_out[1, :, 0],
    )


def solution(mesh):
    in_specs = (
        P(("grp", "tp"), None),
        P(("grp", "tp")),
        P(("grp", "tp")),
        P("grp", "tp"),
        P("tp", None),
        P(("grp", "tp"), None),
        P(None, "tp"),
        P(None, "tp"),
        P("tp"),
        P("grp", "tp"),
    )
    out_specs = (
        P("grp", "tp"),
        P("grp", "tp"),
        P("tp", None),
        P(("grp", "tp"), None),
        P(None, "tp"),
        P(None, "tp"),
        P("tp"),
    )
    return jax.shard_map(local, mesh=mesh, in_specs=in_specs, out_specs=out_specs, check_vma=False)
```

time: 2030 us -> 244 us (0.12)
  waiting for transfers between devices: 1150 us -> 0 us
  blocking collectives: 781 us -> 0 us
  Pallas kernels: 0 us -> 223 us
  matrix products: 56.3 us -> 1.24 us
    psum x6 -> x0, blocking collectives: 776 us -> none  [the longest x1 284 us: local(): lax.psum(col_dot(grad_lat_out, output_weight), 'tp').astype(jnp.bfloat16)]
    psum x4 -> x0, waiting for transfers between devices: 735 us -> none  [the longest x1 410 us: local(): square_total, proj_query = lax.psum((square_part, product_part), 'tp')]
    reduce_scatter x1 -> x0, waiting for transfers between devices: 281 us -> none  [local(): lax.psum_scatter(col_dot(grad_hidden, project_weight), 'tp', scatter_dime...]
    pallas_call x0 -> x1, Pallas kernels: none -> 223 us  [local(): pl.pallas_call(whole_kernel, out_shape=[jax.ShapeDtypeStruct(s, d) for s,...]
    all_gather x4 -> x0, waiting for transfers between devices: 134 us -> none  [the longest x1 102 us: local(): latents_full = lax.all_gather(latents_out, 'tp', axis=1, tiled=True)]
    dot_general x59 -> x1, matrix products: 56.3 us -> 1.24 us  [dot(): return jnp.dot(left, right, preferred_element_type=F32)]
  transfers between devices with their start and end apart: 9 -> 0, of which waited for: 8 -> 0; matrix products, arithmetic and copies ran while one was open for 1% -> 0% of each run, Pallas kernels for 0% -> 0%
where the time goes in v2:
time: 244 us; the launch traced here: 243 us
  Pallas kernels  223 us (91%)
  local copies, waits for them, and re-layouts  13.5 us (6%)
  other arithmetic  3.92 us (2%)
    pallas_call x1, Pallas kernels, local(): pl.pallas_call(whole_kernel, out_shape=[jax.ShapeDtypeStruct(s, d) for s,...  223 us
    unnamed x7, local copies, waits for them, and re-layouts  7.86 us

profile of v2, /device:TPU:1, one launch (start us, length us, event | category | flops | bytes accessed | tf_op | source)
XLA Modules:
  0.0 243.0 jit_solution(17852305416106347662)
XLA Ops:
  1.3 0.7 and_convert_fusion
  2.0 0.8 multiply_reduce_fusion
  2.7 0.8 pad.4
  3.6 0.1 copy.36
  3.7 0.7 reshape.46.wpl
  4.4 0.8 broadcast_in_dim.6.val
  5.1 1.4 broadcast_in_dim.8.gain
  6.5 0.1 broadcast_in_dim.7
  6.6 1.2 convolution_convert_fusion
  7.9 1.0 pad_maximum_fusion.qpart
  8.9 223.0 %whole.1 = (bf16[128,256]{1,0:T(8,128)(2,1)}, f32[2,128,128]{2,1,0:T(8,128)}, f32[4,2,512,128]{3,2,1,0:T(8,128)}, f32[64,1024]{1,0:T(8,128)}, f32[64,1024]{1,0:T...) custom-call(bf16[256,1664]{1,0:T(8,128)(2,1)} %tokens.1, f32[256,128]{1,0:T(8,128)} %broadcast_in_dim.6.val, ...), custom_call_target="tpu_custom_call" | custom-call | tf_op jit(solution)/shard_map/whole/pallas_call | solution.py:739
  231.9 0.0 copy-start
  231.9 1.7 copy.29
  233.6 1.5 add_reduce_fusion
  235.1 1.0 reshape.51
  236.1 0.1 copy.28
  236.2 0.7 reshape.49
  236.9 1.5 copy.42
  238.4 1.7 copy.43
  240.0 1.7 copy.44
  241.7 0.0 copy-done
  241.7 1.3 copy.45
  (2 shorter events, 0.1 us)
Async XLA Ops:
  231.9 9.9 %copy-start = (f32[4,2,512,128]{3,2,1,0:T(8,128)S(1)}, f32[4,2,512,128]{3,2,1,0:T(8,128)}, u32[]{:S(2)}) copy-start(f32[4,2,512,128]{3,2,1,0:T(8,128)} %get-tuple-element.19) | copy-start | bytes 6291460

commit v3 on v2

--- a/solution.py
+++ b/solution.py
@@ -25,7 +25,7 @@
 
 ORDERS = ((2, 1, 0), (1, 0, 2), (0, 2, 1))
 WIDE = ((0, 384), (384, 384), (768, 256))
-WIDE_TURNED = ((0, 256), (256, 384), (640, 384))
+COLUMNS_512 = ((0, 256), (256, 128), (384, 128))
 ROWS_64 = ((0, 16), (16, 32), (48, 16))
 
 
@@ -83,8 +83,9 @@
 
 
 class Gather:
-    def __init__(self, place, ref, view, sends, recvs):
+    def __init__(self, place, ref, view, sends, recvs, whole=True):
         self.place, self.ref, self.view, self.sends, self.recvs = place, ref, view, sends, recvs
+        self.whole = whole
 
     def copies(self, phase):
         pc = self.place
@@ -94,9 +95,13 @@
             for axis in order[:phase]:
                 held[axis] = None
             block = self.view(self.ref, *held, part)
-            for step in (1, 3, 2):
+            near = order[phase] == 0 and not self.whole
+            for step in (1,) if near else (1, 3, 2):
                 peer = list(mine)
-                peer[order[phase]] = (peer[order[phase]] + step) % 4
+                if near:
+                    peer[0] = pc.g * 2 + 1 - pc.xl
+                else:
+                    peer[order[phase]] = (peer[order[phase]] + step) % 4
                 g, j = pc.chip(*peer)
                 spot = (part * 3 + phase) * 3 + step - 1
                 yield remote(
@@ -130,8 +135,11 @@
 
 
 def view_output(core, ref, x, y, z, part):
-    hi, lo = halves(x)
-    return ref.at[pick(y), lo, pick(z), core, hi, :, pl.ds(*WIDE_TURNED[part])]
+    return ref.at[pick(y), slice(None) if x is None else x % 2, pick(z), core, :, pl.ds(*COLUMNS_512[part])]
+
+
+def view_own(core, ref, x, y, z, part):
+    return ref.at[pick(y), slice(None) if x is None else x % 2, pick(z), core, pl.ds(*ROWS_64[part]), :]
 
 
 def view_latents(core, ref, x, y, z, part):
@@ -160,6 +168,24 @@
         each_peer(self.n, lambda k: self.make(k).wait_send())
 
 
+class PairPushes(Pushes):
+    def __init__(self, place, make):
+        super().__init__(CHIPS, make)
+        self.place = place
+
+    def start_pair(self, p):
+        def body(i, carry):
+            k = (i // 2) * 4 + (i % 2) * 2 + (self.place.z + p) % 2
+
+            @pl.when(k > 0)
+            def _():
+                self.make(k).start()
+
+            return carry
+
+        lax.fori_loop(0, 32, body, 0)
+
+
 def at16(n):
     return pl.ds(pl.multiple_of(n * 16, 16), 16)
 
@@ -173,13 +199,14 @@
 
 
 def whole_kernel(
-    tokens, val, qpart, wpl, owt, lt, pw, igrad, gain, qw,
+    tokens, keep, count, lat, qw, keyval_w, owt, lt, pw, igrad, gain_in,
     llm_t, gain_out, gpw, gow_t, gqw, gl_out, gw,
-    wg, tokb, tok_t, valb, qx, qsum, recvq, qblk, qg, ow, la, kv, kv_t, fac, half, npk, recvn,
+    val, qpart, wpl, gain,
+    wg, tokb, tok_t, valb, qx, qsum, recvq, qblk, qg, qo, owe, lown, ltp, la, kv, kv_t, fac, half, npk, recvn,
     ablk, attf, pw_t, pwx, fold, foldx, sumx, sumo, sumr, gh_t, ghx, ghp, gap, recvg, glp, recvl,
     lblk, glf, gblk, gg, ds, gqp, recvgq, gkv, sblk, sq, r1a, r1b, r1c, s1a, s1b, s1c,
     r2a, r2b, r2c, s2a, s2b, s2c, r3a, r3b, r3c, fin, oth,
-    w_s, w_r, ow_s, ow_r, l_s, l_r, q_s, q_r, qa_s, qa_r, n_s, n_r, a_s, a_r, t_s, t_r,
+    w_s, w_r, ow_s, ow_r, lo_s, lo_r, l_s, l_r, q_s, q_r, qa_s, qa_r, n_s, n_r, a_s, a_r, t_s, t_r,
     g_s, g_r, gl_s, gl_r, gga_s, gga_r, gq_s, gq_r, sqa_s, sqa_r, p_s, p_r, x_s, x_r, loc,
 ):
     pc = Place()
@@ -205,13 +232,27 @@
     pl.semaphore_signal(barrier, inc=1, device_id=sib, device_id_type=MESH)
     each_peer(CHIPS, greet)
 
+    rows_f32 = jnp.concatenate([keyval_w[...].astype(F32), jnp.zeros((3, 2048), F32)], axis=0).astype(BF16)
+    for c in range(2):
+        wpl[c, :, :512] = rows_f32[:, c * 512 : c * 512 + 512]
+        wpl[c, :, 512:] = rows_f32[:, 1024 + c * 512 : 1536 + c * 512]
+    feats_f32 = lat[...].astype(F32)
+    squares = jnp.broadcast_to(jnp.sum(feats_f32 * feats_f32, axis=1, keepdims=True), (256, 128)).astype(BF16)
+    for c in range(2):
+        for p in range(2):
+            columns = (c * 2 + p) * 256
+            qpart[c, p, :, :256] = dot(lat[...], qw[:, columns : columns + 256]).astype(BF16)
+            qpart[c, p, :, 256:] = squares
+    spot = lax.broadcasted_iota(jnp.int32, (1, 256), 1)
+    kept = ((keep[...] == 1) | (spot == 0)) & (spot < count[...])
+    val[...] = jnp.broadcast_to(jnp.where(kept, 1.0, 0.0), (128, 256)).T
+    gain[...] = jnp.broadcast_to(gain_in[...].astype(F32), (256, 128)).T
+
+    group_half = pl.ds(pl.multiple_of(pc.g * 512, 512), 512)
     local_copies = [
-        pltpu.make_async_copy(
-            owt.at[pl.ds(pl.multiple_of(pc.g * 32, 32), 32), :],
-            ow.at[pc.y, pc.xl, pc.z, core, pc.g],
-            loc.at[0],
-        ),
-        pltpu.make_async_copy(lt, la.at[pc.g, pc.y, pc.xl, pc.z, core], loc.at[1]),
+        pltpu.make_async_copy(owt.at[:, group_half], owe.at[pc.y, pc.xl, pc.z, core], loc.at[0]),
+        pltpu.make_async_copy(lt, lown.at[pc.y, pc.xl, pc.z, core], loc.at[1]),
+        pltpu.make_async_copy(lt, ltp.at[pc.g], loc.at[11]),
         pltpu.make_async_copy(val, valb.at[core], loc.at[2]),
         pltpu.make_async_copy(wpl.at[core], wg.at[pc.x, pc.y, pc.z, at16(core)], loc.at[3]),
     ]
@@ -237,8 +278,9 @@
         tokb[core, :, pl.ds(block * 128, 128)] = dot(tokens[:, pl.ds(base, width)], place).astype(BF16)
 
     weight = Gather(pc, wg, view_weight, w_s, w_r)
-    output = Gather(pc, ow, functools.partial(view_output, core), ow_s, ow_r)
-    latents = Gather(pc, la, functools.partial(view_latents, core), l_s, l_r)
+    output = Gather(pc, owe, functools.partial(view_output, core), ow_s, ow_r, False)
+    latents = Gather(pc, lown, functools.partial(view_own, core), lo_s, lo_r, False)
+    resampled = Gather(pc, la, functools.partial(view_latents, core), l_s, l_r)
     for copy in local_copies:
         copy.wait()
     w_sib.wait_recv()
@@ -260,8 +302,6 @@
     t_sib.start()
     v_sib = over(3, val, valb.at[core], sib)
     v_sib.start()
-    pw_sib = over(4, pw.at[:, 1 - core], pwx, sib)
-    pw_sib.start()
     weight.wait(0)
     weight.start(1)
     q_push.landed()
@@ -277,12 +317,14 @@
     qa_push.start()
     q_own = pltpu.make_async_copy(qblk, q_spot, loc.at[4])
     q_own.start()
-    latents.start(0)
     t_sib.wait()
     v_sib.wait()
     weight.wait(1)
     weight.start(2)
-    output.start(0)
+    pw_sib = over(4, pw.at[:, 1 - core], pwx, sib)
+    pw_sib.start()
+    lt_part = over(16, lt, ltp.at[pc.g], partner)
+    lt_part.start()
 
     for y in range(4):
         pw_t[:, pl.ds(y * 1024, 1024)] = turned(pw[pl.ds(y * 8, 8)].reshape(1024, 128))
@@ -290,11 +332,14 @@
         tok_t[pl.ds(block * 512, 512), :] = turned(
             tokb[:, :, pl.ds(block * 512, 512)].reshape(512, 512)
         )
-    latents.wait(0)
+    q_push.drain()
+    q_own.wait()
+    qa_push.landed()
+    qo_sib = over(17, qg.at[at256(pc.g), :], qo, sib)
+    qo_sib.start()
+    latents.start(0)
+    output.start(0)
     weight.wait(2)
-    latents.start(1)
-    output.wait(0)
-    output.start(1)
 
     tok = tokb[...].reshape(512, 2048)
 
@@ -306,15 +351,18 @@
     lax.fori_loop(0, 4, project, 0)
     for n in range(4):
         kv_t[pl.ds(n * 256, 256), :] = turned(kv[:, n * 256 : n * 256 + 256])
-    q_own.wait()
-    qa_push.landed()
-
-    def n_copy(p, k):
+    latents.wait(0)
+    latents.start(1)
+    output.wait(0)
+    output.start(1)
+
+    def n_copy(k):
         g, j = pc.plane_peer(k)
         return remote(
             npk.at[j % 2, at16(g * 16 + j // 2), :], recvn.at[k], n_s.at[k], n_r.at[k], chip_device(g, j)
         )
 
+    n_push = PairPushes(pc, n_copy)
     for p in range(2):
         packed = []
         sums = []
@@ -335,14 +383,14 @@
             packed.append(dot(kv_t[pl.ds(512 + head * 128, 128), :], half[head]))
             sums.append(jnp.broadcast_to(total, (64, 512)))
         npk[p] = jnp.concatenate(packed + sums, axis=0).T.astype(BF16)
-    n_push = Pushes(CHIPS, lambda k: n_copy(0, k))
-    n_push.start()
+        n_push.start_pair(p)
 
     latents.wait(1)
     latents.start(2)
     output.wait(1)
     output.start(2)
     weight.drain()
+    qa_push.drain()
     n_push.landed()
     total = total_slots(npk[pair, all_rows, :], recvn, CHIPS)
     whole = jnp.concatenate(
@@ -359,40 +407,46 @@
     a_own = pltpu.make_async_copy(ablk, a_spot, loc.at[5])
     a_own.start()
 
+    n_push.drain()
     latents.wait(2)
-    la_sib = over(5, la.at[:, :, :, :, core], la.at[:, :, :, :, core], sib)
-    la_sib.start()
+    lown_sib = over(5, lown.at[:, :, :, core], lown.at[:, :, :, core], sib)
+    lown_sib.start()
     output.wait(2)
-    ow_sib = over(6, ow.at[:, :, :, core], ow.at[:, :, :, core], sib)
-    ow_sib.start()
+    owe_sib = over(6, owe.at[:, :, :, core], owe.at[:, :, :, core], sib)
+    owe_sib.start()
+    lown_sib.wait()
+    owe_sib.wait()
+
+    for n in range(2):
+        folded = dot(pw_t[...], owe[:, :, :, :, :, n * 256 : n * 256 + 256].reshape(4096, 256))
+        fold[:, at256(pc.g * 2 + n)] = folded.astype(BF16)
+    f_part = over(18, fold.at[:, group_half], fold.at[:, group_half], partner)
+    f_part.start()
+    hidden = dot(pw_t[...], lown[...].reshape(4096, 256))
+    squares = jnp.zeros((1, 256), F32)
+    for y in range(4):
+        feats = lown[y].reshape(1024, 256).astype(F32)
+        squares = squares + jnp.sum(feats * feats, axis=0, keepdims=True)
+    rinv_row = lax.rsqrt(squares / D_LAT + 1e-06)
     a_own.wait()
     a_push.landed()
     a_sib = over(7, attf.at[core], attf.at[core], sib)
     a_sib.start()
-
-    la_sib.wait()
-    ow_sib.wait()
-
-    def fold_in(n, carry):
-        columns = at256(n)
-        fold[:, columns] = dot(pw_t[...], ow[:, :, :, :, :, :, columns].reshape(4096, 256)).astype(BF16)
-        return carry
-
-    lax.fori_loop(0, 4, fold_in, 0)
+    f_part.wait()
     f_sib = over(8, fold.at[:, pl.ds(pl.multiple_of((1 - core) * 512, 512), 512)], foldx, sib)
     f_sib.start()
-    hidden = dot(pw_t[...], la[pc.g].reshape(4096, 256))
     a_sib.wait()
     group_rows = at256(pc.g)
     hidden = hidden + col_dot(fold[:, :512], attf[0, group_rows, :])
     hidden = (hidden + col_dot(fold[:, 512:], attf[1, group_rows, :])).astype(BF16).astype(F32)
     grad_y = igrad[...].astype(F32).T
     scaled_dy = grad_y * gain[...]
+    square_row = jnp.sum(hidden * hidden, axis=0, keepdims=True)
+    inner_row = jnp.sum(hidden * scaled_dy, axis=0, keepdims=True)
     sumo[...] = jnp.concatenate(
         [
-            jnp.sum(hidden * hidden, axis=0, keepdims=True),
-            jnp.sum(hidden * scaled_dy, axis=0, keepdims=True),
-            jnp.zeros((6, 256), F32),
+            square_row[:, :128], square_row[:, 128:], inner_row[:, :128], inner_row[:, 128:],
+            jnp.zeros((4, 128), F32),
         ],
         axis=0,
     )
@@ -405,13 +459,17 @@
         lambda k: remote(sumx.at[1], sumr.at[k], t_s.at[k], t_r.at[k], chip_device(pc.g, pc.group_peer(k))),
     )
     t_push.start()
+    lat_out = lt[...].astype(F32) + col_dot(owt[:, :512], attf[0, group_rows, :])
+    la[pc.g, pc.y, pc.xl, pc.z, core] = (lat_out + col_dot(owt[:, 512:], attf[1, group_rows, :])).astype(BF16)
     t_push.landed()
     total = total_slots(sumx[1], sumr, GROUP)
-    hrinv = lax.rsqrt(total[0:1, :] / D_LLM + 1e-05)
+    square_row = jnp.concatenate([total[0:1], total[1:2]], axis=1)
+    inner_row = jnp.concatenate([total[2:3], total[3:4]], axis=1)
+    hrinv = lax.rsqrt(square_row / D_LLM + 1e-05)
     normed = hidden * hrinv
     llm_t[...] = (normed * gain[...]).astype(BF16)
     gain_own = jnp.broadcast_to(jnp.sum(grad_y * normed, axis=1, keepdims=True), (128, 128))
-    grad_h = hrinv * scaled_dy - (hrinv * hrinv * hrinv / D_LLM * total[1:2, :]) * hidden
+    grad_h = hrinv * scaled_dy - (hrinv * hrinv * hrinv / D_LLM * inner_row) * hidden
     gh_t[...] = grad_h.astype(BF16)
     h_sib = over(10, gh_t, ghx, sib)
     h_sib.start()
@@ -437,6 +495,21 @@
     g_push = Pushes(GROUP, g_copy)
     g_push.start()
 
+    resampled.start(0)
+    for push in (a_push, t_push):
+        push.drain()
+    g_push.landed()
+    grad = total_slots(gap[own_rows, at256(pair)], recvg, GROUP).astype(BF16).astype(F32)
+    gblk[...] = (grad / whole).astype(BF16)
+    g_spot = gg.at[all_rows, at256(pair)]
+    gga_push = Pushes(
+        CHIPS,
+        lambda k: remote(gblk, g_spot, gga_s.at[k], gga_r.at[k], chip_device(*pc.plane_peer(k))),
+    )
+    gga_push.start()
+    g_own = pltpu.make_async_copy(gblk, g_spot, loc.at[6])
+    g_own.start()
+
     pw_sib.wait()
     for n in range(4):
         part = dot(pw[pl.ds(n * 8, 8), core].reshape(512, 128), gh_t[...])
@@ -448,46 +521,43 @@
         return remote(glp.at[j], recvl.at[k], gl_s.at[k], gl_r.at[k], chip_device(pc.g, j))
 
     l_push = Pushes(GROUP, l_copy)
-    l_push.start()
-    g_push.landed()
-    grad = total_slots(gap[own_rows, at256(pair)], recvg, GROUP).astype(BF16).astype(F32)
-    prod = grad * ablk[...].astype(F32)
-    first = jnp.sum(prod[:, :128], axis=1, keepdims=True) / whole[:, :1]
-    second = jnp.sum(prod[:, 128:], axis=1, keepdims=True) / whole[:, 128:129]
-    lane = lax.broadcasted_iota(jnp.int32, (16, 128), 1)
-    gblk[:, :256] = (grad / whole).astype(BF16)
-    gblk[:, 256:] = jnp.where(lane < 64, first, second).astype(BF16)
-    g_spot = gg.at[pair, all_rows, :]
-    gga_push = Pushes(
-        CHIPS,
-        lambda k: remote(gblk, g_spot, gga_s.at[k], gga_r.at[k], chip_device(*pc.plane_peer(k))),
-    )
-    gga_push.start()
-    g_own = pltpu.make_async_copy(gblk, g_spot, loc.at[6])
-    g_own.start()
-    l_push.landed()
-    lblk[...] = total_slots(glp[pc.j], recvl, GROUP).astype(BF16)
-    glf[pc.g] = lblk[...]
-    l_part = over(13, lblk, glf.at[pc.g], partner)
-    l_part.start()
+    resampled.wait(0)
+    resampled.start(1)
+    g_push.drain()
     g_own.wait()
     gga_push.landed()
-
+    l_push.start()
+
+    def gq_copy(k):
+        g, j = pc.plane_peer(k)
+        return remote(
+            gqp.at[at16(g * 16 + j // 2), at256(j % 2)], recvgq.at[k], gq_s.at[k], gq_r.at[k], chip_device(g, j)
+        )
+
+    gq_push = PairPushes(pc, gq_copy)
+    ones = jnp.ones((8, 128), BF16)
     for p in range(2):
-        deltas = gg[p, :, 256:].astype(F32).T
-        for side in range(2):
-            head = p * 2 + side
+        parts = []
+        for head in (p * 2, p * 2 + 1):
             columns = pl.ds(head * 128, 128)
-            grads = gg[p, :, side * 128 : side * 128 + 128]
-            query = qg[:, columns]
-            delta = deltas[side * 64 : side * 64 + 1, :]
+            grads = gg[:, columns]
+            prod = grads.astype(F32) * attf[core, :, columns].astype(F32)
+            high = prod.astype(BF16)
+            rest = (prod - high.astype(F32)).astype(BF16)
+            delta = (col_dot(ones, high) + col_dot(ones, rest))[:1, :].astype(BF16).astype(F32)
             for chunk in range(4):
                 slots = pl.ds(chunk * 128, 128)
                 prob = col_dot(kv[slots, 512 + head * 128 : 640 + head * 128], grads)
-                score = (fac[head, slots, :] * (prob - delta)).astype(BF16)
-                ds[head, slots, :] = score
-                gkv[slots, columns] = dot(score, query).astype(BF16)
-                gkv[slots, 512 + head * 128 : 640 + head * 128] = dot(half[head, slots, :], grads).astype(BF16)
+                ds[head, slots, :] = (fac[head, slots, :] * (prob - delta)).astype(BF16)
+            parts.append(dot(kv_t[pl.ds(head * 128, 128), :], ds[head]))
+        gqp[:, p * 256 : p * 256 + 256] = jnp.concatenate(parts, axis=0).T.astype(BF16)
+        gq_push.start_pair(p)
+    resampled.wait(1)
+    resampled.start(2)
+    for head in range(4):
+        columns = pl.ds(head * 128, 128)
+        gkv[:, columns] = dot(ds[head], qg[:, columns]).astype(BF16)
+        gkv[:, 512 + head * 128 : 640 + head * 128] = dot(half[head], gg[:, columns]).astype(BF16)
 
     first, once = (r1a, r1b, r1c), (s1a, s1b, s1c)
     second, twice = (r2a, r2b, r2c), (s2a, s2b, s2c)
@@ -528,45 +598,16 @@
         copy.start()
         held_first.append(copy)
 
-    for p in range(2):
-        parts = [
-            dot(kv_t[pl.ds(head * 128, 128), :], ds[head]) for head in (p * 2, p * 2 + 1)
-        ]
-        gqp[:, p * 256 : p * 256 + 256] = jnp.concatenate(parts, axis=0).T.astype(BF16)
-
-    def gq_copy(k):
-        g, j = pc.plane_peer(k)
-        return remote(
-            gqp.at[at16(g * 16 + j // 2), at256(j % 2)], recvgq.at[k], gq_s.at[k], gq_r.at[k], chip_device(g, j)
-        )
-
-    gq_push = Pushes(CHIPS, gq_copy)
-    gq_push.start()
-
-    h_part.wait()
-    mixed = [
-        (dot(ghp[0], attf[c, :256, :]) + dot(ghp[1], attf[c, 256:, :])).astype(BF16) for c in range(2)
-    ]
-    mixed_t = jnp.concatenate(mixed, axis=1)
-    gh_both = [turned(ghp[n]) for n in range(2)]
-
-    def project_grad(n, carry):
-        y, xl = n // 2, n % 2
-        gpw[y, xl] = (
-            dot(la[0, y, xl].reshape(512, 256), gh_both[0])
-            + dot(la[1, y, xl].reshape(512, 256), gh_both[1])
-            + col_dot(ow[y, xl].reshape(512, 1024), mixed_t)
-        )
-        return carry
-
-    lax.fori_loop(0, 8, project_grad, 0)
-
+    gga_push.drain()
+    l_push.landed()
+    lblk[...] = total_slots(glp[pc.j], recvl, GROUP).astype(BF16)
+    glf[pc.g] = lblk[...]
+    l_part = over(13, lblk, glf.at[pc.g], partner)
+    l_part.start()
     gq_push.landed()
     grad = total_slots(gqp[all_rows, at256(pair)], recvgq, CHIPS)
-    sblk[:, :256] = (grad * rinv[:, :1]).astype(BF16)
-    ratio = jnp.sum(grad * proj, axis=1, keepdims=True) * (rinv * rinv * rinv / D_LAT)
-    sblk[:, 256:] = ratio.astype(BF16)
-    s_spot = sq.at[core, pair, all_rows, :]
+    sblk[...] = (grad * rinv[:, :1]).astype(BF16)
+    s_spot = sq.at[core, all_rows, at256(pair)]
     sqa_push = Pushes(
         CHIPS,
         lambda k: remote(sblk, s_spot, sqa_s.at[k], sqa_r.at[k], chip_device(*pc.plane_peer(k))),
@@ -574,6 +615,10 @@
     sqa_push.start()
     s_own = pltpu.make_async_copy(sblk, s_spot, loc.at[10])
     s_own.start()
+
+    resampled.wait(2)
+    la_sib = over(14, la.at[:, :, :, :, core], la.at[:, :, :, :, core], sib)
+    la_sib.start()
 
     for part in range(3):
         held_first[part].wait()
@@ -591,12 +636,11 @@
             copy.start()
 
     l_part.wait()
-    gow_t[...] = jnp.concatenate(
-        [dot(glf[0], attf[c, :256, :]) + dot(glf[1], attf[c, 256:, :]) for c in range(2)], axis=1
-    )
+    l_push.drain()
+    gq_push.drain()
     s_own.wait()
     sqa_push.landed()
-    s_sib2 = over(14, sq.at[core], sq.at[core], sib)
+    s_sib2 = over(15, sq.at[core], sq.at[core], sib)
     s_sib2.start()
 
     for part in range(3):
@@ -616,21 +660,39 @@
         for copy in copies(part, 2):
             copy.start()
 
+    h_part.wait()
+    la_sib.wait()
+    gh_both = [turned(ghp[n]) for n in range(2)]
+
+    def project_grad(n, carry):
+        y, xl = n // 2, n % 2
+        gpw[y, xl] = dot(la[0, y, xl].reshape(512, 256), gh_both[0]) + dot(
+            la[1, y, xl].reshape(512, 256), gh_both[1]
+        )
+        return carry
+
+    lax.fori_loop(0, 8, project_grad, 0)
+    for c in range(2):
+        gow_t[:, c * 512 : c * 512 + 512] = dot(glf[0], attf[c, :256, :]) + dot(glf[1], attf[c, 256:, :])
+    lt_part.wait()
+    qo_sib.wait()
     s_sib2.wait()
-    feats = [la[n, pc.y, pc.xl, pc.z, core] for n in range(2)]
+    back = glf[pc.g].astype(F32)
+    ratio = jnp.zeros((256, 128), F32)
     for c in range(2):
-        for p in range(2):
-            columns = pl.ds((c * 2 + p) * 256, 256)
-            gqw[:, columns] = dot(feats[0], sq[c, p, :256, :256]) + dot(feats[1], sq[c, p, 256:, :256])
-    mine_f = la[pc.g, pc.y, pc.xl, pc.z, core].astype(F32)
-    back = glf[pc.g].astype(F32)
-    coef = jnp.zeros((256, 128), F32)
-    for c in range(2):
-        for p in range(2):
-            block = sq[c, p, group_rows, :]
-            back = back + col_dot(qw[:, (c * 2 + p) * 256 : (c * 2 + p) * 256 + 256], block[:, :256])
-            coef = coef + block[:, 256:].astype(F32)
-    gl_out[...] = back - coef.T[:1, :] * mine_f
+        columns = pl.ds(c * 512, 512)
+        gqw[:, columns] = dot(ltp[0], sq[c, :256, :]) + dot(ltp[1], sq[c, 256:, :])
+        block = sq[c, group_rows, :]
+        back = back + col_dot(qw[:, columns], block)
+    for block, query in ((sq[core, group_rows, :], qg[group_rows, :]), (sq[1 - core, group_rows, :], qo[...])):
+        prod = block.astype(F32) * query.astype(F32)
+        for n in range(4):
+            ratio = ratio + prod[:, n * 128 : n * 128 + 128]
+    coef = jnp.sum(ratio.T, axis=0, keepdims=True) * rinv_row / D_LAT
+    gl_out[...] = back - coef * lt[...].astype(F32)
+    sqa_push.drain()
+    for gather in (latents, output, resampled):
+        gather.drain()
 
     for part in range(3):
         for copy in copies(part, 2):
@@ -639,7 +701,7 @@
         fin[:, pl.ds(*WIDE[part])] = twice[part][here].astype(F32) + sum(
             third[part][s].astype(F32) for s in range(1, 4)
         )
-    give = over(15, fin.at[at16(1 - core), :], oth, sib)
+    give = over(19, fin.at[at16(1 - core), :], oth, sib)
     give.start()
     gw[core] = fin[at16(core), :]
     give.wait()
@@ -648,10 +710,6 @@
     gain_part.wait()
     w_sib.wait_send()
     q_sib.wait_send()
-    for gather in (latents, output):
-        gather.drain()
-    for push in (q_push, qa_push, n_push, a_push, t_push, g_push, l_push, gga_push, gq_push, sqa_push):
-        push.drain()
     for part in range(3):
         for phase in range(3):
             for copy in copies(part, phase):
@@ -662,29 +720,31 @@
     return [pltpu.SemaphoreType.DMA((n,)) for n in counts]
 
 
+def finish_kernel(llm_t, gl_t, gqw, gw, gow_t, gains, gpw, llm, gl, gqw_out, gkw, gow, gpw_out, gain, done):
+    copy = pltpu.make_async_copy(gpw, gpw_out, done)
+    copy.start()
+    llm[...] = turned(llm_t[...])
+    gl[...] = gl_t[...].T
+    gqw_out[...] = gqw[...]
+    gow[...] = gow_t[...].T
+    for c in range(2):
+        rows = gw[c]
+        gkw[:, c * 512 : c * 512 + 512] = rows[:13, :512]
+        gkw[:, 1024 + c * 512 : 1536 + c * 512] = rows[:13, 512:]
+    gain[...] = (gains[0] + gains[1]).T[0, :]
+    copy.wait()
+
+
 def local(
     tokens, keep_mask, shard_counts, latents, query_weight, keyval_weight, output_weight,
     project_weight, llm_gain, input_grad,
 ):
-    latent_f32 = latents.astype(F32)
-    squares = jnp.sum(latent_f32 * latent_f32, axis=1)
-    product = dot(latents, query_weight)
-    qpart = jnp.concatenate(
-        [
-            product.reshape(256, 4, 256).transpose(1, 0, 2),
-            jnp.broadcast_to(squares[None, :, None], (4, 256, 128)),
-        ],
-        axis=2,
-    ).astype(BF16)
-    padded = jnp.pad(keyval_weight, ((0, 3), (0, 0)))
-    wpl = padded.reshape(16, 2, 2, 512).transpose(2, 0, 1, 3).reshape(2, 16, 1024)
-    positions = jnp.arange(256, dtype=jnp.int32)
-    valid = (((keep_mask == 1) | (positions == 0)) & (positions < shard_counts[0])).astype(F32)
-    val = jnp.broadcast_to(valid[:, None], (256, 128))
-    gain = jnp.broadcast_to(llm_gain.astype(F32)[:, None], (128, 256))
-
     widths = [w for _, w in WIDE]
     scratch = [
+        ((256, 128), F32),
+        ((2, 2, 256, 384), BF16),
+        ((2, 16, 1024), BF16),
+        ((128, 256), F32),
         ((4, 4, 4, 32, 1024), BF16),
         ((2, 256, 2048), BF16),
         ((2048, 512), BF16),
@@ -694,7 +754,10 @@
         ((32, 16, 384), BF16),
         ((16, 256), BF16),
         ((512, 512), BF16),
-        ((4, 2, 4, 2, 2, 32, 1024), BF16),
+        ((256, 512), BF16),
+        ((4, 2, 4, 2, 64, 512), BF16),
+        ((4, 2, 4, 2, 64, 256), BF16),
+        ((2, 64, 256), BF16),
         ((2, 4, 2, 4, 2, 64, 256), BF16),
         ((512, 1024), BF16),
         ((1024, 512), BF16),
@@ -708,9 +771,9 @@
         ((32, 64, 128), BF16),
         ((128, 1024), BF16),
         ((128, 512), BF16),
-        ((2, 8, 256), F32),
-        ((8, 256), F32),
-        ((32, 8, 256), F32),
+        ((2, 8, 128), F32),
+        ((8, 128), F32),
+        ((32, 8, 128), F32),
         ((128, 256), BF16),
         ((128, 256), BF16),
         ((2, 128, 256), BF16),
@@ -720,14 +783,14 @@
         ((32, 64, 256), BF16),
         ((64, 256), BF16),
         ((2, 64, 256), BF16),
-        ((16, 384), BF16),
-        ((2, 512, 384), BF16),
+        ((16, 256), BF16),
+        ((512, 512), BF16),
         ((4, 512, 512), BF16),
         ((512, 512), BF16),
         ((64, 16, 256), BF16),
         ((512, 1024), BF16),
-        ((16, 384), BF16),
-        ((2, 2, 512, 384), BF16),
+        ((16, 256), BF16),
+        ((2, 512, 512), BF16),
         *[((4, 4, 4, 32, w), BF16) for w in widths],
         *[((4, 4, 32, w), BF16) for w in widths],
         *[((4, 4, 32, w), BF16) for w in widths],
@@ -750,29 +813,41 @@
                 ((2, 16, 1024), F32),
             )
         ],
-        in_specs=[VMEM] * 10,
+        in_specs=[VMEM] * 11,
         out_specs=[VMEM] * 7,
         scratch_shapes=[pltpu.VMEM(s, d) for s, d in scratch]
-        + sems(27, 27, 27, 27, 27, 27, 32, 32, 64, 64, 64, 64, 64, 64, 32, 32)
-        + sems(32, 32, 32, 32, 64, 64, 64, 64, 64, 64, 27, 27, 16, 16, 11),
+        + sems(27, 27, 27, 27, 27, 27, 27, 27, 32, 32, 64, 64, 64, 64, 64, 64, 32, 32)
+        + sems(32, 32, 32, 32, 64, 64, 64, 64, 64, 64, 27, 27, 20, 20, 12),
         compiler_params=pltpu.CompilerParams(
             has_side_effects=True, vmem_limit_bytes=62 << 20, collective_id=0
         ),
         name="whole",
     )(
-        tokens, val, qpart.reshape(2, 2, 256, 384), wpl, output_weight.T, latents.T,
-        project_weight.reshape(32, 2, 64, 128), input_grad, gain, query_weight,
-    )
-
-    return (
-        llm_t.T,
-        gl_out.T,
-        gqw,
-        gw[:, :13].reshape(2, 13, 2, 512).transpose(1, 2, 0, 3).reshape(13, 2048),
-        gow_t.T,
-        gpw.reshape(4096, 128),
-        gain_out[0, :, 0] + gain_out[1, :, 0],
-    )
+        tokens, keep_mask.reshape(1, 256), shard_counts.reshape(1, 1), latents, query_weight, keyval_weight,
+        output_weight.T, latents.T, project_weight.reshape(32, 2, 64, 128), input_grad,
+        llm_gain.reshape(1, 128),
+    )
+
+    return pl.pallas_call(
+        finish_kernel,
+        out_shape=[
+            jax.ShapeDtypeStruct(shape, dtype)
+            for shape, dtype in (
+                ((256, 128), BF16),
+                ((256, 64), F32),
+                ((64, 1024), F32),
+                ((13, 2048), F32),
+                ((1024, 64), F32),
+                ((4096, 128), F32),
+                ((128,), F32),
+            )
+        ],
+        in_specs=[VMEM] * 6 + [ANY],
+        out_specs=[VMEM] * 5 + [ANY, VMEM],
+        scratch_shapes=[pltpu.SemaphoreType.DMA],
+        compiler_params=pltpu.CompilerParams(vmem_limit_bytes=32 << 20),
+        name="finish",
+    )(llm_t, gl_out, gqw, gw, gow_t, gain_out, gpw.reshape(4096, 128))
 
 
 def solution(mesh):

time: 244 us -> 216 us (0.89)
  Pallas kernels: 223 us -> 205 us
  other arithmetic: 3.92 us -> 0 us
  local copies, waits for them, and re-layouts: 13.5 us -> 10.1 us
    pallas_call x1, Pallas kernels: 223 us -> 202 us  [local(): pl.pallas_call(whole_kernel, out_shape=[jax.ShapeDtypeStruct(s, d) for s,...]
    reshape x6 -> x0, local copies, waits for them, and re-layouts: 2.53 us -> none  [the longest x2 1.74 us: local(): gw[:, :13].reshape(2, 13, 2, 512).transpose(1, 2, 0, 3).reshape(13, 2048)]
    unnamed x7 -> x15, local copies, waits for them, and re-layouts: 7.86 us -> 8.46 us
where the time goes in v3:
time: 216 us
  Pallas kernels  205 us (95%)
  local copies, waits for them, and re-layouts  10.1 us (5%)
    pallas_call x1, Pallas kernels, local(): pl.pallas_call(whole_kernel, out_shape=[jax.ShapeDtypeStruct(s, d) for s,...  202 us
    unnamed x15, local copies, waits for them, and re-layouts  8.46 us

profile of v3, /device:TPU:1, one launch (start us, length us, event | category | flops | bytes accessed | tf_op | source)
XLA Modules:
  0.0 216.0 jit_solution(6160623219485670473)
XLA Ops:
  1.3 1.5 copy.17.lat
  2.8 202.5 %whole.1 = (bf16[128,256]{1,0:T(8,128)(2,1)}, f32[2,128,128]{2,1,0:T(8,128)}, f32[4,2,512,128]{3,2,1,0:T(8,128)}, f32[64,1024]{1,0:T(8,128)}, f32[64,1024]{1,0:T...) custom-call(bf16[256,1664]{1,0:T(8,128)(2,1)} %tokens.1, s32[1,256]{1,0:T(1,128)} %bitcast.12, s32[1,1]{1,0:T(1,128)} %bitcast.7.count, ...), custom_call_target="tpu_custom_call" | custom-call | tf_op jit(solution)/shard_map/whole/pallas_call | solution.py:802
  205.3 0.0 copy-start
  205.3 1.6 copy-done
  206.9 0.0 copy-start.1
  206.9 0.9 copy-done.1
  207.8 0.0 copy-start.2
  207.8 0.9 copy-done.2
  208.8 0.0 copy-start.3
  208.8 0.9 copy-done.3
  209.7 0.0 copy-start.4
  209.7 0.9 copy-done.4
  210.6 0.0 copy-start.5
  210.6 0.8 copy-done.5
  211.4 0.0 copy-start.6
  211.4 0.8 copy-done.6
  212.2 2.1 finish.1
  214.4 0.7 copy.18
  215.1 0.9 copy.19
Async XLA Ops:
  205.3 1.6 copy-start
  206.9 0.9 copy-start.1
  207.8 0.9 copy-start.2
  208.8 0.9 copy-start.3
  209.7 0.9 copy-start.4
  210.6 0.8 copy-start.5
  211.4 0.8 copy-start.6

commit v4 on v3

--- a/solution.py
+++ b/solution.py
@@ -72,6 +72,20 @@
     return pltpu.make_async_remote_copy(
         src_ref=src, dst_ref=dst, send_sem=sends, recv_sem=recvs, device_id=device, device_id_type=MESH
     )
+
+
+class Later:
+    def __init__(self, make):
+        self.make = make
+
+    def start(self):
+        self.make().start()
+
+    def wait_recv(self):
+        self.make().wait_recv()
+
+    def wait_send(self):
+        self.make().wait_send()
 
 
 def each_peer(n, do):
@@ -102,32 +116,101 @@
                     peer[0] = pc.g * 2 + 1 - pc.xl
                 else:
                     peer[order[phase]] = (peer[order[phase]] + step) % 4
-                g, j = pc.chip(*peer)
-                spot = (part * 3 + phase) * 3 + step - 1
-                yield remote(
-                    block, block, self.sends.at[spot], self.recvs.at[spot], (g, j * 2 + pc.core)
-                )
+                yield self.push(block, (part * 2 + phase) * 3 + step - 1, peer)
+
+    def push(self, block, spot, peer):
+        g, j = self.place.chip(*peer)
+        device = (g, j * 2 + self.place.core)
+        return Later(lambda: remote(block, block, self.sends.at[spot], self.recvs.at[spot], device))
+
+    def last(self, part):
+        pc = self.place
+        order = ORDERS[part]
+        axis = order[2]
+        mine = [pc.x, pc.y, pc.z]
+        base = 18 + part * 6
+        if axis == 0 and not self.whole:
+            held = [mine[0], None, None]
+            block = self.view(self.ref, *held, part)
+            return [self.push(block, base, [pc.g * 2 + 1 - pc.xl, pc.y, pc.z])]
+
+        def at(place, half):
+            held = [None, None, None]
+            held[axis] = place
+            held[order[0]] = Half(half)
+            return self.view(self.ref, *held, part)
+
+        here, up, down = mine[axis], (mine[axis] + 1) % 4, (mine[axis] + 3) % 4
+        above, below = list(mine), list(mine)
+        above[axis], below[axis] = up, down
+        return [
+            self.push(at(here, 0), base, above),
+            self.push(at(here, 1), base + 1, above),
+            self.push(at(here, 1), base + 2, below),
+            self.push(at(here, 0), base + 3, below),
+            self.push(at(down, 0), base + 4, above),
+            self.push(at(up, 1), base + 5, below),
+        ]
 
     def start(self, phase):
-        for copy in self.copies(phase):
-            copy.start()
+        if phase < 2:
+            for copy in self.copies(phase):
+                copy.start()
+            return
+        for part in range(3):
+            copies = self.last(part)
+            for n in (0,) if len(copies) == 1 else (0, 2, 1, 3):
+                copies[n].start()
+
+    def relay(self):
+        for part in range(3):
+            copies = self.last(part)
+            if len(copies) > 1:
+                copies[0].wait_recv()
+                copies[4].start()
+                copies[2].wait_recv()
+                copies[5].start()
 
     def wait(self, phase):
-        for copy in self.copies(phase):
-            copy.wait_recv()
+        if phase < 2:
+            for copy in self.copies(phase):
+                copy.wait_recv()
+            return
+        for part in range(3):
+            copies = self.last(part)
+            for n in (0,) if len(copies) == 1 else (1, 3, 4, 5):
+                copies[n].wait_recv()
 
     def drain(self):
-        for phase in range(3):
+        for phase in range(2):
             for copy in self.copies(phase):
                 copy.wait_send()
+        for part in range(3):
+            for copy in self.last(part):
+                copy.wait_send()
+
+
+class Half:
+    def __init__(self, n):
+        self.n = n
 
 
 def pick(value):
+    if isinstance(value, Half):
+        return slice(value.n * 2, value.n * 2 + 2)
     return slice(None) if value is None else value
 
 
 def halves(x):
+    if isinstance(x, Half):
+        return x.n, slice(None)
     return (slice(None), slice(None)) if x is None else (x // 2, x % 2)
+
+
+def in_group(x):
+    if isinstance(x, Half):
+        return slice(x.n, x.n + 1)
+    return slice(None) if x is None else x % 2
 
 
 def view_weight(ref, x, y, z, part):
@@ -135,11 +218,11 @@
 
 
 def view_output(core, ref, x, y, z, part):
-    return ref.at[pick(y), slice(None) if x is None else x % 2, pick(z), core, :, pl.ds(*COLUMNS_512[part])]
+    return ref.at[pick(y), in_group(x), pick(z), core, :, pl.ds(*COLUMNS_512[part])]
 
 
 def view_own(core, ref, x, y, z, part):
-    return ref.at[pick(y), slice(None) if x is None else x % 2, pick(z), core, pl.ds(*ROWS_64[part]), :]
+    return ref.at[pick(y), in_group(x), pick(z), core, pl.ds(*ROWS_64[part]), :]
 
 
 def view_latents(core, ref, x, y, z, part):
@@ -199,15 +282,16 @@
 
 
 def whole_kernel(
-    tokens, keep, count, lat, qw, keyval_w, owt, lt, pw, igrad, gain_in,
-    llm_t, gain_out, gpw, gow_t, gqw, gl_out, gw,
+    keep, count, gain_in, tokens_in, keyval_in, qw_in, lt_in, owt_in, pw_in, igrad_in,
+    llm_to, gl_to, gqw_to, gkw_to, gow_to, gpw_to, gain_to,
+    tokens, keyval_w, qw, lt, owt, pw, igrad, llm, gl_out, gqw, gkw, gow_t, gpw, gain_row, gain_out,
     val, qpart, wpl, gain,
     wg, tokb, tok_t, valb, qx, qsum, recvq, qblk, qg, qo, owe, lown, ltp, la, kv, kv_t, fac, half, npk, recvn,
     ablk, attf, pw_t, pwx, fold, foldx, sumx, sumo, sumr, gh_t, ghx, ghp, gap, recvg, glp, recvl,
     lblk, glf, gblk, gg, ds, gqp, recvgq, gkv, sblk, sq, r1a, r1b, r1c, s1a, s1b, s1c,
-    r2a, r2b, r2c, s2a, s2b, s2c, r3a, r3b, r3c, fin, oth,
+    r2a, r2b, r2c, s2a, s2b, s2c, r3a, r3b, r3c, fara, farb, farc, fin, oth,
     w_s, w_r, ow_s, ow_r, lo_s, lo_r, l_s, l_r, q_s, q_r, qa_s, qa_r, n_s, n_r, a_s, a_r, t_s, t_r,
-    g_s, g_r, gl_s, gl_r, gga_s, gga_r, gq_s, gq_r, sqa_s, sqa_r, p_s, p_r, x_s, x_r, loc,
+    g_s, g_r, gl_s, gl_r, gga_s, gga_r, gq_s, gq_r, sqa_s, sqa_r, p_s, p_r, x_s, x_r, loc, out_s,
 ):
     pc = Place()
     core = pc.core
@@ -232,16 +316,32 @@
     pl.semaphore_signal(barrier, inc=1, device_id=sib, device_id_type=MESH)
     each_peer(CHIPS, greet)
 
+    loads = [
+        pltpu.make_async_copy(src, dst, loc.at[12 + n])
+        for n, (src, dst) in enumerate(
+            (
+                (keyval_in, keyval_w), (lt_in, lt), (qw_in, qw), (owt_in, owt),
+                (tokens_in, tokens), (pw_in, pw), (igrad_in, igrad),
+            )
+        )
+    ]
+    for copy in loads:
+        copy.start()
+    for copy in loads:
+        copy.wait()
+
     rows_f32 = jnp.concatenate([keyval_w[...].astype(F32), jnp.zeros((3, 2048), F32)], axis=0).astype(BF16)
     for c in range(2):
         wpl[c, :, :512] = rows_f32[:, c * 512 : c * 512 + 512]
         wpl[c, :, 512:] = rows_f32[:, 1024 + c * 512 : 1536 + c * 512]
-    feats_f32 = lat[...].astype(F32)
-    squares = jnp.broadcast_to(jnp.sum(feats_f32 * feats_f32, axis=1, keepdims=True), (256, 128)).astype(BF16)
+    feats_f32 = lt[...].astype(F32)
+    lat = feats_f32.T.astype(BF16)
+    squares = jnp.sum(feats_f32 * feats_f32, axis=0, keepdims=True)
+    squares = jnp.broadcast_to(squares, (128, 256)).T.astype(BF16)
     for c in range(2):
         for p in range(2):
             columns = (c * 2 + p) * 256
-            qpart[c, p, :, :256] = dot(lat[...], qw[:, columns : columns + 256]).astype(BF16)
+            qpart[c, p, :, :256] = dot(lat, qw[:, columns : columns + 256]).astype(BF16)
             qpart[c, p, :, 256:] = squares
     spot = lax.broadcasted_iota(jnp.int32, (1, 256), 1)
     kept = ((keep[...] == 1) | (spot == 0)) & (spot < count[...])
@@ -326,6 +426,8 @@
     lt_part = over(16, lt, ltp.at[pc.g], partner)
     lt_part.start()
 
+    weight.relay()
+
     for y in range(4):
         pw_t[:, pl.ds(y * 1024, 1024)] = turned(pw[pl.ds(y * 8, 8)].reshape(1024, 128))
     for block in range(4):
@@ -340,6 +442,10 @@
     latents.start(0)
     output.start(0)
     weight.wait(2)
+    latents.wait(0)
+    latents.start(1)
+    output.wait(0)
+    output.start(1)
 
     tok = tokb[...].reshape(512, 2048)
 
@@ -351,10 +457,6 @@
     lax.fori_loop(0, 4, project, 0)
     for n in range(4):
         kv_t[pl.ds(n * 256, 256), :] = turned(kv[:, n * 256 : n * 256 + 256])
-    latents.wait(0)
-    latents.start(1)
-    output.wait(0)
-    output.start(1)
 
     def n_copy(k):
         g, j = pc.plane_peer(k)
@@ -384,11 +486,14 @@
             sums.append(jnp.broadcast_to(total, (64, 512)))
         npk[p] = jnp.concatenate(packed + sums, axis=0).T.astype(BF16)
         n_push.start_pair(p)
-
-    latents.wait(1)
-    latents.start(2)
-    output.wait(1)
-    output.start(2)
+        if p == 0:
+            latents.wait(1)
+            latents.start(2)
+            output.wait(1)
+            output.start(2)
+
+    latents.relay()
+    output.relay()
     weight.drain()
     qa_push.drain()
     n_push.landed()
@@ -461,13 +566,16 @@
     t_push.start()
     lat_out = lt[...].astype(F32) + col_dot(owt[:, :512], attf[0, group_rows, :])
     la[pc.g, pc.y, pc.xl, pc.z, core] = (lat_out + col_dot(owt[:, 512:], attf[1, group_rows, :])).astype(BF16)
+    resampled.start(0)
     t_push.landed()
     total = total_slots(sumx[1], sumr, GROUP)
     square_row = jnp.concatenate([total[0:1], total[1:2]], axis=1)
     inner_row = jnp.concatenate([total[2:3], total[3:4]], axis=1)
     hrinv = lax.rsqrt(square_row / D_LLM + 1e-05)
     normed = hidden * hrinv
-    llm_t[...] = (normed * gain[...]).astype(BF16)
+    llm[...] = turned(normed * gain[...])
+    give_llm = pltpu.make_async_copy(llm, llm_to, out_s.at[0])
+    give_llm.start()
     gain_own = jnp.broadcast_to(jnp.sum(grad_y * normed, axis=1, keepdims=True), (128, 128))
     grad_h = hrinv * scaled_dy - (hrinv * hrinv * hrinv / D_LLM * inner_row) * hidden
     gh_t[...] = grad_h.astype(BF16)
@@ -495,7 +603,8 @@
     g_push = Pushes(GROUP, g_copy)
     g_push.start()
 
-    resampled.start(0)
+    resampled.wait(0)
+    resampled.start(1)
     for push in (a_push, t_push):
         push.drain()
     g_push.landed()
@@ -521,8 +630,8 @@
         return remote(glp.at[j], recvl.at[k], gl_s.at[k], gl_r.at[k], chip_device(pc.g, j))
 
     l_push = Pushes(GROUP, l_copy)
-    resampled.wait(0)
-    resampled.start(1)
+    resampled.wait(1)
+    resampled.start(2)
     g_push.drain()
     g_own.wait()
     gga_push.landed()
@@ -552,8 +661,7 @@
             parts.append(dot(kv_t[pl.ds(head * 128, 128), :], ds[head]))
         gqp[:, p * 256 : p * 256 + 256] = jnp.concatenate(parts, axis=0).T.astype(BF16)
         gq_push.start_pair(p)
-    resampled.wait(1)
-    resampled.start(2)
+    resampled.relay()
     for head in range(4):
         columns = pl.ds(head * 128, 128)
         gkv[:, columns] = dot(ds[head], qg[:, columns]).astype(BF16)
@@ -571,32 +679,86 @@
                 .reshape(4, 4, 32, 512)
             )
 
-    def slab(part, phase, spot):
-        order = ORDERS[part]
-        index = [spot if axis == order[phase] else slice(None) for axis in range(3) if axis not in order[:phase]]
-        if phase == 0:
-            return wg.at[(*index, slice(None), pl.ds(*WIDE[part]))]
-        return (once, twice)[phase - 1][part].at[tuple(index)]
+    far = (fara, farb, farc)
+
+    def slab(part, spot, half=None):
+        axis = ORDERS[part][0]
+        index = [pick(None if half is None else Half(half))] + [slice(None)]
+        index.insert(axis, spot)
+        return wg.at[(*index, slice(None), pl.ds(*WIDE[part]))]
+
+    def ring(part):
+        axis = ORDERS[part][0]
+        up, down = (mine[axis] + 1) % 4, (mine[axis] + 3) % 4
+        beyond = (mine[axis] + 2) % 4
+        above, below = list(mine), list(mine)
+        above[axis], below[axis] = up, down
+        moves = (
+            (slab(part, beyond, 0), far[part].at[0], above),
+            (slab(part, beyond, 1), far[part].at[1], below),
+            (slab(part, up, 1), first[part].at[1, 2:4], above),
+            (slab(part, down, 0), first[part].at[2, 0:2], below),
+            (slab(part, up, 0), first[part].at[1, 0:2], above),
+            (slab(part, down, 1), first[part].at[2, 2:4], below),
+        )
+
+        def move(n):
+            src, dst, peer = moves[n]
+            spot = part * 6 + n
+            return remote(src, dst, p_s.at[spot], p_r.at[spot], chip_device(*pc.chip(*peer)))
+
+        return [Later(functools.partial(move, n)) for n in range(6)]
+
+    def add_far(part, spot, half):
+        axis = ORDERS[part][0]
+        columns = pl.ds(*WIDE[part])
+
+        def body(n, carry):
+            index = [half * 2 + n // 4, n % 4]
+            index.insert(axis, spot)
+            held = wg[(*index, slice(None), columns)].astype(F32)
+            wg[(*index, slice(None), columns)] = (held + far[part][half, n // 4, n % 4].astype(F32)).astype(BF16)
+            return carry
+
+        lax.fori_loop(0, 8, body, 0)
 
     def copies(part, phase):
         axis = ORDERS[part][phase]
         for step in (1, 3, 2):
             peer = list(mine)
             peer[axis] = (peer[axis] + step) % 4
-            spot = (part * 3 + phase) * 3 + step - 1
+            spot = 18 + (part * 2 + phase - 1) * 3 + step - 1
+            order = ORDERS[part]
+            index = [
+                peer[axis] if n == axis else slice(None) for n in range(3) if n not in order[:phase]
+            ]
             yield remote(
-                slab(part, phase, peer[axis]),
-                (first, second, third)[phase][part].at[step],
+                (once, twice)[phase - 1][part].at[tuple(index)],
+                (second, third)[phase - 1][part].at[step],
                 p_s.at[spot], p_r.at[spot], chip_device(*pc.chip(*peer)),
             )
 
+    for part in range(3):
+        sent = ring(part)
+        for n in range(2):
+            sent[n].start()
     held_first = []
     for part in range(3):
-        for copy in copies(part, 0):
-            copy.start()
-        copy = pltpu.make_async_copy(slab(part, 0, mine[ORDERS[part][0]]), first[part].at[0], loc.at[7 + part])
+        sent = ring(part)
+        for n in range(2, 4):
+            sent[n].start()
+        copy = pltpu.make_async_copy(slab(part, mine[ORDERS[part][0]]), first[part].at[0], loc.at[7 + part])
         copy.start()
         held_first.append(copy)
+    for part in range(3):
+        sent = ring(part)
+        place = mine[ORDERS[part][0]]
+        sent[0].wait_recv()
+        add_far(part, (place + 1) % 4, 0)
+        sent[4].start()
+        sent[1].wait_recv()
+        add_far(part, (place + 3) % 4, 1)
+        sent[5].start()
 
     gga_push.drain()
     l_push.landed()
@@ -622,13 +784,14 @@
 
     for part in range(3):
         held_first[part].wait()
-        for copy in copies(part, 0):
-            copy.wait_recv()
+        sent = ring(part)
+        for n in range(2, 6):
+            sent[n].wait_recv()
         src, dst = first[part], once[part]
 
         def add_first(n, carry, src=src, dst=dst):
             a, b = n // 4, n % 4
-            dst[a, b] = sum(src[s, a, b].astype(F32) for s in range(4)).astype(BF16)
+            dst[a, b] = sum(src[s, a, b].astype(F32) for s in range(3)).astype(BF16)
             return carry
 
         lax.fori_loop(0, 16, add_first, 0)
@@ -672,8 +835,16 @@
         return carry
 
     lax.fori_loop(0, 8, project_grad, 0)
+    give_gpw = pltpu.make_async_copy(gpw, gpw_to, out_s.at[1])
+    give_gpw.start()
     for c in range(2):
         gow_t[:, c * 512 : c * 512 + 512] = dot(glf[0], attf[c, :256, :]) + dot(glf[1], attf[c, 256:, :])
+    give_gow = pltpu.make_async_copy(gow_t, gow_to, out_s.at[2])
+    give_gow.start()
+    gain_part.wait()
+    gain_row[...] = (gain_out[0] + gain_out[1]).T[:1, :]
+    give_gain = pltpu.make_async_copy(gain_row, gain_to, out_s.at[3])
+    give_gain.start()
     lt_part.wait()
     qo_sib.wait()
     s_sib2.wait()
@@ -690,6 +861,10 @@
             ratio = ratio + prod[:, n * 128 : n * 128 + 128]
     coef = jnp.sum(ratio.T, axis=0, keepdims=True) * rinv_row / D_LAT
     gl_out[...] = back - coef * lt[...].astype(F32)
+    give_gl = pltpu.make_async_copy(gl_out, gl_to, out_s.at[4])
+    give_gl.start()
+    give_gqw = pltpu.make_async_copy(gqw, gqw_to, out_s.at[5])
+    give_gqw.start()
     sqa_push.drain()
     for gather in (latents, output, resampled):
         gather.drain()
@@ -703,36 +878,52 @@
         )
     give = over(19, fin.at[at16(1 - core), :], oth, sib)
     give.start()
-    gw[core] = fin[at16(core), :]
-    give.wait()
-    gw[1 - core] = oth[...]
-
-    gain_part.wait()
+
+    def put(plane, rows):
+        for n in range(2):
+            spot = pl.multiple_of(n * 1024 + plane * 512, 512)
+            gkw[:, pl.ds(spot, 512)] = rows[:13, n * 512 : n * 512 + 512]
+
+    put(core, fin[at16(core), :])
     w_sib.wait_send()
     q_sib.wait_send()
     for part in range(3):
-        for phase in range(3):
+        for copy in ring(part):
+            copy.wait_send()
+        for phase in (1, 2):
             for copy in copies(part, phase):
                 copy.wait_send()
+    give.wait()
+    put(1 - core, oth[...])
+    give_gkw = pltpu.make_async_copy(gkw, gkw_to, out_s.at[6])
+    give_gkw.start()
+    for copy in (give_llm, give_gpw, give_gow, give_gain, give_gl, give_gqw, give_gkw):
+        copy.wait()
 
 
 def sems(*counts):
     return [pltpu.SemaphoreType.DMA((n,)) for n in counts]
 
 
-def finish_kernel(llm_t, gl_t, gqw, gw, gow_t, gains, gpw, llm, gl, gqw_out, gkw, gow, gpw_out, gain, done):
-    copy = pltpu.make_async_copy(gpw, gpw_out, done)
-    copy.start()
-    llm[...] = turned(llm_t[...])
-    gl[...] = gl_t[...].T
-    gqw_out[...] = gqw[...]
-    gow[...] = gow_t[...].T
-    for c in range(2):
-        rows = gw[c]
-        gkw[:, c * 512 : c * 512 + 512] = rows[:13, :512]
-        gkw[:, 1024 + c * 512 : 1536 + c * 512] = rows[:13, 512:]
-    gain[...] = (gains[0] + gains[1]).T[0, :]
-    copy.wait()
+def finish_kernel(*refs):
+    got, done = refs[-2:]
+    n = len(refs) // 3
+    moves = []
+    for i in range(n):
+        src, dst, held = refs[i], refs[n + i], refs[2 * n + i]
+        if len(src.shape) > 2:
+            moves += [(src.at[m], held.at[m], dst.at[m]) for m in range(src.shape[0])]
+        else:
+            moves.append((src, held, dst))
+    loads = [pltpu.make_async_copy(src, held, got.at[m]) for m, (src, held, dst) in enumerate(moves)]
+    stores = [pltpu.make_async_copy(held, dst, done.at[m]) for m, (src, held, dst) in enumerate(moves)]
+    for copy in loads:
+        copy.start()
+    for load, store in zip(loads, stores):
+        load.wait()
+        store.start()
+    for copy in stores:
+        copy.wait()
 
 
 def local(
@@ -741,6 +932,21 @@
 ):
     widths = [w for _, w in WIDE]
     scratch = [
+        ((256, 1664), BF16),
+        ((13, 2048), BF16),
+        ((64, 1024), BF16),
+        ((64, 256), BF16),
+        ((64, 1024), BF16),
+        ((32, 2, 64, 128), BF16),
+        ((256, 128), BF16),
+        ((256, 128), BF16),
+        ((64, 256), F32),
+        ((64, 1024), F32),
+        ((13, 2048), F32),
+        ((64, 1024), F32),
+        ((4, 2, 512, 128), F32),
+        ((1, 128), F32),
+        ((2, 128, 128), F32),
         ((256, 128), F32),
         ((2, 2, 256, 384), BF16),
         ((2, 16, 1024), BF16),
@@ -791,63 +997,54 @@
         ((512, 1024), BF16),
         ((16, 256), BF16),
         ((2, 512, 512), BF16),
-        *[((4, 4, 4, 32, w), BF16) for w in widths],
+        *[((3, 4, 4, 32, w), BF16) for w in widths],
         *[((4, 4, 32, w), BF16) for w in widths],
         *[((4, 4, 32, w), BF16) for w in widths],
         *[((4, 32, w), BF16) for w in widths],
         *[((4, 32, w), BF16) for w in widths],
+        *[((2, 2, 4, 32, w), BF16) for w in widths],
         ((32, 1024), F32),
         ((16, 1024), F32),
     ]
-    llm_t, gain_out, gpw, gow_t, gqw, gl_out, gw = pl.pallas_call(
+    results = [
+        jax.ShapeDtypeStruct(shape, dtype)
+        for shape, dtype in (
+            ((256, 128), BF16),
+            ((64, 256), F32),
+            ((64, 1024), F32),
+            ((13, 2048), F32),
+            ((64, 1024), F32),
+            ((4, 2, 512, 128), F32),
+            ((1, 128), F32),
+        )
+    ]
+    made = pl.pallas_call(
         whole_kernel,
-        out_shape=[
-            jax.ShapeDtypeStruct(s, d)
-            for s, d in (
-                ((128, 256), BF16),
-                ((2, 128, 128), F32),
-                ((4, 2, 512, 128), F32),
-                ((64, 1024), F32),
-                ((64, 1024), F32),
-                ((64, 256), F32),
-                ((2, 16, 1024), F32),
-            )
-        ],
-        in_specs=[VMEM] * 11,
-        out_specs=[VMEM] * 7,
+        out_shape=results,
+        in_specs=[VMEM] * 3 + [ANY] * 7,
+        out_specs=[ANY] * 7,
         scratch_shapes=[pltpu.VMEM(s, d) for s, d in scratch]
-        + sems(27, 27, 27, 27, 27, 27, 27, 27, 32, 32, 64, 64, 64, 64, 64, 64, 32, 32)
-        + sems(32, 32, 32, 32, 64, 64, 64, 64, 64, 64, 27, 27, 20, 20, 12),
+        + sems(36, 36, 36, 36, 36, 36, 36, 36, 32, 32, 64, 64, 64, 64, 64, 64, 32, 32)
+        + sems(32, 32, 32, 32, 64, 64, 64, 64, 64, 64, 36, 36, 20, 20, 20, 7),
         compiler_params=pltpu.CompilerParams(
             has_side_effects=True, vmem_limit_bytes=62 << 20, collective_id=0
         ),
         name="whole",
     )(
-        tokens, keep_mask.reshape(1, 256), shard_counts.reshape(1, 1), latents, query_weight, keyval_weight,
-        output_weight.T, latents.T, project_weight.reshape(32, 2, 64, 128), input_grad,
-        llm_gain.reshape(1, 128),
+        keep_mask.reshape(1, 256), shard_counts.reshape(1, 1), llm_gain.reshape(1, 128), tokens,
+        keyval_weight, query_weight, latents.T, output_weight.T, project_weight.reshape(32, 2, 64, 128),
+        input_grad,
     )
-
-    return pl.pallas_call(
+    llm, gl, gqw, gkw, gow, gpw, gain = pl.pallas_call(
         finish_kernel,
-        out_shape=[
-            jax.ShapeDtypeStruct(shape, dtype)
-            for shape, dtype in (
-                ((256, 128), BF16),
-                ((256, 64), F32),
-                ((64, 1024), F32),
-                ((13, 2048), F32),
-                ((1024, 64), F32),
-                ((4096, 128), F32),
-                ((128,), F32),
-            )
-        ],
-        in_specs=[VMEM] * 6 + [ANY],
-        out_specs=[VMEM] * 5 + [ANY, VMEM],
-        scratch_shapes=[pltpu.SemaphoreType.DMA],
-        compiler_params=pltpu.CompilerParams(vmem_limit_bytes=32 << 20),
+        out_shape=results,
+        in_specs=[ANY] * 7,
+        out_specs=[ANY] * 7,
+        scratch_shapes=[pltpu.VMEM(r.shape, r.dtype) for r in results] + sems(10, 10),
+        compiler_params=pltpu.CompilerParams(vmem_limit_bytes=62 << 20),
         name="finish",
-    )(llm_t, gl_out, gqw, gw, gow_t, gain_out, gpw.reshape(4096, 128))
+    )(*made)
+    return (llm, gl.T, gqw, gkw, gow.T, gpw.reshape(4096, 128), gain.reshape(128))
 
 
 def solution(mesh):

time: 216 us -> 193 us (0.89)
  Pallas kernels: 205 us -> 191 us
  local copies, waits for them, and re-layouts: 10.1 us -> 0 us
    pallas_call x2, Pallas kernels: 205 us -> 191 us  [the longest x1 189 us: local(): pl.pallas_call(whole_kernel, out_shape=results, in_specs=[VMEM] * 3 + [AN...]
    unnamed x15 -> x0, local copies, waits for them, and re-layouts: 8.46 us -> none
where the time goes in v4:
time: 193 us
  Pallas kernels  191 us (99%)
    pallas_call x1, Pallas kernels, local(): pl.pallas_call(whole_kernel, out_shape=results, in_specs=[VMEM] * 3 + [AN...  189 us

profile of v4, /device:TPU:1, one launch (start us, length us, event | category | flops | bytes accessed | tf_op | source)
XLA Modules:
  0.0 192.9 jit_solution(18283089831235030071)
XLA Ops:
  1.3 188.6 %whole.1 = (bf16[256,128]{1,0:T(8,128)(2,1)}, f32[64,256]{1,0:T(8,128)}, f32[64,1024]{1,0:T(8,128)}, f32[13,2048]{1,0:T(8,128)}, f32[64,1024]{1,0:T(8,128)}, /*i...) custom-call(s32[1,256]{1,0:T(1,128)} %bitcast.14, s32[1,1]{1,0:T(1,128)} %bitcast.10.count, bf16[1,128]{1,0:T(2,128)(2,1)} %bitcast.15, ...), custom_call_target="tpu_custom_call" | custom-call | tf_op jit(solution)/shard_map/whole/pallas_call | solution.py:1021
  189.9 2.8 %finish.1 = (bf16[256,128]{1,0:T(8,128)(2,1)}, f32[64,256]{1,0:T(8,128)}, f32[64,1024]{1,0:T(8,128)}, f32[13,2048]{1,0:T(8,128)}, f32[64,1024]{1,0:T(8,128)}, /*...) custom-call(bf16[256,128]{1,0:T(8,128)(2,1)} %get-tuple-element.21.refs_0_, f32[64,256]{1,0:T(8,128)} %get-tuple-element.22.refs_1_, ...), custom_call_target="tpu_custom_call" | custom-call | tf_op jit(solution)/shard_map/finish/pallas_call | solution.py:1038

commit v5 on v4

--- a/solution.py
+++ b/solution.py
@@ -25,8 +25,10 @@
 
 ORDERS = ((2, 1, 0), (1, 0, 2), (0, 2, 1))
 WIDE = ((0, 384), (384, 384), (768, 256))
-COLUMNS_512 = ((0, 256), (256, 128), (384, 128))
+COLUMNS_512 = ((0, 128), (128, 256), (384, 128))
 ROWS_64 = ((0, 16), (16, 32), (48, 16))
+ROWS_OWN = ((0, 16), (16, 16), (32, 32))
+PAIR_ORDERS = ((2, 1, 0), (1, 0, 2))
 
 
 def row_dot(left, right):
@@ -97,14 +99,14 @@
 
 
 class Gather:
-    def __init__(self, place, ref, view, sends, recvs, whole=True):
+    def __init__(self, place, ref, view, sends, recvs, whole=True, orders=ORDERS, ring=True):
         self.place, self.ref, self.view, self.sends, self.recvs = place, ref, view, sends, recvs
-        self.whole = whole
+        self.whole, self.orders, self.ring = whole, orders, ring
 
     def copies(self, phase):
         pc = self.place
         mine = [pc.x, pc.y, pc.z]
-        for part, order in enumerate(ORDERS):
+        for part, order in enumerate(self.orders):
             held = list(mine)
             for axis in order[:phase]:
                 held[axis] = None
@@ -116,7 +118,7 @@
                     peer[0] = pc.g * 2 + 1 - pc.xl
                 else:
                     peer[order[phase]] = (peer[order[phase]] + step) % 4
-                yield self.push(block, (part * 2 + phase) * 3 + step - 1, peer)
+                yield self.push(block, (part * (2 if self.ring else 3) + phase) * 3 + step - 1, peer)
 
     def push(self, block, spot, peer):
         g, j = self.place.chip(*peer)
@@ -125,7 +127,7 @@
 
     def last(self, part):
         pc = self.place
-        order = ORDERS[part]
+        order = self.orders[part]
         axis = order[2]
         mine = [pc.x, pc.y, pc.z]
         base = 18 + part * 6
@@ -153,7 +155,7 @@
         ]
 
     def start(self, phase):
-        if phase < 2:
+        if phase < 2 or not self.ring:
             for copy in self.copies(phase):
                 copy.start()
             return
@@ -172,7 +174,7 @@
                 copies[5].start()
 
     def wait(self, phase):
-        if phase < 2:
+        if phase < 2 or not self.ring:
             for copy in self.copies(phase):
                 copy.wait_recv()
             return
@@ -182,10 +184,10 @@
                 copies[n].wait_recv()
 
     def drain(self):
-        for phase in range(2):
+        for phase in range(2 if self.ring else 3):
             for copy in self.copies(phase):
                 copy.wait_send()
-        for part in range(3):
+        for part in range(3 if self.ring else 0):
             for copy in self.last(part):
                 copy.wait_send()
 
@@ -217,12 +219,18 @@
     return ref.at[pick(x), pick(y), pick(z), :, pl.ds(*WIDE[part])]
 
 
-def view_output(core, ref, x, y, z, part):
-    return ref.at[pick(y), in_group(x), pick(z), core, :, pl.ds(*COLUMNS_512[part])]
-
-
-def view_own(core, ref, x, y, z, part):
-    return ref.at[pick(y), in_group(x), pick(z), core, pl.ds(*ROWS_64[part]), :]
+def view_output(ref, x, y, z, part):
+    return ref.at[pick(y), in_group(x), pick(z), :, pl.ds(*COLUMNS_512[part])]
+
+
+def view_own(ref, x, y, z, part):
+    return ref.at[pick(y), in_group(x), pick(z), pl.ds(*ROWS_OWN[part]), :]
+
+
+def view_rows(ref, x, y, z, part):
+    hi, lo = halves(x)
+    up, pair = halves(z)
+    return ref.at[hi, pick(y), lo, up, pair, :, pl.ds(part * 128, 128)]
 
 
 def view_latents(core, ref, x, y, z, part):
@@ -275,6 +283,10 @@
 
 def at256(n):
     return pl.ds(pl.multiple_of(n * 256, 256), 256)
+
+
+def heads_of(ref, pair, side):
+    return ref[:, :, :, :, pair, :, side * 128 : side * 128 + 128].reshape(512, 128)
 
 
 def turned(value, dtype=BF16):
@@ -286,9 +298,9 @@
     llm_to, gl_to, gqw_to, gkw_to, gow_to, gpw_to, gain_to,
     tokens, keyval_w, qw, lt, owt, pw, igrad, llm, gl_out, gqw, gkw, gow_t, gpw, gain_row, gain_out,
     val, qpart, wpl, gain,
-    wg, tokb, tok_t, valb, qx, qsum, recvq, qblk, qg, qo, owe, lown, ltp, la, kv, kv_t, fac, half, npk, recvn,
-    ablk, attf, pw_t, pwx, fold, foldx, sumx, sumo, sumr, gh_t, ghx, ghp, gap, recvg, glp, recvl,
-    lblk, glf, gblk, gg, ds, gqp, recvgq, gkv, sblk, sq, r1a, r1b, r1c, s1a, s1b, s1c,
+    wg, tokb, tok_t, valb, qx, qsum, recvq, qg, qo, owe, lown, ltp, la, kv, kv_t, fac, half, npk, recvn,
+    ablk, attf, pw_t, pwx, lat_s, lat_x, fold_s, fold_x, fold, foldx, sumx, sumo, sumr, gh_t, ghx, ghp, gap, recvg, glp, recvl,
+    lblk, glf, gblk, gg, ds, gqp, recvgq, gkv, sq, r1a, r1b, r1c, s1a, s1b, s1c,
     r2a, r2b, r2c, s2a, s2b, s2c, r3a, r3b, r3c, fara, farb, farc, fin, oth,
     w_s, w_r, ow_s, ow_r, lo_s, lo_r, l_s, l_r, q_s, q_r, qa_s, qa_r, n_s, n_r, a_s, a_r, t_s, t_r,
     g_s, g_r, gl_s, gl_r, gga_s, gga_r, gq_s, gq_r, sqa_s, sqa_r, p_s, p_r, x_s, x_r, loc, out_s,
@@ -327,13 +339,21 @@
     ]
     for copy in loads:
         copy.start()
-    for copy in loads:
-        copy.wait()
+    loads[0].wait()
 
     rows_f32 = jnp.concatenate([keyval_w[...].astype(F32), jnp.zeros((3, 2048), F32)], axis=0).astype(BF16)
     for c in range(2):
         wpl[c, :, :512] = rows_f32[:, c * 512 : c * 512 + 512]
         wpl[c, :, 512:] = rows_f32[:, 1024 + c * 512 : 1536 + c * 512]
+    w_own = pltpu.make_async_copy(wpl.at[core], wg.at[pc.x, pc.y, pc.z, at16(core)], loc.at[3])
+    w_own.start()
+    pl.semaphore_wait(barrier, CHIPS)
+
+    w_sib = over(0, wpl.at[1 - core], wg.at[pc.x, pc.y, pc.z, at16(core)], sib)
+    w_sib.start()
+
+    for copy in loads[1:]:
+        copy.wait()
     feats_f32 = lt[...].astype(F32)
     lat = feats_f32.T.astype(BF16)
     squares = jnp.sum(feats_f32 * feats_f32, axis=0, keepdims=True)
@@ -348,22 +368,37 @@
     val[...] = jnp.broadcast_to(jnp.where(kept, 1.0, 0.0), (128, 256)).T
     gain[...] = jnp.broadcast_to(gain_in[...].astype(F32), (256, 128)).T
 
+    q_sib = over(1, qpart.at[1 - core], qx, sib)
+    q_sib.start()
+    weight = Gather(pc, wg, view_weight, w_s, w_r)
+    output = Gather(pc, owe, view_output, ow_s, ow_r, False)
+    latents = Gather(pc, lown, view_own, lo_s, lo_r, False)
+    resampled = Gather(pc, la, functools.partial(view_latents, core), l_s, l_r)
+    w_own.wait()
+    w_sib.wait_recv()
+    weight.start(0)
     group_half = pl.ds(pl.multiple_of(pc.g * 512, 512), 512)
     local_copies = [
-        pltpu.make_async_copy(owt.at[:, group_half], owe.at[pc.y, pc.xl, pc.z, core], loc.at[0]),
-        pltpu.make_async_copy(lt, lown.at[pc.y, pc.xl, pc.z, core], loc.at[1]),
+        pltpu.make_async_copy(owt.at[:, group_half], owe.at[pc.y, pc.xl, pc.z], loc.at[0]),
+        pltpu.make_async_copy(lt, lown.at[pc.y, pc.xl, pc.z], loc.at[1]),
         pltpu.make_async_copy(lt, ltp.at[pc.g], loc.at[11]),
         pltpu.make_async_copy(val, valb.at[core], loc.at[2]),
-        pltpu.make_async_copy(wpl.at[core], wg.at[pc.x, pc.y, pc.z, at16(core)], loc.at[3]),
     ]
     for copy in local_copies:
         copy.start()
-    pl.semaphore_wait(barrier, CHIPS)
-
-    w_sib = over(0, wpl.at[1 - core], wg.at[pc.x, pc.y, pc.z, at16(core)], sib)
-    w_sib.start()
-    q_sib = over(1, qpart.at[1 - core], qx, sib)
-    q_sib.start()
+
+    q_sib.wait_recv()
+    for p in range(2):
+        qsum[p] = (qpart[core, p].astype(F32) + qx[p].astype(F32)).astype(BF16)
+
+    def q_copy(k):
+        j = pc.group_peer(k)
+        return remote(
+            qsum.at[j % 2, at16(j // 2), :], recvq.at[k], q_s.at[k], q_r.at[k], chip_device(pc.g, j)
+        )
+
+    q_push = Pushes(GROUP, q_copy)
+    q_push.start()
 
     for block in range(16):
         x, y = block // 4, block % 4
@@ -377,75 +412,60 @@
         place = jnp.where(hit, 1.0, 0.0).astype(BF16)
         tokb[core, :, pl.ds(block * 128, 128)] = dot(tokens[:, pl.ds(base, width)], place).astype(BF16)
 
-    weight = Gather(pc, wg, view_weight, w_s, w_r)
-    output = Gather(pc, owe, functools.partial(view_output, core), ow_s, ow_r, False)
-    latents = Gather(pc, lown, functools.partial(view_own, core), lo_s, lo_r, False)
-    resampled = Gather(pc, la, functools.partial(view_latents, core), l_s, l_r)
+    t_sib = over(2, tokb.at[core], tokb.at[core], sib)
+    t_sib.start()
     for copy in local_copies:
         copy.wait()
-    w_sib.wait_recv()
-    weight.start(0)
-
-    q_sib.wait_recv()
-    for p in range(2):
-        qsum[p] = (qpart[core, p].astype(F32) + qx[p].astype(F32)).astype(BF16)
-
-    def q_copy(k):
-        j = pc.group_peer(k)
-        return remote(
-            qsum.at[j % 2, at16(j // 2), :], recvq.at[k], q_s.at[k], q_r.at[k], chip_device(pc.g, j)
-        )
-
-    q_push = Pushes(GROUP, q_copy)
-    q_push.start()
-    t_sib = over(2, tokb.at[core], tokb.at[core], sib)
-    t_sib.start()
+    latents.start(0)
+    output.start(0)
     v_sib = over(3, val, valb.at[core], sib)
     v_sib.start()
+    pw_sib = over(4, pw.at[:, 1 - core], pwx, sib)
+    pw_sib.start()
     weight.wait(0)
     weight.start(1)
+    for y in range(4):
+        pw_t[0, :, pl.ds(y * 512, 512)] = turned(pw[pl.ds(y * 8, 8), core].reshape(512, 128))
+    latents.wait(0)
+    latents.start(1)
+    output.wait(0)
+    output.start(1)
+    weight.wait(1)
+    weight.start(2)
     q_push.landed()
     total = total_slots(qsum[pair, own_rows, :], recvq, GROUP)
     rinv = lax.rsqrt(total[:, 256:] / D_LAT + 1e-06)
     proj = total[:, :256]
-    qblk[...] = (proj * rinv[:, :1]).astype(BF16)
-    q_spot = qg.at[all_rows, at256(pair)]
-    qa_push = Pushes(
-        CHIPS,
-        lambda k: remote(qblk, q_spot, qa_s.at[k], qa_r.at[k], chip_device(*pc.plane_peer(k))),
-    )
-    qa_push.start()
-    q_own = pltpu.make_async_copy(qblk, q_spot, loc.at[4])
-    q_own.start()
+    q_spot = (pc.g, pc.y, pc.xl, pc.z // 2, pair)
+    qg[q_spot] = (proj * rinv[:, :1]).astype(BF16)
+    queries = Gather(pc, qg, view_rows, qa_s, qa_r, True, PAIR_ORDERS, False)
+    queries.start(0)
     t_sib.wait()
     v_sib.wait()
-    weight.wait(1)
-    weight.start(2)
-    pw_sib = over(4, pw.at[:, 1 - core], pwx, sib)
-    pw_sib.start()
-    lt_part = over(16, lt, ltp.at[pc.g], partner)
-    lt_part.start()
-
-    weight.relay()
-
-    for y in range(4):
-        pw_t[:, pl.ds(y * 1024, 1024)] = turned(pw[pl.ds(y * 8, 8)].reshape(1024, 128))
-    for block in range(4):
+    for block in range(2):
         tok_t[pl.ds(block * 512, 512), :] = turned(
             tokb[:, :, pl.ds(block * 512, 512)].reshape(512, 512)
         )
+    weight.relay()
+    queries.wait(0)
+    queries.start(1)
+    queries.wait(1)
+    queries.start(2)
+    for block in range(2, 4):
+        tok_t[pl.ds(block * 512, 512), :] = turned(
+            tokb[:, :, pl.ds(block * 512, 512)].reshape(512, 512)
+        )
+    pw_sib.wait()
+    for y in range(4):
+        pw_t[1, :, pl.ds(y * 512, 512)] = turned(pwx[pl.ds(y * 8, 8)].reshape(512, 128))
+    lt_part = over(16, lt, ltp.at[pc.g], partner)
+    lt_part.start()
     q_push.drain()
-    q_own.wait()
-    qa_push.landed()
-    qo_sib = over(17, qg.at[at256(pc.g), :], qo, sib)
-    qo_sib.start()
-    latents.start(0)
-    output.start(0)
     weight.wait(2)
-    latents.wait(0)
-    latents.start(1)
-    output.wait(0)
-    output.start(1)
+    latents.wait(1)
+    latents.start(2)
+    output.wait(1)
+    output.start(2)
 
     tok = tokb[...].reshape(512, 2048)
 
@@ -457,6 +477,9 @@
     lax.fori_loop(0, 4, project, 0)
     for n in range(4):
         kv_t[pl.ds(n * 256, 256), :] = turned(kv[:, n * 256 : n * 256 + 256])
+    queries.wait(2)
+    qo_sib = over(17, qg.at[pc.g], qo, sib)
+    qo_sib.start()
 
     def n_copy(k):
         g, j = pc.plane_peer(k)
@@ -471,7 +494,7 @@
         for side in range(2):
             head = p * 2 + side
             columns = pl.ds(head * 128, 128)
-            query = qg[:, columns]
+            query = heads_of(qg, p, side)
             total = jnp.zeros((1, 512), F32)
             for chunk in range(4):
                 slots = pl.ds(chunk * 128, 128)
@@ -487,15 +510,11 @@
         npk[p] = jnp.concatenate(packed + sums, axis=0).T.astype(BF16)
         n_push.start_pair(p)
         if p == 0:
-            latents.wait(1)
-            latents.start(2)
-            output.wait(1)
-            output.start(2)
-
-    latents.relay()
-    output.relay()
+            latents.relay()
+            output.relay()
+
     weight.drain()
-    qa_push.drain()
+    queries.drain()
     n_push.landed()
     total = total_slots(npk[pair, all_rows, :], recvn, CHIPS)
     whole = jnp.concatenate(
@@ -514,25 +533,30 @@
 
     n_push.drain()
     latents.wait(2)
-    lown_sib = over(5, lown.at[:, :, :, core], lown.at[:, :, :, core], sib)
-    lown_sib.start()
+    feats = lown[...].reshape(2048, 256)
+    lat_s[:128, :] = dot(pw_t[1], feats)
+    squares = jnp.zeros((1, 256), F32)
+    for y in range(4):
+        block = lown[y].reshape(512, 256).astype(F32)
+        squares = squares + jnp.sum(block * block, axis=0, keepdims=True)
+    lat_s[128:, :] = jnp.broadcast_to(squares, (8, 256))
+    lat_sib = over(5, lat_s, lat_x, sib)
+    lat_sib.start()
+    hidden = dot(pw_t[0], feats)
     output.wait(2)
-    owe_sib = over(6, owe.at[:, :, :, core], owe.at[:, :, :, core], sib)
-    owe_sib.start()
-    lown_sib.wait()
-    owe_sib.wait()
-
-    for n in range(2):
-        folded = dot(pw_t[...], owe[:, :, :, :, :, n * 256 : n * 256 + 256].reshape(4096, 256))
-        fold[:, at256(pc.g * 2 + n)] = folded.astype(BF16)
+
+    rows = owe[...].reshape(2048, 512)
+    fold_s[...] = dot(pw_t[1], rows).astype(BF16)
+    fold_sib = over(6, fold_s, fold_x, sib)
+    fold_sib.start()
+    folded = dot(pw_t[0], rows)
+    fold_sib.wait()
+    fold[:, group_half] = (folded + fold_x[...].astype(F32)).astype(BF16)
     f_part = over(18, fold.at[:, group_half], fold.at[:, group_half], partner)
     f_part.start()
-    hidden = dot(pw_t[...], lown[...].reshape(4096, 256))
-    squares = jnp.zeros((1, 256), F32)
-    for y in range(4):
-        feats = lown[y].reshape(1024, 256).astype(F32)
-        squares = squares + jnp.sum(feats * feats, axis=0, keepdims=True)
-    rinv_row = lax.rsqrt(squares / D_LAT + 1e-06)
+    lat_sib.wait()
+    hidden = hidden + lat_x[:128, :]
+    rinv_row = lax.rsqrt((squares + lat_x[128:129, :]) / D_LAT + 1e-06)
     a_own.wait()
     a_push.landed()
     a_sib = over(7, attf.at[core], attf.at[core], sib)
@@ -567,6 +591,8 @@
     lat_out = lt[...].astype(F32) + col_dot(owt[:, :512], attf[0, group_rows, :])
     la[pc.g, pc.y, pc.xl, pc.z, core] = (lat_out + col_dot(owt[:, 512:], attf[1, group_rows, :])).astype(BF16)
     resampled.start(0)
+    resampled.wait(0)
+    resampled.start(1)
     t_push.landed()
     total = total_slots(sumx[1], sumr, GROUP)
     square_row = jnp.concatenate([total[0:1], total[1:2]], axis=1)
@@ -603,10 +629,19 @@
     g_push = Pushes(GROUP, g_copy)
     g_push.start()
 
-    resampled.wait(0)
-    resampled.start(1)
-    for push in (a_push, t_push):
-        push.drain()
+    resampled.wait(1)
+    resampled.start(2)
+
+    for n in range(4):
+        part = dot(pw[pl.ds(n * 8, 8), core].reshape(512, 128), gh_t[...])
+        part = part + dot(pwx[pl.ds(n * 8, 8)].reshape(512, 128), ghx[...])
+        glp[pl.ds(n * 8, 8)] = part.astype(BF16).reshape(8, 64, 256)
+
+    def l_copy(k):
+        j = pc.group_peer(k)
+        return remote(glp.at[j], recvl.at[k], gl_s.at[k], gl_r.at[k], chip_device(pc.g, j))
+
+    l_push = Pushes(GROUP, l_copy)
     g_push.landed()
     grad = total_slots(gap[own_rows, at256(pair)], recvg, GROUP).astype(BF16).astype(F32)
     gblk[...] = (grad / whole).astype(BF16)
@@ -616,26 +651,14 @@
         lambda k: remote(gblk, g_spot, gga_s.at[k], gga_r.at[k], chip_device(*pc.plane_peer(k))),
     )
     gga_push.start()
+    l_push.start()
     g_own = pltpu.make_async_copy(gblk, g_spot, loc.at[6])
     g_own.start()
-
-    pw_sib.wait()
-    for n in range(4):
-        part = dot(pw[pl.ds(n * 8, 8), core].reshape(512, 128), gh_t[...])
-        part = part + dot(pwx[pl.ds(n * 8, 8)].reshape(512, 128), ghx[...])
-        glp[pl.ds(n * 8, 8)] = part.astype(BF16).reshape(8, 64, 256)
-
-    def l_copy(k):
-        j = pc.group_peer(k)
-        return remote(glp.at[j], recvl.at[k], gl_s.at[k], gl_r.at[k], chip_device(pc.g, j))
-
-    l_push = Pushes(GROUP, l_copy)
-    resampled.wait(1)
-    resampled.start(2)
-    g_push.drain()
+    resampled.relay()
+    for push in (a_push, t_push, g_push):
+        push.drain()
     g_own.wait()
     gga_push.landed()
-    l_push.start()
 
     def gq_copy(k):
         g, j = pc.plane_peer(k)
@@ -661,10 +684,9 @@
             parts.append(dot(kv_t[pl.ds(head * 128, 128), :], ds[head]))
         gqp[:, p * 256 : p * 256 + 256] = jnp.concatenate(parts, axis=0).T.astype(BF16)
         gq_push.start_pair(p)
-    resampled.relay()
     for head in range(4):
         columns = pl.ds(head * 128, 128)
-        gkv[:, columns] = dot(ds[head], qg[:, columns]).astype(BF16)
+        gkv[:, columns] = dot(ds[head], heads_of(qg, head // 2, head % 2)).astype(BF16)
         gkv[:, 512 + head * 128 : 640 + head * 128] = dot(half[head], gg[:, columns]).astype(BF16)
 
     first, once = (r1a, r1b, r1c), (s1a, s1b, s1c)
@@ -738,6 +760,11 @@
                 p_s.at[spot], p_r.at[spot], chip_device(*pc.chip(*peer)),
             )
 
+    gq_push.landed()
+    grad = total_slots(gqp[all_rows, at256(pair)], recvgq, CHIPS)
+    sq[core, q_spot[0], q_spot[1], q_spot[2], q_spot[3], pair] = (grad * rinv[:, :1]).astype(BF16)
+    scaled = Gather(pc, sq.at[core], view_rows, sqa_s, sqa_r, True, PAIR_ORDERS, False)
+    scaled.start(0)
     for part in range(3):
         sent = ring(part)
         for n in range(2):
@@ -750,6 +777,16 @@
         copy = pltpu.make_async_copy(slab(part, mine[ORDERS[part][0]]), first[part].at[0], loc.at[7 + part])
         copy.start()
         held_first.append(copy)
+    l_push.landed()
+    lblk[...] = total_slots(glp[pc.j], recvl, GROUP).astype(BF16)
+    glf[pc.g] = lblk[...]
+    l_part = over(13, lblk, glf.at[pc.g], partner)
+    l_part.start()
+    resampled.wait(2)
+    la_sib = over(14, la.at[:, :, :, :, core], la.at[:, :, :, :, core], sib)
+    la_sib.start()
+    scaled.wait(0)
+    scaled.start(1)
     for part in range(3):
         sent = ring(part)
         place = mine[ORDERS[part][0]]
@@ -759,28 +796,23 @@
         sent[1].wait_recv()
         add_far(part, (place + 3) % 4, 1)
         sent[5].start()
-
+    scaled.wait(1)
+    scaled.start(2)
+    h_part.wait()
+    la_sib.wait()
+    gh_both = [turned(ghp[n]) for n in range(2)]
+
+    def project_grad(n, carry):
+        y, xl = n // 2, n % 2
+        gpw[y, xl] = dot(la[0, y, xl].reshape(512, 256), gh_both[0]) + dot(
+            la[1, y, xl].reshape(512, 256), gh_both[1]
+        )
+        return carry
+
+    lax.fori_loop(0, 8, project_grad, 0)
+    give_gpw = pltpu.make_async_copy(gpw, gpw_to, out_s.at[1])
+    give_gpw.start()
     gga_push.drain()
-    l_push.landed()
-    lblk[...] = total_slots(glp[pc.j], recvl, GROUP).astype(BF16)
-    glf[pc.g] = lblk[...]
-    l_part = over(13, lblk, glf.at[pc.g], partner)
-    l_part.start()
-    gq_push.landed()
-    grad = total_slots(gqp[all_rows, at256(pair)], recvgq, CHIPS)
-    sblk[...] = (grad * rinv[:, :1]).astype(BF16)
-    s_spot = sq.at[core, all_rows, at256(pair)]
-    sqa_push = Pushes(
-        CHIPS,
-        lambda k: remote(sblk, s_spot, sqa_s.at[k], sqa_r.at[k], chip_device(*pc.plane_peer(k))),
-    )
-    sqa_push.start()
-    s_own = pltpu.make_async_copy(sblk, s_spot, loc.at[10])
-    s_own.start()
-
-    resampled.wait(2)
-    la_sib = over(14, la.at[:, :, :, :, core], la.at[:, :, :, :, core], sib)
-    la_sib.start()
 
     for part in range(3):
         held_first[part].wait()
@@ -798,45 +830,12 @@
         for copy in copies(part, 1):
             copy.start()
 
+    scaled.wait(2)
+    s_sib2 = over(15, sq.at[core], sq.at[core], sib)
+    s_sib2.start()
     l_part.wait()
     l_push.drain()
     gq_push.drain()
-    s_own.wait()
-    sqa_push.landed()
-    s_sib2 = over(15, sq.at[core], sq.at[core], sib)
-    s_sib2.start()
-
-    for part in range(3):
-        for copy in copies(part, 1):
-            copy.wait_recv()
-        src, dst, held = second[part], twice[part], once[part]
-        left = [axis for axis in range(3) if axis != ORDERS[part][0]]
-        leading = left[0] == ORDERS[part][1]
-        here = mine[ORDERS[part][1]]
-
-        def add_second(n, carry, src=src, dst=dst, held=held, leading=leading, here=here):
-            base = held[here, n] if leading else held[n, here]
-            dst[n] = (base.astype(F32) + sum(src[s, n].astype(F32) for s in range(1, 4))).astype(BF16)
-            return carry
-
-        lax.fori_loop(0, 4, add_second, 0)
-        for copy in copies(part, 2):
-            copy.start()
-
-    h_part.wait()
-    la_sib.wait()
-    gh_both = [turned(ghp[n]) for n in range(2)]
-
-    def project_grad(n, carry):
-        y, xl = n // 2, n % 2
-        gpw[y, xl] = dot(la[0, y, xl].reshape(512, 256), gh_both[0]) + dot(
-            la[1, y, xl].reshape(512, 256), gh_both[1]
-        )
-        return carry
-
-    lax.fori_loop(0, 8, project_grad, 0)
-    give_gpw = pltpu.make_async_copy(gpw, gpw_to, out_s.at[1])
-    give_gpw.start()
     for c in range(2):
         gow_t[:, c * 512 : c * 512 + 512] = dot(glf[0], attf[c, :256, :]) + dot(glf[1], attf[c, 256:, :])
     give_gow = pltpu.make_async_copy(gow_t, gow_to, out_s.at[2])
@@ -845,28 +844,49 @@
     gain_row[...] = (gain_out[0] + gain_out[1]).T[:1, :]
     give_gain = pltpu.make_async_copy(gain_row, gain_to, out_s.at[3])
     give_gain.start()
+
+    for part in range(3):
+        for copy in copies(part, 1):
+            copy.wait_recv()
+        src, dst, held = second[part], twice[part], once[part]
+        left = [axis for axis in range(3) if axis != ORDERS[part][0]]
+        leading = left[0] == ORDERS[part][1]
+        here = mine[ORDERS[part][1]]
+
+        def add_second(n, carry, src=src, dst=dst, held=held, leading=leading, here=here):
+            base = held[here, n] if leading else held[n, here]
+            dst[n] = (base.astype(F32) + sum(src[s, n].astype(F32) for s in range(1, 4))).astype(BF16)
+            return carry
+
+        lax.fori_loop(0, 4, add_second, 0)
+        for copy in copies(part, 2):
+            copy.start()
+
     lt_part.wait()
     qo_sib.wait()
     s_sib2.wait()
     back = glf[pc.g].astype(F32)
     ratio = jnp.zeros((256, 128), F32)
     for c in range(2):
-        columns = pl.ds(c * 512, 512)
-        gqw[:, columns] = dot(ltp[0], sq[c, :256, :]) + dot(ltp[1], sq[c, 256:, :])
-        block = sq[c, group_rows, :]
-        back = back + col_dot(qw[:, columns], block)
-    for block, query in ((sq[core, group_rows, :], qg[group_rows, :]), (sq[1 - core, group_rows, :], qo[...])):
-        prod = block.astype(F32) * query.astype(F32)
-        for n in range(4):
-            ratio = ratio + prod[:, n * 128 : n * 128 + 128]
+        for p in range(2):
+            columns = pl.ds(c * 512 + p * 256, 256)
+            blocks = [sq[c, n, :, :, :, p].reshape(256, 256) for n in range(2)]
+            gqw[:, columns] = dot(ltp[0], blocks[0]) + dot(ltp[1], blocks[1])
+            back = back + col_dot(qw[:, columns], sq[c, pc.g, :, :, :, p].reshape(256, 256))
+    for p in range(2):
+        for block, query in (
+            (sq[core, pc.g, :, :, :, p], qg[pc.g, :, :, :, p]),
+            (sq[1 - core, pc.g, :, :, :, p], qo[:, :, :, p]),
+        ):
+            prod = block.astype(F32).reshape(256, 256) * query.astype(F32).reshape(256, 256)
+            ratio = ratio + prod[:, :128] + prod[:, 128:]
     coef = jnp.sum(ratio.T, axis=0, keepdims=True) * rinv_row / D_LAT
     gl_out[...] = back - coef * lt[...].astype(F32)
     give_gl = pltpu.make_async_copy(gl_out, gl_to, out_s.at[4])
     give_gl.start()
     give_gqw = pltpu.make_async_copy(gqw, gqw_to, out_s.at[5])
     give_gqw.start()
-    sqa_push.drain()
-    for gather in (latents, output, resampled):
+    for gather in (latents, output, resampled, scaled):
         gather.drain()
 
     for part in range(3):
@@ -958,11 +978,10 @@
         ((2, 256, 384), BF16),
         ((2, 256, 384), BF16),
         ((32, 16, 384), BF16),
-        ((16, 256), BF16),
-        ((512, 512), BF16),
-        ((256, 512), BF16),
-        ((4, 2, 4, 2, 64, 512), BF16),
-        ((4, 2, 4, 2, 64, 256), BF16),
+        ((2, 4, 2, 2, 2, 16, 256), BF16),
+        ((4, 2, 2, 2, 16, 256), BF16),
+        ((4, 2, 4, 64, 512), BF16),
+        ((4, 2, 4, 64, 256), BF16),
         ((2, 64, 256), BF16),
         ((2, 4, 2, 4, 2, 64, 256), BF16),
         ((512, 1024), BF16),
@@ -973,8 +992,12 @@
         ((64, 16, 384), BF16),
         ((16, 256), BF16),
         ((2, 512, 512), BF16),
-        ((128, 4096), BF16),
+        ((2, 128, 2048), BF16),
         ((32, 64, 128), BF16),
+        ((136, 256), F32),
+        ((136, 256), F32),
+        ((128, 512), BF16),
+        ((128, 512), BF16),
         ((128, 1024), BF16),
         ((128, 512), BF16),
         ((2, 8, 128), F32),
@@ -995,8 +1018,7 @@
         ((512, 512), BF16),
         ((64, 16, 256), BF16),
         ((512, 1024), BF16),
-        ((16, 256), BF16),
-        ((2, 512, 512), BF16),
+        ((2, 2, 4, 2, 2, 2, 16, 256), BF16),
         *[((3, 4, 4, 32, w), BF16) for w in widths],
         *[((4, 4, 32, w), BF16) for w in widths],
         *[((4, 4, 32, w), BF16) for w in widths],
@@ -1024,8 +1046,8 @@
         in_specs=[VMEM] * 3 + [ANY] * 7,
         out_specs=[ANY] * 7,
         scratch_shapes=[pltpu.VMEM(s, d) for s, d in scratch]
-        + sems(36, 36, 36, 36, 36, 36, 36, 36, 32, 32, 64, 64, 64, 64, 64, 64, 32, 32)
-        + sems(32, 32, 32, 32, 64, 64, 64, 64, 64, 64, 36, 36, 20, 20, 20, 7),
+        + sems(36, 36, 36, 36, 36, 36, 36, 36, 32, 32, 18, 18, 64, 64, 64, 64, 32, 32)
+        + sems(32, 32, 32, 32, 64, 64, 64, 64, 18, 18, 36, 36, 20, 20, 20, 7),
         compiler_params=pltpu.CompilerParams(
             has_side_effects=True, vmem_limit_bytes=62 << 20, collective_id=0
         ),

time: 193 us -> 178 us (0.922)
  Pallas kernels: 191 us -> 176 us
    pallas_call x1, Pallas kernels: 189 us -> 174 us  [local(): pl.pallas_call(whole_kernel, out_shape=results, in_specs=[VMEM] * 3 + [AN...]
where the time goes in v5:
time: 178 us
  Pallas kernels  176 us (99%)
    pallas_call x1, Pallas kernels, local(): pl.pallas_call(whole_kernel, out_shape=results, in_specs=[VMEM] * 3 + [AN...  174 us

profile of v5, /device:TPU:1, one launch (start us, length us, event | category | flops | bytes accessed | tf_op | source)
XLA Modules:
  0.0 177.9 jit_solution(14458282706355940665)
XLA Ops:
  1.3 173.6 %whole.1 = (bf16[256,128]{1,0:T(8,128)(2,1)}, f32[64,256]{1,0:T(8,128)}, f32[64,1024]{1,0:T(8,128)}, f32[13,2048]{1,0:T(8,128)}, f32[64,1024]{1,0:T(8,128)}, /*i...) custom-call(s32[1,256]{1,0:T(1,128)} %bitcast.14, s32[1,1]{1,0:T(1,128)} %bitcast.10.count, bf16[1,128]{1,0:T(2,128)(2,1)} %bitcast.15, ...), custom_call_target="tpu_custom_call" | custom-call | tf_op jit(solution)/shard_map/whole/pallas_call | solution.py:1043
  174.9 2.8 %finish.1 = (bf16[256,128]{1,0:T(8,128)(2,1)}, f32[64,256]{1,0:T(8,128)}, f32[64,1024]{1,0:T(8,128)}, f32[13,2048]{1,0:T(8,128)}, f32[64,1024]{1,0:T(8,128)}, /*...) custom-call(bf16[256,128]{1,0:T(8,128)(2,1)} %get-tuple-element.21.refs_0_, f32[64,256]{1,0:T(8,128)} %get-tuple-element.22.refs_1_, ...), custom_call_target="tpu_custom_call" | custom-call | tf_op jit(solution)/shard_map/finish/pallas_call | solution.py:1060

commit v6 on v5

--- a/solution.py
+++ b/solution.py
@@ -25,6 +25,9 @@
 
 ORDERS = ((2, 1, 0), (1, 0, 2), (0, 2, 1))
 WIDE = ((0, 384), (384, 384), (768, 256))
+SPLIT = ((0, 256), (256, 128), (384, 128), (512, 128), (640, 128), (768, 256))
+SPLIT_ORDERS = ORDERS + ORDERS
+KEYS, VALUES = (0, 1, 2), (3, 4, 5)
 COLUMNS_512 = ((0, 128), (128, 256), (384, 128))
 ROWS_64 = ((0, 16), (16, 32), (48, 16))
 ROWS_OWN = ((0, 16), (16, 16), (32, 32))
@@ -103,10 +106,11 @@
         self.place, self.ref, self.view, self.sends, self.recvs = place, ref, view, sends, recvs
         self.whole, self.orders, self.ring = whole, orders, ring
 
-    def copies(self, phase):
+    def copies(self, phase, parts=None):
         pc = self.place
         mine = [pc.x, pc.y, pc.z]
-        for part, order in enumerate(self.orders):
+        for part in self.parts(parts):
+            order = self.orders[part]
             held = list(mine)
             for axis in order[:phase]:
                 held[axis] = None
@@ -130,7 +134,7 @@
         order = self.orders[part]
         axis = order[2]
         mine = [pc.x, pc.y, pc.z]
-        base = 18 + part * 6
+        base = (len(self.orders) + part) * 6
         if axis == 0 and not self.whole:
             held = [mine[0], None, None]
             block = self.view(self.ref, *held, part)
@@ -154,18 +158,21 @@
             self.push(at(up, 1), base + 5, below),
         ]
 
-    def start(self, phase):
+    def parts(self, some):
+        return range(len(self.orders)) if some is None else some
+
+    def start(self, phase, parts=None):
         if phase < 2 or not self.ring:
-            for copy in self.copies(phase):
+            for copy in self.copies(phase, parts):
                 copy.start()
             return
-        for part in range(3):
+        for part in self.parts(parts):
             copies = self.last(part)
             for n in (0,) if len(copies) == 1 else (0, 2, 1, 3):
                 copies[n].start()
 
-    def relay(self):
-        for part in range(3):
+    def relay(self, parts=None):
+        for part in self.parts(parts):
             copies = self.last(part)
             if len(copies) > 1:
                 copies[0].wait_recv()
@@ -173,12 +180,12 @@
                 copies[2].wait_recv()
                 copies[5].start()
 
-    def wait(self, phase):
+    def wait(self, phase, parts=None):
         if phase < 2 or not self.ring:
-            for copy in self.copies(phase):
+            for copy in self.copies(phase, parts):
                 copy.wait_recv()
             return
-        for part in range(3):
+        for part in self.parts(parts):
             copies = self.last(part)
             for n in (0,) if len(copies) == 1 else (1, 3, 4, 5):
                 copies[n].wait_recv()
@@ -187,7 +194,7 @@
         for phase in range(2 if self.ring else 3):
             for copy in self.copies(phase):
                 copy.wait_send()
-        for part in range(3 if self.ring else 0):
+        for part in self.parts(None) if self.ring else ():
             for copy in self.last(part):
                 copy.wait_send()
 
@@ -216,7 +223,7 @@
 
 
 def view_weight(ref, x, y, z, part):
-    return ref.at[pick(x), pick(y), pick(z), :, pl.ds(*WIDE[part])]
+    return ref.at[pick(x), pick(y), pick(z), :, pl.ds(*SPLIT[part])]
 
 
 def view_output(ref, x, y, z, part):
@@ -299,7 +306,7 @@
     tokens, keyval_w, qw, lt, owt, pw, igrad, llm, gl_out, gqw, gkw, gow_t, gpw, gain_row, gain_out,
     val, qpart, wpl, gain,
     wg, tokb, tok_t, valb, qx, qsum, recvq, qg, qo, owe, lown, ltp, la, kv, kv_t, fac, half, npk, recvn,
-    ablk, attf, pw_t, pwx, lat_s, lat_x, fold_s, fold_x, fold, foldx, sumx, sumo, sumr, gh_t, ghx, ghp, gap, recvg, glp, recvl,
+    ablk, attf, pw_t, pwx, lat_s, lat_x, fold_s, fold_x, fold, foldx, sumx, sumo, sumr, gh_t, ghx, ghp, gap, recvg, glp, u1a, u1b, v1a, v1b, u2, v2, u3,
     lblk, glf, gblk, gg, ds, gqp, recvgq, gkv, sq, r1a, r1b, r1c, s1a, s1b, s1c,
     r2a, r2b, r2c, s2a, s2b, s2c, r3a, r3b, r3c, fara, farb, farc, fin, oth,
     w_s, w_r, ow_s, ow_r, lo_s, lo_r, l_s, l_r, q_s, q_r, qa_s, qa_r, n_s, n_r, a_s, a_r, t_s, t_r,
@@ -347,11 +354,6 @@
         wpl[c, :, 512:] = rows_f32[:, 1024 + c * 512 : 1536 + c * 512]
     w_own = pltpu.make_async_copy(wpl.at[core], wg.at[pc.x, pc.y, pc.z, at16(core)], loc.at[3])
     w_own.start()
-    pl.semaphore_wait(barrier, CHIPS)
-
-    w_sib = over(0, wpl.at[1 - core], wg.at[pc.x, pc.y, pc.z, at16(core)], sib)
-    w_sib.start()
-
     for copy in loads[1:]:
         copy.wait()
     feats_f32 = lt[...].astype(F32)
@@ -368,9 +370,14 @@
     val[...] = jnp.broadcast_to(jnp.where(kept, 1.0, 0.0), (128, 256)).T
     gain[...] = jnp.broadcast_to(gain_in[...].astype(F32), (256, 128)).T
 
+    pl.semaphore_wait(barrier, CHIPS)
+
+    w_sib = over(0, wpl.at[1 - core], wg.at[pc.x, pc.y, pc.z, at16(core)], sib)
+    w_sib.start()
+
     q_sib = over(1, qpart.at[1 - core], qx, sib)
     q_sib.start()
-    weight = Gather(pc, wg, view_weight, w_s, w_r)
+    weight = Gather(pc, wg, view_weight, w_s, w_r, True, SPLIT_ORDERS)
     output = Gather(pc, owe, view_output, ow_s, ow_r, False)
     latents = Gather(pc, lown, view_own, lo_s, lo_r, False)
     resampled = Gather(pc, la, functools.partial(view_latents, core), l_s, l_r)
@@ -430,8 +437,6 @@
     latents.start(1)
     output.wait(0)
     output.start(1)
-    weight.wait(1)
-    weight.start(2)
     q_push.landed()
     total = total_slots(qsum[pair, own_rows, :], recvq, GROUP)
     rinv = lax.rsqrt(total[:, 256:] / D_LAT + 1e-06)
@@ -440,17 +445,20 @@
     qg[q_spot] = (proj * rinv[:, :1]).astype(BF16)
     queries = Gather(pc, qg, view_rows, qa_s, qa_r, True, PAIR_ORDERS, False)
     queries.start(0)
+    weight.wait(1)
+    weight.start(2, KEYS)
+    queries.wait(0)
+    queries.start(1)
+    weight.start(2, VALUES)
+    queries.wait(1)
+    queries.start(2)
     t_sib.wait()
     v_sib.wait()
     for block in range(2):
         tok_t[pl.ds(block * 512, 512), :] = turned(
             tokb[:, :, pl.ds(block * 512, 512)].reshape(512, 512)
         )
-    weight.relay()
-    queries.wait(0)
-    queries.start(1)
-    queries.wait(1)
-    queries.start(2)
+    weight.relay(KEYS)
     for block in range(2, 4):
         tok_t[pl.ds(block * 512, 512), :] = turned(
             tokb[:, :, pl.ds(block * 512, 512)].reshape(512, 512)
@@ -461,7 +469,8 @@
     lt_part = over(16, lt, ltp.at[pc.g], partner)
     lt_part.start()
     q_push.drain()
-    weight.wait(2)
+    weight.relay(VALUES)
+    weight.wait(2, KEYS)
     latents.wait(1)
     latents.start(2)
     output.wait(1)
@@ -474,12 +483,26 @@
         kv[:, columns] = dot(tok, wg[:, :, :, :, columns].reshape(2048, 256)).astype(BF16)
         return carry
 
-    lax.fori_loop(0, 4, project, 0)
-    for n in range(4):
-        kv_t[pl.ds(n * 256, 256), :] = turned(kv[:, n * 256 : n * 256 + 256])
+    lax.fori_loop(0, 2, project, 0)
     queries.wait(2)
     qo_sib = over(17, qg.at[pc.g], qo, sib)
     qo_sib.start()
+    totals = []
+    for head in range(4):
+        query = heads_of(qg, head // 2, head % 2)
+        total = jnp.zeros((1, 512), F32)
+        for chunk in range(4):
+            slots = pl.ds(chunk * 128, 128)
+            raw = col_dot(kv[slots, head * 128 : head * 128 + 128], query)
+            squash = jnp.tanh(raw * (SCALE / SCORE_CAP))
+            kept = valb[chunk // 2, pl.ds(chunk % 2 * 128, 128), :][:, :1]
+            weights = jnp.exp(SCORE_CAP * squash) * kept
+            half[head, slots, :] = weights.astype(BF16)
+            fac[head, slots, :] = weights * (1.0 - squash * squash) * SCALE
+            total = total + jnp.sum(weights, axis=0, keepdims=True)
+        totals.append(total)
+    weight.wait(2, VALUES)
+    lax.fori_loop(2, 4, project, 0)
 
     def n_copy(k):
         g, j = pc.plane_peer(k)
@@ -489,30 +512,17 @@
 
     n_push = PairPushes(pc, n_copy)
     for p in range(2):
-        packed = []
-        sums = []
-        for side in range(2):
-            head = p * 2 + side
-            columns = pl.ds(head * 128, 128)
-            query = heads_of(qg, p, side)
-            total = jnp.zeros((1, 512), F32)
-            for chunk in range(4):
-                slots = pl.ds(chunk * 128, 128)
-                raw = col_dot(kv[slots, columns], query)
-                squash = jnp.tanh(raw * (SCALE / SCORE_CAP))
-                keep = valb[chunk // 2, pl.ds(chunk % 2 * 128, 128), :][:, :1]
-                weights = jnp.exp(SCORE_CAP * squash) * keep
-                half[head, slots, :] = weights.astype(BF16)
-                fac[head, slots, :] = weights * (1.0 - squash * squash) * SCALE
-                total = total + jnp.sum(weights, axis=0, keepdims=True)
-            packed.append(dot(kv_t[pl.ds(512 + head * 128, 128), :], half[head]))
-            sums.append(jnp.broadcast_to(total, (64, 512)))
-        npk[p] = jnp.concatenate(packed + sums, axis=0).T.astype(BF16)
+        heads = (p * 2, p * 2 + 1)
+        packed = [
+            dot(turned(kv[:, 512 + head * 128 : 640 + head * 128]), half[head]) for head in heads
+        ] + [jnp.broadcast_to(totals[head], (64, 512)) for head in heads]
+        npk[p] = jnp.concatenate(packed, axis=0).T.astype(BF16)
         n_push.start_pair(p)
-        if p == 0:
-            latents.relay()
-            output.relay()
-
+
+    latents.relay()
+    output.relay()
+    for n in range(2):
+        kv_t[pl.ds(n * 256, 256), :] = turned(kv[:, n * 256 : n * 256 + 256])
     weight.drain()
     queries.drain()
     n_push.landed()
@@ -635,13 +645,53 @@
     for n in range(4):
         part = dot(pw[pl.ds(n * 8, 8), core].reshape(512, 128), gh_t[...])
         part = part + dot(pwx[pl.ds(n * 8, 8)].reshape(512, 128), ghx[...])
-        glp[pl.ds(n * 8, 8)] = part.astype(BF16).reshape(8, 64, 256)
-
-    def l_copy(k):
-        j = pc.group_peer(k)
-        return remote(glp.at[j], recvl.at[k], gl_s.at[k], gl_r.at[k], chip_device(pc.g, j))
-
-    l_push = Pushes(GROUP, l_copy)
+        glp[n] = part.astype(BF16).reshape(2, 4, 64, 256)
+
+    def gl_copies(phase):
+        for part in range(2):
+            axis = ((1, 2), (2, 1))[part][phase] if phase < 2 else 0
+            for step in (1, 3, 2) if phase < 2 else (1,):
+                peer = list(mine)
+                if phase < 2:
+                    peer[axis] = (peer[axis] + step) % 4
+                else:
+                    peer[0] = pc.g * 2 + 1 - pc.xl
+                spot = part * 7 + phase * 3 + step - 1
+                if phase == 0:
+                    rows = pl.ds(part * 32, 32)
+                    src = glp.at[peer[1], :, :, rows] if axis == 1 else glp.at[:, :, peer[2], rows]
+                    dst = (u1a, u1b)[part].at[step - 1]
+                elif phase == 1:
+                    src = v1a.at[:, peer[2]] if axis == 2 else v1b.at[peer[1]]
+                    dst = u2.at[part, step - 1]
+                else:
+                    src, dst = v2.at[part, 1 - pc.xl], u3.at[part]
+                yield remote(src, dst, gl_s.at[spot], gl_r.at[spot], chip_device(*pc.chip(*peer)))
+
+    def gl_start(phase):
+        for copy in gl_copies(phase):
+            copy.start()
+
+    def gl_add(phase):
+        for copy in gl_copies(phase):
+            copy.wait_recv()
+        if phase == 0:
+            for n in range(4):
+                for xl in range(2):
+                    own = glp[pc.y, xl, n, :32, :].astype(F32)
+                    v1a[xl, n] = (own + sum(u1a[i, xl, n].astype(F32) for i in range(3))).astype(BF16)
+                    own = glp[n, xl, pc.z, 32:, :].astype(F32)
+                    v1b[n, xl] = (own + sum(u1b[i, n, xl].astype(F32) for i in range(3))).astype(BF16)
+        elif phase == 1:
+            for xl in range(2):
+                for part, own in ((0, v1a[xl, pc.z]), (1, v1b[pc.y, xl])):
+                    added = own.astype(F32) + sum(u2[part, i, xl].astype(F32) for i in range(3))
+                    v2[part, xl] = added.astype(BF16)
+        else:
+            for part in range(2):
+                added = v2[part, pc.xl].astype(F32) + u3[part].astype(F32)
+                lblk[part * 32 : part * 32 + 32, :] = added.astype(BF16)
+
     g_push.landed()
     grad = total_slots(gap[own_rows, at256(pair)], recvg, GROUP).astype(BF16).astype(F32)
     gblk[...] = (grad / whole).astype(BF16)
@@ -651,7 +701,7 @@
         lambda k: remote(gblk, g_spot, gga_s.at[k], gga_r.at[k], chip_device(*pc.plane_peer(k))),
     )
     gga_push.start()
-    l_push.start()
+    gl_start(0)
     g_own = pltpu.make_async_copy(gblk, g_spot, loc.at[6])
     g_own.start()
     resampled.relay()
@@ -684,6 +734,8 @@
             parts.append(dot(kv_t[pl.ds(head * 128, 128), :], ds[head]))
         gqp[:, p * 256 : p * 256 + 256] = jnp.concatenate(parts, axis=0).T.astype(BF16)
         gq_push.start_pair(p)
+    gl_add(0)
+    gl_start(1)
     for head in range(4):
         columns = pl.ds(head * 128, 128)
         gkv[:, columns] = dot(ds[head], heads_of(qg, head // 2, head % 2)).astype(BF16)
@@ -760,15 +812,17 @@
                 p_s.at[spot], p_r.at[spot], chip_device(*pc.chip(*peer)),
             )
 
+    for part in range(3):
+        sent = ring(part)
+        for n in range(2):
+            sent[n].start()
+    gl_add(1)
+    gl_start(2)
     gq_push.landed()
     grad = total_slots(gqp[all_rows, at256(pair)], recvgq, CHIPS)
     sq[core, q_spot[0], q_spot[1], q_spot[2], q_spot[3], pair] = (grad * rinv[:, :1]).astype(BF16)
     scaled = Gather(pc, sq.at[core], view_rows, sqa_s, sqa_r, True, PAIR_ORDERS, False)
     scaled.start(0)
-    for part in range(3):
-        sent = ring(part)
-        for n in range(2):
-            sent[n].start()
     held_first = []
     for part in range(3):
         sent = ring(part)
@@ -777,16 +831,15 @@
         copy = pltpu.make_async_copy(slab(part, mine[ORDERS[part][0]]), first[part].at[0], loc.at[7 + part])
         copy.start()
         held_first.append(copy)
-    l_push.landed()
-    lblk[...] = total_slots(glp[pc.j], recvl, GROUP).astype(BF16)
-    glf[pc.g] = lblk[...]
-    l_part = over(13, lblk, glf.at[pc.g], partner)
-    l_part.start()
     resampled.wait(2)
     la_sib = over(14, la.at[:, :, :, :, core], la.at[:, :, :, :, core], sib)
     la_sib.start()
     scaled.wait(0)
     scaled.start(1)
+    gl_add(2)
+    glf[pc.g] = lblk[...]
+    l_part = over(13, lblk, glf.at[pc.g], partner)
+    l_part.start()
     for part in range(3):
         sent = ring(part)
         place = mine[ORDERS[part][0]]
@@ -834,7 +887,9 @@
     s_sib2 = over(15, sq.at[core], sq.at[core], sib)
     s_sib2.start()
     l_part.wait()
-    l_push.drain()
+    for phase in range(3):
+        for copy in gl_copies(phase):
+            copy.wait_send()
     gq_push.drain()
     for c in range(2):
         gow_t[:, c * 512 : c * 512 + 512] = dot(glf[0], attf[c, :256, :]) + dot(glf[1], attf[c, 256:, :])
@@ -985,7 +1040,7 @@
         ((2, 64, 256), BF16),
         ((2, 4, 2, 4, 2, 64, 256), BF16),
         ((512, 1024), BF16),
-        ((1024, 512), BF16),
+        ((512, 512), BF16),
         ((4, 512, 512), F32),
         ((4, 512, 512), BF16),
         ((2, 512, 384), BF16),
@@ -1008,8 +1063,14 @@
         ((2, 128, 256), BF16),
         ((256, 512), BF16),
         ((32, 16, 256), BF16),
-        ((32, 64, 256), BF16),
-        ((32, 64, 256), BF16),
+        ((4, 2, 4, 64, 256), BF16),
+        ((3, 2, 4, 32, 256), BF16),
+        ((3, 4, 2, 32, 256), BF16),
+        ((2, 4, 32, 256), BF16),
+        ((4, 2, 32, 256), BF16),
+        ((2, 3, 2, 32, 256), BF16),
+        ((2, 2, 32, 256), BF16),
+        ((2, 32, 256), BF16),
         ((64, 256), BF16),
         ((2, 64, 256), BF16),
         ((16, 256), BF16),
@@ -1046,8 +1107,8 @@
         in_specs=[VMEM] * 3 + [ANY] * 7,
         out_specs=[ANY] * 7,
         scratch_shapes=[pltpu.VMEM(s, d) for s, d in scratch]
-        + sems(36, 36, 36, 36, 36, 36, 36, 36, 32, 32, 18, 18, 64, 64, 64, 64, 32, 32)
-        + sems(32, 32, 32, 32, 64, 64, 64, 64, 18, 18, 36, 36, 20, 20, 20, 7),
+        + sems(72, 72, 36, 36, 36, 36, 36, 36, 32, 32, 18, 18, 64, 64, 64, 64, 32, 32)
+        + sems(32, 32, 14, 14, 64, 64, 64, 64, 18, 18, 36, 36, 20, 20, 20, 7),
         compiler_params=pltpu.CompilerParams(
             has_side_effects=True, vmem_limit_bytes=62 << 20, collective_id=0
         ),

time: 178 us -> 165 us (0.927)
  Pallas kernels: 176 us -> 163 us
    pallas_call x1, Pallas kernels: 174 us -> 161 us  [local(): pl.pallas_call(whole_kernel, out_shape=results, in_specs=[VMEM] * 3 + [AN...]
where the time goes in v6:
time: 165 us
  Pallas kernels  163 us (99%)
    pallas_call x1, Pallas kernels, local(): pl.pallas_call(whole_kernel, out_shape=results, in_specs=[VMEM] * 3 + [AN...  161 us

profile of v6, /device:TPU:1, one launch (start us, length us, event | category | flops | bytes accessed | tf_op | source)
XLA Modules:
  0.0 164.9 jit_solution(7094365684000578191)
XLA Ops:
  1.3 160.7 %whole.1 = (bf16[256,128]{1,0:T(8,128)(2,1)}, f32[64,256]{1,0:T(8,128)}, f32[64,1024]{1,0:T(8,128)}, f32[13,2048]{1,0:T(8,128)}, f32[64,1024]{1,0:T(8,128)}, /*i...) custom-call(s32[1,256]{1,0:T(1,128)} %bitcast.14, s32[1,1]{1,0:T(1,128)} %bitcast.10.count, bf16[1,128]{1,0:T(2,128)(2,1)} %bitcast.15, ...), custom_call_target="tpu_custom_call" | custom-call | tf_op jit(solution)/shard_map/whole/pallas_call | solution.py:1104
  161.9 2.8 %finish.1 = (bf16[256,128]{1,0:T(8,128)(2,1)}, f32[64,256]{1,0:T(8,128)}, f32[64,1024]{1,0:T(8,128)}, f32[13,2048]{1,0:T(8,128)}, f32[64,1024]{1,0:T(8,128)}, /*...) custom-call(bf16[256,128]{1,0:T(8,128)(2,1)} %get-tuple-element.21.refs_0_, f32[64,256]{1,0:T(8,128)} %get-tuple-element.22.refs_1_, ...), custom_call_target="tpu_custom_call" | custom-call | tf_op jit(solution)/shard_map/finish/pallas_call | solution.py:1121

commit v7 on v6

--- a/solution.py
+++ b/solution.py
@@ -98,7 +98,7 @@
         do(k)
         return carry
 
-    lax.fori_loop(1, n, body, 0)
+    lax.fori_loop(1, n, body, 0, unroll=9 if n == 64 else 31)
 
 
 class Gather:
@@ -249,7 +249,7 @@
     def body(k, total):
         return total + slots[k].astype(F32)
 
-    return lax.fori_loop(1, n, body, own.astype(F32))
+    return lax.fori_loop(1, n, body, own.astype(F32), unroll=9 if n == 64 else 31)
 
 
 class Pushes:
@@ -281,7 +281,7 @@
 
             return carry
 
-        lax.fori_loop(0, 32, body, 0)
+        lax.fori_loop(0, 32, body, 0, unroll=4)
 
 
 def at16(n):
@@ -305,12 +305,12 @@
     llm_to, gl_to, gqw_to, gkw_to, gow_to, gpw_to, gain_to,
     tokens, keyval_w, qw, lt, owt, pw, igrad, llm, gl_out, gqw, gkw, gow_t, gpw, gain_row, gain_out,
     val, qpart, wpl, gain,
-    wg, tokb, tok_t, valb, qx, qsum, recvq, qg, qo, owe, lown, ltp, la, kv, kv_t, fac, half, npk, recvn,
+    wg, tokb, tok_t, valb, qx, qsum, recvq, qg, qo, owe, lown, ltp, la, kv, kv_t, fac, half, npk, recvn, tot_all, tots, rtot,
     ablk, attf, pw_t, pwx, lat_s, lat_x, fold_s, fold_x, fold, foldx, sumx, sumo, sumr, gh_t, ghx, ghp, gap, recvg, glp, u1a, u1b, v1a, v1b, u2, v2, u3,
     lblk, glf, gblk, gg, ds, gqp, recvgq, gkv, sq, r1a, r1b, r1c, s1a, s1b, s1c,
     r2a, r2b, r2c, s2a, s2b, s2c, r3a, r3b, r3c, fara, farb, farc, fin, oth,
     w_s, w_r, ow_s, ow_r, lo_s, lo_r, l_s, l_r, q_s, q_r, qa_s, qa_r, n_s, n_r, a_s, a_r, t_s, t_r,
-    g_s, g_r, gl_s, gl_r, gga_s, gga_r, gq_s, gq_r, sqa_s, sqa_r, p_s, p_r, x_s, x_r, loc, out_s,
+    g_s, g_r, gl_s, gl_r, tot_s, tot_r, gga_s, gga_r, gq_s, gq_r, sqa_s, sqa_r, p_s, p_r, x_s, x_r, loc, out_s,
 ):
     pc = Place()
     core = pc.core
@@ -510,14 +510,26 @@
             npk.at[j % 2, at16(g * 16 + j // 2), :], recvn.at[k], n_s.at[k], n_r.at[k], chip_device(g, j)
         )
 
+    def tot_copy(k):
+        g, j = pc.plane_peer(k)
+        return remote(
+            tots.at[g * 2 + j // 16, pl.ds(j % 2 * 2, 2)], rtot.at[k], tot_s.at[k], tot_r.at[k], chip_device(g, j)
+        )
+
     n_push = PairPushes(pc, n_copy)
+    tot_push = Pushes(CHIPS, tot_copy)
+    tot_all[...] = jnp.concatenate(totals + [jnp.zeros((4, 512), F32)], axis=0)
+    for head in range(4):
+        for n in range(4):
+            tots[n, head] = tot_all[head : head + 1, n * 128 : n * 128 + 128]
     for p in range(2):
         heads = (p * 2, p * 2 + 1)
         packed = [
             dot(turned(kv[:, 512 + head * 128 : 640 + head * 128]), half[head]) for head in heads
-        ] + [jnp.broadcast_to(totals[head], (64, 512)) for head in heads]
+        ]
         npk[p] = jnp.concatenate(packed, axis=0).T.astype(BF16)
         n_push.start_pair(p)
+    tot_push.start()
 
     latents.relay()
     output.relay()
@@ -527,11 +539,25 @@
     queries.drain()
     n_push.landed()
     total = total_slots(npk[pair, all_rows, :], recvn, CHIPS)
+    tot_push.landed()
+
+    def add_rows(k, held):
+        return (held[0] + rtot[k, 0], held[1] + rtot[k, 1])
+
+    here = pc.g * 2 + pc.j // 16
+    row_sums = lax.fori_loop(1, CHIPS, add_rows, (tots[here, pair * 2], tots[here, pair * 2 + 1]))
+    row = lax.broadcasted_iota(jnp.int32, (16, 128), 0)
+    hit = lax.broadcasted_iota(jnp.int32, (16, 128), 1) == row + (pc.j // 2) % 8 * 16
     whole = jnp.concatenate(
-        [jnp.broadcast_to(total[:, 256:257], (16, 128)), jnp.broadcast_to(total[:, 320:321], (16, 128))],
+        [
+            jnp.broadcast_to(
+                jnp.sum(jnp.where(hit, row_sums[n], 0.0), axis=1, keepdims=True), (16, 128)
+            )
+            for n in range(2)
+        ],
         axis=1,
     )
-    ablk[...] = (total[:, :256] / whole).astype(BF16)
+    ablk[...] = (total / whole).astype(BF16)
     a_spot = attf.at[core, all_rows, at256(pair)]
     a_push = Pushes(
         CHIPS,
@@ -542,6 +568,7 @@
     a_own.start()
 
     n_push.drain()
+    tot_push.drain()
     latents.wait(2)
     feats = lown[...].reshape(2048, 256)
     lat_s[:128, :] = dot(pw_t[1], feats)
@@ -1043,8 +1070,11 @@
         ((512, 512), BF16),
         ((4, 512, 512), F32),
         ((4, 512, 512), BF16),
-        ((2, 512, 384), BF16),
-        ((64, 16, 384), BF16),
+        ((2, 512, 256), BF16),
+        ((64, 16, 256), BF16),
+        ((8, 512), F32),
+        ((4, 4, 1, 128), F32),
+        ((64, 2, 1, 128), F32),
         ((16, 256), BF16),
         ((2, 512, 512), BF16),
         ((2, 128, 2048), BF16),
@@ -1108,7 +1138,7 @@
         out_specs=[ANY] * 7,
         scratch_shapes=[pltpu.VMEM(s, d) for s, d in scratch]
         + sems(72, 72, 36, 36, 36, 36, 36, 36, 32, 32, 18, 18, 64, 64, 64, 64, 32, 32)
-        + sems(32, 32, 14, 14, 64, 64, 64, 64, 18, 18, 36, 36, 20, 20, 20, 7),
+        + sems(32, 32, 14, 14, 64, 64, 64, 64, 64, 64, 18, 18, 36, 36, 20, 20, 20, 7),
         compiler_params=pltpu.CompilerParams(
             has_side_effects=True, vmem_limit_bytes=62 << 20, collective_id=0
         ),

time: 165 us -> 162 us (0.982)
  Pallas kernels: 163 us -> 160 us
    pallas_call x1, Pallas kernels: 161 us -> 157 us  [local(): pl.pallas_call(whole_kernel, out_shape=results, in_specs=[VMEM] * 3 + [AN...]
where the time goes in v7:
time: 162 us; the launch traced here: 161 us
  Pallas kernels  160 us (99%)
    pallas_call x1, Pallas kernels, local(): pl.pallas_call(whole_kernel, out_shape=results, in_specs=[VMEM] * 3 + [AN...  157 us

profile of v7, /device:TPU:1, one launch (start us, length us, event | category | flops | bytes accessed | tf_op | source)
XLA Modules:
  0.0 161.4 jit_solution(2759153248069450819)
XLA Ops:
  1.3 157.1 %whole.1 = (bf16[256,128]{1,0:T(8,128)(2,1)}, f32[64,256]{1,0:T(8,128)}, f32[64,1024]{1,0:T(8,128)}, f32[13,2048]{1,0:T(8,128)}, f32[64,1024]{1,0:T(8,128)}, /*i...) custom-call(s32[1,256]{1,0:T(1,128)} %bitcast.14, s32[1,1]{1,0:T(1,128)} %bitcast.10.count, bf16[1,128]{1,0:T(2,128)(2,1)} %bitcast.15, ...), custom_call_target="tpu_custom_call" | custom-call | tf_op jit(solution)/shard_map/whole/pallas_call | solution.py:1134
  158.3 2.8 %finish.1 = (bf16[256,128]{1,0:T(8,128)(2,1)}, f32[64,256]{1,0:T(8,128)}, f32[64,1024]{1,0:T(8,128)}, f32[13,2048]{1,0:T(8,128)}, f32[64,1024]{1,0:T(8,128)}, /*...) custom-call(bf16[256,128]{1,0:T(8,128)(2,1)} %get-tuple-element.21.refs_0_, f32[64,256]{1,0:T(8,128)} %get-tuple-element.22.refs_1_, ...), custom_call_target="tpu_custom_call" | custom-call | tf_op jit(solution)/shard_map/finish/pallas_call | solution.py:1151

commit v8 on v7

--- a/solution.py
+++ b/solution.py
@@ -301,9 +301,9 @@
 
 
 def whole_kernel(
-    keep, count, gain_in, tokens_in, keyval_in, qw_in, lt_in, owt_in, pw_in, igrad_in,
+    keep, count, gain_in, keyval_w, tokens_in, qw_in, lt_in, owt_in, pw_in, igrad_in,
     llm_to, gl_to, gqw_to, gkw_to, gow_to, gpw_to, gain_to,
-    tokens, keyval_w, qw, lt, owt, pw, igrad, llm, gl_out, gqw, gkw, gow_t, gpw, gain_row, gain_out,
+    tokens, qw, lt, owt, pw, igrad, llm, gl_out, gqw, gkw, gow_t, gpw, gain_row, gain_out,
     val, qpart, wpl, gain,
     wg, tokb, tok_t, valb, qx, qsum, recvq, qg, qo, owe, lown, ltp, la, kv, kv_t, fac, half, npk, recvn, tot_all, tots, rtot,
     ablk, attf, pw_t, pwx, lat_s, lat_x, fold_s, fold_x, fold, foldx, sumx, sumo, sumr, gh_t, ghx, ghp, gap, recvg, glp, u1a, u1b, v1a, v1b, u2, v2, u3,
@@ -339,14 +339,13 @@
         pltpu.make_async_copy(src, dst, loc.at[12 + n])
         for n, (src, dst) in enumerate(
             (
-                (keyval_in, keyval_w), (lt_in, lt), (qw_in, qw), (owt_in, owt),
+                (lt_in, lt), (qw_in, qw), (owt_in, owt),
                 (tokens_in, tokens), (pw_in, pw), (igrad_in, igrad),
             )
         )
     ]
     for copy in loads:
         copy.start()
-    loads[0].wait()
 
     rows_f32 = jnp.concatenate([keyval_w[...].astype(F32), jnp.zeros((3, 2048), F32)], axis=0).astype(BF16)
     for c in range(2):
@@ -354,7 +353,7 @@
         wpl[c, :, 512:] = rows_f32[:, 1024 + c * 512 : 1536 + c * 512]
     w_own = pltpu.make_async_copy(wpl.at[core], wg.at[pc.x, pc.y, pc.z, at16(core)], loc.at[3])
     w_own.start()
-    for copy in loads[1:]:
+    for copy in loads:
         copy.wait()
     feats_f32 = lt[...].astype(F32)
     lat = feats_f32.T.astype(BF16)
@@ -1035,7 +1034,6 @@
     widths = [w for _, w in WIDE]
     scratch = [
         ((256, 1664), BF16),
-        ((13, 2048), BF16),
         ((64, 1024), BF16),
         ((64, 256), BF16),
         ((64, 1024), BF16),
@@ -1134,7 +1132,7 @@
     made = pl.pallas_call(
         whole_kernel,
         out_shape=results,
-        in_specs=[VMEM] * 3 + [ANY] * 7,
+        in_specs=[VMEM] * 4 + [ANY] * 6,
         out_specs=[ANY] * 7,
         scratch_shapes=[pltpu.VMEM(s, d) for s, d in scratch]
         + sems(72, 72, 36, 36, 36, 36, 36, 36, 32, 32, 18, 18, 64, 64, 64, 64, 32, 32)
@@ -1144,8 +1142,8 @@
         ),
         name="whole",
     )(
-        keep_mask.reshape(1, 256), shard_counts.reshape(1, 1), llm_gain.reshape(1, 128), tokens,
-        keyval_weight, query_weight, latents.T, output_weight.T, project_weight.reshape(32, 2, 64, 128),
+        keep_mask.reshape(1, 256), shard_counts.reshape(1, 1), llm_gain.reshape(1, 128),
+        keyval_weight, tokens, query_weight, latents.T, output_weight.T, project_weight.reshape(32, 2, 64, 128),
         input_grad,
     )
     llm, gl, gqw, gkw, gow, gpw, gain = pl.pallas_call(

time: 162 us -> 162 us (level)
  no operation moved by 1% of the time
where the time goes in v8:
time: 162 us
  Pallas kernels  161 us (99%)
    pallas_call x1, Pallas kernels, local(): pl.pallas_call(whole_kernel, out_shape=results, in_specs=[VMEM] * 4 + [AN...  158 us

profile of v8, /device:TPU:1, one launch (start us, length us, event | category | flops | bytes accessed | tf_op | source)
XLA Modules:
  0.0 162.1 jit_solution(13105008515989482300)
XLA Ops:
  1.3 157.8 %whole.1 = (bf16[256,128]{1,0:T(8,128)(2,1)}, f32[64,256]{1,0:T(8,128)}, f32[64,1024]{1,0:T(8,128)}, f32[13,2048]{1,0:T(8,128)}, f32[64,1024]{1,0:T(8,128)}, /*i...) custom-call(s32[1,256]{1,0:T(1,128)} %bitcast.14, s32[1,1]{1,0:T(1,128)} %bitcast.10.count, bf16[1,128]{1,0:T(2,128)(2,1)} %bitcast.15, ...), custom_call_target="tpu_custom_call" | custom-call | tf_op jit(solution)/shard_map/whole/pallas_call | solution.py:1132
  159.0 2.8 %finish.1 = (bf16[256,128]{1,0:T(8,128)(2,1)}, f32[64,256]{1,0:T(8,128)}, f32[64,1024]{1,0:T(8,128)}, f32[13,2048]{1,0:T(8,128)}, f32[64,1024]{1,0:T(8,128)}, /*...) custom-call(bf16[256,128]{1,0:T(8,128)(2,1)} %get-tuple-element.21.refs_0_, f32[64,256]{1,0:T(8,128)} %get-tuple-element.22.refs_1_, ...), custom_call_target="tpu_custom_call" | custom-call | tf_op jit(solution)/shard_map/finish/pallas_call | solution.py:1149
